TPU v7x, 512 devices: a whole 4x8x8 slice. The times are simulated.
512 devices in a mesh: row: 32 (over z, y_hi, core), col: 16 (over x, y_lo).
Axes of the slice: x: 4, y: 8 (y_hi: 2, y_lo: 4; y = y_hi * 4 + y_lo), z: 8, core: 2. Of those that a mesh axis runs over, the one named last changes fastest.
Arguments:
- density: bfloat16 [64, 48, 128, 128], P('row', 'col'), as said below
- block_cols: int32 [64, 48], P('row', 'col'), may hold values from 0 to 63, as said below
- block_counts: int32 [64, 16], P('row', 'col'), may hold values from 0 to 3, as said below
Outputs:
- purified: bfloat16 [64, 48, 128, 128], P('row', 'col')
Inputs may be any that keep to these rules, and one draw needn't show every extreme that they name: The 3 slots c*3 to c*3 + 2 of block_cols[i] name distinct block-columns of group c, that is of [c*4, (c+1)*4); the first block_counts[i, c] of them are live, the rest are padding. The pattern is symmetric: column j is live in block-row i exactly when column i is live in block-row j; column i is always live in block-row i. `block_counts`: every block-row has 3 live slots in the group that holds its own index. `density`: P is symmetric: the live block of block-row i at column j equals the transpose of the live block of block-row j at column i. Padding slots hold arbitrary finite values.
All inputs are finite; a program needn't handle non-finite values.
Results may differ from a plain program's by a relative error of at most 0.0041.
Values may be sent and summed in bfloat16 or wider, within the bound.
No kernel may reach another device: no remote copies, remote signals or barrier semaphores. Data moves between devices by JAX's collectives and lax.ppermute only.
A program may use at most 64 MiB of HBM per device.

v0:
```python
import jax
import jax.numpy as jnp
from jax import lax
from jax.sharding import PartitionSpec as P


def live_slots(counts, per_group):
    slot_ids = jnp.arange(counts.shape[1] * per_group, dtype=jnp.int32)
    return (slot_ids % per_group)[None, :] < jnp.repeat(counts, per_group, axis=1)


def add_terms(running, left_strip, index_table, source):
    piece_rows = left_strip.shape[1]
    index_part = lax.slice_in_dim(index_table, 0, piece_rows, axis=1)
    products = []
    for target in range(index_table.shape[2]):
        blocks = jnp.take(source, index_part[:, :, target], axis=0)
        product = jnp.einsum(
            "iaxy,iayz->ixz", left_strip, blocks, preferred_element_type=jnp.float32
        )
        products.append(product)
    return running + jnp.stack(products, axis=1)


def local(density, block_cols, block_counts):
    row_count = density.shape[0]
    per_group = density.shape[1]
    block_size = density.shape[2]
    strip_vals, strip_cols, strip_counts = (
        lax.all_gather(density, "col", axis=1, tiled=True),
        lax.all_gather(block_cols, "col", axis=1, tiled=True),
        lax.all_gather(block_counts, "col", axis=1, tiled=True),
    )
    strip_live = live_slots(strip_counts, per_group)
    own_live = live_slots(block_counts, per_group)
    offsets = jnp.arange(per_group, dtype=jnp.int32)
    col_vals, col_cols, col_counts = (
        lax.all_gather(density, "row", axis=0, tiled=True),
        lax.all_gather(block_cols, "row", axis=0, tiled=True),
        lax.all_gather(block_counts, "row", axis=0, tiled=True),
    )
    col_live = live_slots(col_counts, per_group)
    cand_cols = col_cols[strip_cols]
    cand_live = col_live[strip_cols]
    matches = (cand_cols[:, :, :, None] == block_cols[:, None, None, :]) & cand_live[:, :, :, None]
    matches = matches & strip_live[:, :, None, None] & own_live[:, None, None, :]
    which_slot = jnp.sum(jnp.where(matches, offsets[None, None, :, None], 0), axis=2)
    found_index = strip_cols[:, :, None] * per_group + which_slot
    found_table = jnp.any(matches, axis=2)
    flat_vals = col_vals.reshape(col_vals.shape[0] * per_group, block_size, block_size)
    empty_index = flat_vals.shape[0]
    source = jnp.concatenate(
        [flat_vals, jnp.zeros((1, block_size, block_size), flat_vals.dtype)], axis=0
    )
    index_table = jnp.where(found_table, found_index, empty_index).astype(jnp.int32)
    zero_sums = jnp.zeros((row_count, per_group, block_size, block_size), jnp.float32)
    square = add_terms(zero_sums, strip_vals, index_table, source)
    square_low = square.astype(jnp.bfloat16)
    cube_sums = add_terms(
        zero_sums, lax.all_gather(square_low, "col", axis=1, tiled=True), index_table, source
    )
    return (3.0 * square - 2.0 * cube_sums).astype(jnp.bfloat16)


def solution(mesh):
    return jax.shard_map(
        local,
        mesh=mesh,
        in_specs=(P("row", "col", None, None), P("row", "col"), P("row", "col")),
        out_specs=P("row", "col", None, None),
        check_vma=False,
    )
```

profile of v0, /device:TPU:128, one launch (start us, length us, event | category | flops | bytes accessed | tf_op | source)
XLA Modules:
  0.0 346.7 jit_solution(8454527446803234154)
XLA Ops:
  6.5 0.7 all-gather.7.cloned.1.call-update
  7.3 1.6 copy.79
  9.0 0.8 copy.74
  9.8 42.5 %all-gather.2 = s32[16,1,2]{2,1,0:T(1,128)S(1)} all-gather(s32[1,1,2]{2,1,0:T(1,128)} %bitcast.81), channel_id=1, replica_groups=mesh['row'=32,'col'=16] {'col'}, dimensions={0}, use_global_device_ids=true | all-gather | bytes 136 | tf_op jit(solution)/shard_map/all_gather | solution.py:32
  52.5 39.9 %all-gather.1 = s32[16,3,2]{1,2,0:T(2,128)S(1)} all-gather(s32[1,3,2]{1,2,0:T(2,128)} %bitcast.72), channel_id=1, replica_groups=mesh['row'=32,'col'=16] {'col'}, dimensions={0}, use_global_device_ids=true | all-gather | bytes 408 | tf_op jit(solution)/shard_map/all_gather | solution.py:31
  92.6 1.3 dynamic-slice
  94.5 0.8 bitcast_dynamic-update-slice_fusion
  95.3 25.0 %all-reduce.1 = s32[64]{0:T(128)S(1)} all-reduce(s32[64]{0:T(128)S(1)} %bitcast_dynamic-update-slice_fusion), channel_id=1, replica_groups=mesh['row'=32,'col'=16] {'row'}, use_global_device_ids=true, to_apply=%add.1 | all-reduce | flops 64 | bytes 512
  121.1 45.6 %all-gather = s32[32,2,3]{2,1,0:T(2,128)S(1)} all-gather(s32[1,2,3]{2,1,0:T(2,128)} %bitcast.73), channel_id=1, replica_groups=mesh['row'=32,'col'=16] {'row'}, dimensions={0}, use_global_device_ids=true | all-gather | bytes 792 | tf_op jit(solution)/shard_map/all_gather | solution.py:39
  167.4 0.7 iota_compare_fusion.1
  168.6 8.1 %concatenate.3 = bf16[193,128,128]{2,1,0:T(8,128)(2,1)} pad(bf16[192,128,128]{2,1,0:T(8,128)(2,1)} %bitcast.62, bf16[]{:T(256)} %constant.23.clone.1), padding=0_1x0_0x0_0 | pad | bytes 12615682 | tf_op jit(solution)/shard_map/concatenate | solution.py:52
  176.8 5.6 %gather_fusion.4 = bf16[96,128,128]{2,1,0:T(8,128)(2,1)} fusion(bf16[193,128,128]{2,1,0:T(8,128)(2,1)} %concatenate.3, s32[1024]{0:T(1024)S(1)} %pad_clamp_fusion), kind=kCustom, calls=%fused_computation.2.clone | custom fusion | bytes 6291840 | tf_op jit(solution)/shard_map/jit(_take)/gather | solution.py:17
  182.3 4.0 %gather_fusion.2 = bf16[96,128,128]{2,1,0:T(8,128)(2,1)S(1)} fusion(bf16[193,128,128]{2,1,0:T(8,128)(2,1)} %concatenate.3, s32[1024]{0:T(1024)S(1)} %pad_clamp_fusion.2), kind=kCustom, calls=%fused_computation.clone | custom fusion | bytes 6291840 | tf_op jit(solution)/shard_map/jit(_take)/gather | solution.py:17
  186.3 5.5 %gather_fusion.3 = bf16[96,128,128]{2,1,0:T(8,128)(2,1)} fusion(bf16[193,128,128]{2,1,0:T(8,128)(2,1)} %concatenate.3, s32[1024]{0:T(1024)S(1)} %pad_clamp_fusion.1), kind=kCustom, calls=%fused_computation.1.clone | custom fusion | bytes 6291840 | tf_op jit(solution)/shard_map/jit(_take)/gather | solution.py:17
  191.9 35.6 %all-gather.9.cloned.1.call-done = bf16[2,48,128,128]{3,2,0,1:T(8,128)(2,1)} async-done(((bf16[2,3,128,128]{3,2,0,1:T(8,128)(2,1)}), bf16[2,48,128,128]{3,2,0,1:T(8,128)(2,1)}) %all-gather.9.cloned.1.call-update) | async-done | bytes 3145744 | tf_op jit(solution)/shard_map/all_gather | solution.py:30
  227.5 4.4 %fusion.18 = f32[2,1,128,128]{2,3,0,1:T(8,128)S(1)} fusion(bf16[2,48,128,128]{3,2,0,1:T(8,128)(2,1)} %all-gather.9.cloned.1.call-done, bf16[2,48,128,128]{3,2,1,0:T(8,128)(2,1)} %bitcast.66, pred[2,48]{1,0:T(4,128)(4,1)S(1)} %compare_and_fusion), kind=kOutput, calls=%fused_computation.22 | convolution fusion | flops 404226048 | bytes 6422624 | tf_op jit(solution)/shard_map/iaxy,iayz->ixz/dot_general | solution.py:18
  231.9 1.7 fusion.12
  233.8 1.7 fusion.15
  236.2 0.8 copy.86
  237.1 92.5 %all-gather.11.cloned.1.call-done = bf16[2,48,128,128]{3,2,0,1:T(8,128)(2,1)} async-done(((bf16[2,3,128,128]{3,2,0,1:T(8,128)(2,1)}), bf16[2,48,128,128]{3,2,0,1:T(8,128)(2,1)}) %all-gather.11.cloned.1.call-update) | async-done | bytes 3145744 | tf_op jit(solution)/shard_map/all_gather | solution.py:60
  329.5 5.0 %fusion.27 = f32[2,1,128,128]{2,3,0,1:T(8,128)S(1)} fusion(bf16[2,48,128,128]{3,2,0,1:T(8,128)(2,1)} %all-gather.11.cloned.1.call-done, bf16[2,48,128,128]{3,2,1,0:T(8,128)(2,1)} %bitcast.67, pred[2,48]{1,0:T(4,128)(4,1)S(1)} %compare_and_fusion), kind=kOutput, calls=%fused_computation.25 | convolution fusion | flops 404226048 | bytes 6422624 | tf_op jit(solution)/shard_map/iaxy,iayz->ixz/dot_general | solution.py:18
  334.5 2.3 fusion.24
  336.9 2.3 fusion.21
  339.3 0.8 copy.93
  (56 shorter events, 3.4 us)
Async XLA Ops:
  6.5 162.1 %all-gather.7.cloned.1.call-start = ((), (), s32[]{:S(2)}) async-start(), calls=%async_computation | async-start | bytes 6488064 | tf_op jit(solution)/shard_map/all_gather | solution.py:38
  7.3 220.2 %all-gather.9.cloned.1.call-start = ((), (), s32[]{:S(2)}) async-start(), calls=%async_computation.1 | async-start | bytes 3342336 | tf_op jit(solution)/shard_map/all_gather | solution.py:30
  8.9 320.6 %all-gather.11.cloned.1.call-start = ((), (), s32[]{:S(2)}) async-start(), calls=%async_computation.2 | async-start | bytes 3342336 | tf_op jit(solution)/shard_map/all_gather | solution.py:60
  227.5 4.4 %copy-start.6 = (bf16[2,48,128,128]{3,2,0,1:T(8,128)(2,1)S(1)}, bf16[2,48,128,128]{3,2,0,1:T(8,128)(2,1)}, u32[]{:S(2)}) copy-start(bf16[2,48,128,128]{3,2,0,1:T(8,128)(2,1)} %all-gather.9.cloned.1.call-done) | copy-start | bytes 9437188
  231.9 1.9 copy-start
  233.7 1.9 copy-start.2
  235.5 0.6 copy-start.4
  329.5 5.0 %copy-start.1 = (bf16[96,128,128]{2,1,0:T(8,128)(2,1)S(1)}, bf16[96,128,128]{2,1,0:T(8,128)(2,1)}, u32[]{:S(2)}) copy-start(bf16[96,128,128]{2,1,0:T(8,128)(2,1)} %gather_fusion.3) | copy-start | bytes 9437188
  329.5 5.0 %copy-start.7 = (bf16[2,48,128,128]{3,2,0,1:T(8,128)(2,1)S(1)}, bf16[2,48,128,128]{3,2,0,1:T(8,128)(2,1)}, u32[]{:S(2)}) copy-start(bf16[2,48,128,128]{3,2,0,1:T(8,128)(2,1)} %all-gather.11.cloned.1.call-done) | copy-start | bytes 9437188
  336.9 2.4 copy-start.3
  336.9 2.4 copy-start.5
Sparse Core Ops, SparseCore 0:
  10.7 121.3 all-gather.6
  134.1 93.2 all-gather.8
  237.2 92.3 all-gather.10
where the time goes:
time: 347 us
  blocking collectives  153 us (44%)
  waiting for transfers between devices  129 us (37%)
  local copies, waits for them, and re-layouts  32.2 us (9%)
  matrix products  17.5 us (5%)
  between operations  14 us (4%)
    all_gather x1, waiting for transfers between devices, local(): lax.all_gather(square_low, 'col', axis=1, tiled=True)  92.5 us
    all_gather x1, blocking collectives, local(): lax.all_gather(block_cols, 'row', axis=0, tiled=True)  45.6 us
    all_gather x1, blocking collectives, local(): lax.all_gather(block_counts, 'col', axis=1, tiled=True)  42.5 us
    all_gather x1, blocking collectives, local(): lax.all_gather(block_cols, 'col', axis=1, tiled=True)  39.9 us
    all_gather x1, waiting for transfers between devices, local(): lax.all_gather(density, 'col', axis=1, tiled=True)  35.6 us
    unnamed x1, blocking collectives  25 us
    dot_general x6, matrix products, add_terms(): jnp.einsum('iaxy,iayz->ixz', left_strip, blocks, preferred_element_type=j...  17.5 us
    gather x3, local copies, waits for them, and re-layouts, add_terms(): blocks = jnp.take(source, index_part[:, :, target], axis=0)  15.1 us
  transfers between devices with their start and end apart: 3, of which 2 were waited for; matrix products, arithmetic and copies ran while one was open for 9% of the time, Pallas kernels for 0%

commit v1 on v0

v1 whole, which is shorter than its diff:
```python
import jax
import jax.numpy as jnp
from jax import lax
from jax.experimental import pallas as pl
from jax.experimental.pallas import tpu as pltpu
from jax.sharding import PartitionSpec as P

BS = 128
KD = 3
CG = 4
ROWS = 2
NG = 16
BLK = ROWS * KD * BS
PAY = BLK + 16
BF = jnp.bfloat16
F32 = jnp.float32

CORE_SWAP = [(r, r ^ 1) for r in range(32)]
YH_SWAP = [(r, r ^ 2) for r in range(32)]
Z_STEP = [(r, (r + (4 if r % 2 == 0 else 28)) % 32) for r in range(32)]


def yl_shift(s):
    return [(c, c // 4 * 4 + (c + s) % 4) for c in range(16)]


def x_shift(s):
    return [(c, (c + 4 * s) % 16) for c in range(16)]


def col_gather(own, rows):
    pieces = [own] + [lax.ppermute(own, "col", yl_shift(s)) for s in (1, 3, 2)]
    line = jnp.concatenate(pieces, axis=0)
    left = lax.ppermute(line, "col", x_shift(1))
    right = lax.ppermute(line, "col", x_shift(3))
    far_lo = lax.ppermute(left[: 2 * rows], "col", x_shift(1))
    far_hi = lax.ppermute(right[2 * rows :], "col", x_shift(3))
    return [line, left, right, far_lo, far_hi]


COL_PIECES = (
    [(0, n, 0, o) for n, o in enumerate((0, 3, 1, 2))]
    + [(1, n, 3, o) for n, o in enumerate((0, 3, 1, 2))]
    + [(2, n, 1, o) for n, o in enumerate((0, 3, 1, 2))]
    + [(3, 0, 2, 0), (3, 1, 2, 3), (4, 0, 2, 1), (4, 1, 2, 2)]
)


def row_gather(own):
    other = lax.ppermute(own, "row", CORE_SWAP)
    own_y = lax.ppermute(own, "row", YH_SWAP)
    other_y = lax.ppermute(own_y, "row", CORE_SWAP)
    out = []
    for pair in ((own, other), (own_y, other_y)):
        current = jnp.concatenate(pair, axis=0)
        ring = [current]
        for step in range(4):
            current = lax.ppermute(current if step < 3 else current[:PAY], "row", Z_STEP)
            ring.append(current)
        out.append(ring)
    swapped = [[lax.ppermute(a, "row", CORE_SWAP) for a in ring[1:]] for ring in out]
    arrays, pieces = [], []
    for yh in range(2):
        for step in range(5):
            for n in range(1 if step == 4 else 2):
                pieces.append((len(arrays), n, step, yh, n))
            arrays.append(out[yh][step])
        for step in range(1, 5):
            for n in range(1 if step == 4 else 2):
                pieces.append((len(arrays), n, -step, yh, 1 - n))
            arrays.append(swapped[yh][step - 1])
    return arrays, pieces


def meta_rows(meta):
    wide = meta.astype(F32)
    return [
        jnp.broadcast_to(wide[s : s + 1], (16, BS)).astype(BF) for s in range(ROWS * KD)
    ]


def spread(src, base, slots, store):
    masks = [[m == jnp.full((16, BS), q, BF) for q in range(CG)] for m in slots]

    def step(n, _):
        r = pl.multiple_of(n * 16, 16)
        v = [src[pl.ds(base + t * BS + r, 16), :] for t in range(KD)]
        zero = jnp.zeros((16, BS), BF)
        for q in range(CG):
            d = zero
            for t in range(KD):
                d = jnp.where(masks[t][q], v[t], d)
            store(r, q, d)
        return 0

    lax.fori_loop(0, BS // 16, step, 0, unroll=True)


def spread_strip(src, piece, rows, meta, group, a_ref):
    slots = meta_rows(meta)
    for i in range(ROWS):

        def store(r, q, d, i=i):
            col = pl.multiple_of(group * (CG * BS) + q * BS, BS)
            a_ref[pl.ds(i * BS + r, 16), pl.ds(col, BS)] = d

        spread(src, piece * rows + i * KD * BS, slots[i * KD : (i + 1) * KD], store)


def dot(a_ref, b_ref):
    return jnp.dot(a_ref[...], b_ref[...], preferred_element_type=F32)


def pick(acc, slots):
    out = []
    for i in range(ROWS):
        for t in range(KD):
            m = slots[i * KD + t].astype(F32)[0:1]
            d = jnp.zeros((BS, BS), F32)
            for q in range(CG):
                d = jnp.where(m == float(q), acc[i * BS : (i + 1) * BS, q * BS : (q + 1) * BS], d)
            out.append(d)
    return out


def square_kernel(n_col, row_pieces, pos, *refs):
    cols, rows = refs[:n_col], refs[n_col:-5]
    square_ref, low_ref, b_ref, meta_ref, a_ref = refs[-5:]
    z, yh, core, x, yl = (pos[n] for n in range(5))
    sign = 1 - 2 * core
    for n, (arr, piece, dx, dy) in enumerate(COL_PIECES):
        src = cols[arr]
        group = ((x + dx) & 3) * 4 + ((yl + dy) & 3)
        meta = src[piece * PAY + BLK : (piece + 1) * PAY]
        meta_ref[n * 16 : (n + 1) * 16] = meta
        spread_strip(src, piece, PAY, meta, group, a_ref)
    for arr, piece, step, dyh, dcore in row_pieces:
        src = rows[arr]
        group = ((z - sign * step) & 7) * 2 + (yh ^ dyh)
        slots = meta_rows(src[piece * PAY + BLK : (piece + 1) * PAY])
        for i in range(ROWS):
            top = pl.multiple_of((group * CG + (core ^ dcore) * 2 + i) * BS, BS)

            def store(r, q, d, top=top):
                b_ref[pl.ds(top + r, 16), q * BS : (q + 1) * BS] = d

            spread(src, piece * PAY + i * KD * BS, slots[i * KD : (i + 1) * KD], store)
    own = meta_rows(cols[0][BLK:PAY])
    for s, d in enumerate(pick(dot(a_ref, b_ref), own)):
        square_ref[s * BS : (s + 1) * BS] = d
        low_ref[s * BS : (s + 1) * BS] = d.astype(BF)


def cube_kernel(pos, meta_ref, b_ref, square_ref, *refs):
    cols, (out_ref, a_ref) = refs[:-2], refs[-2:]
    x, yl = pos[3], pos[4]
    for n, (arr, piece, dx, dy) in enumerate(COL_PIECES):
        group = ((x + dx) & 3) * 4 + ((yl + dy) & 3)
        spread_strip(cols[arr], piece, BLK, meta_ref[n * 16 : (n + 1) * 16], group, a_ref)
    own = meta_rows(meta_ref[0:16])
    for s, d in enumerate(pick(dot(a_ref, b_ref), own)):
        square = square_ref[s * BS : (s + 1) * BS]
        out_ref[s * BS : (s + 1) * BS] = (3.0 * square - 2.0 * d).astype(BF)


VM = pl.BlockSpec(memory_space=pltpu.VMEM)
SM = pl.BlockSpec(memory_space=pltpu.SMEM)
PARAMS = pltpu.CompilerParams(vmem_limit_bytes=36 * 1024 * 1024)


def local(density, block_cols, block_counts):
    slot = lax.broadcasted_iota(jnp.int32, (ROWS, KD), 1)
    where = jnp.where(slot < block_counts, block_cols % CG, -1).reshape(ROWS * KD, 1)
    meta = jnp.broadcast_to(where, (ROWS * KD, BS)).astype(BF)
    own = jnp.concatenate(
        [density.reshape(BLK, BS), meta, jnp.zeros((16 - ROWS * KD, BS), BF)], axis=0
    )
    r, c = lax.axis_index("row"), lax.axis_index("col")
    pos = jnp.stack([r // 4, r // 2 % 2, r % 2, c // 4, c % 4]).astype(jnp.int32)
    cols = col_gather(own, PAY)
    rows, row_pieces = row_gather(own)

    def call(pos, *arrays):
        return square_kernel(len(cols), row_pieces, pos, *arrays)

    square, low, b, metas = pl.pallas_call(
        call,
        out_shape=[
            jax.ShapeDtypeStruct((BLK, BS), F32),
            jax.ShapeDtypeStruct((BLK, BS), BF),
            jax.ShapeDtypeStruct((NG * CG * BS, CG * BS), BF),
            jax.ShapeDtypeStruct((NG * 16, BS), BF),
        ],
        in_specs=[SM] + [VM] * (len(cols) + len(rows)),
        out_specs=[VM] * 4,
        scratch_shapes=[pltpu.VMEM((ROWS * BS, NG * CG * BS), BF)],
        compiler_params=PARAMS,
        name="square",
    )(pos, *cols, *rows)
    lows = col_gather(low, BLK)
    out = pl.pallas_call(
        cube_kernel,
        out_shape=jax.ShapeDtypeStruct((BLK, BS), BF),
        in_specs=[SM] + [VM] * (3 + len(lows)),
        out_specs=VM,
        scratch_shapes=[pltpu.VMEM((ROWS * BS, NG * CG * BS), BF)],
        compiler_params=PARAMS,
        name="cube",
    )(pos, metas, b, square, *lows)
    return out.reshape(density.shape)


def solution(mesh):
    return jax.shard_map(
        local,
        mesh=mesh,
        in_specs=(P("row", "col", None, None), P("row", "col"), P("row", "col")),
        out_specs=P("row", "col", None, None),
        check_vma=False,
    )
```

time: 347 us -> 205 us (0.59)
  the two profiles are of different devices: /device:TPU:128 before, /device:TPU:8 now
where the time goes in v1:
time: 205 us; the launch traced here: 203 us
  starting transfers between devices  102 us (50%)
  waiting for transfers between devices  68.2 us (33%)
  local copies, waits for them, and re-layouts  19.9 us (10%)
  Pallas kernels  10.7 us (5%)
    ppermute x6, waiting for transfers between devices, col_gather(): pieces = [own] + [lax.ppermute(own, 'col', yl_shift(s)) for s in (1, 3, 2)]  24.8 us
    ppermute x8, starting transfers between devices, row_gather(): lax.ppermute(current if step < 3 else current[:PAY], 'row', Z_STEP)  24.1 us
    ppermute x8, starting transfers between devices, row_gather(): lax.ppermute(a, 'row', CORE_SWAP)  19.9 us
    ppermute x6, starting transfers between devices, col_gather(): pieces = [own] + [lax.ppermute(own, 'col', yl_shift(s)) for s in (1, 3, 2)]  19.6 us
    unnamed x52, local copies, waits for them, and re-layouts  16.9 us
    ppermute x2, waiting for transfers between devices, col_gather(): right = lax.ppermute(line, 'col', x_shift(3))  15 us
    ppermute x2, starting transfers between devices, col_gather(): far_hi = lax.ppermute(right[2 * rows:], 'col', x_shift(3))  10.4 us
    ppermute x2, starting transfers between devices, col_gather(): right = lax.ppermute(line, 'col', x_shift(3))  9.8 us
  transfers between devices with their start and end apart: 33, of which 11 were waited for; matrix products, arithmetic and copies ran while one was open for 1% of the time, Pallas kernels for 0%

profile of v1, /device:TPU:8, one launch (start us, length us, event | category | flops | bytes accessed | tf_op | source)
XLA Modules:
  0.0 203.4 jit_solution(13847626034682548577)
XLA Ops:
  1.9 6.8 %collective-permute-start.16 = (bf16[784,128]{1,0:T(8,128)(2,1)S(1)}, bf16[784,128]{1,0:T(8,128)(2,1)S(1)}, u32[]{:S(2)}, u32[]{:S(2)}) collective-permute-start(bf16[784,128]{1,0:T(8,128)(2,1)S(1)} %pad_maximum_fusion), channel_id=1, source_target_pairs={{0,32},{16,48},{32,0},{48,16},{64,96},{80,112},{96,64},{112,80},{1... | collective-permute-start | bytes 602120 | tf_op jit(solution)/shard_map/ppermute | solution.py:51
  10.6 6.5 %collective-permute-done.16 = bf16[784,128]{1,0:T(8,128)(2,1)S(1)} collective-permute-done((bf16[784,128]{1,0:T(8,128)(2,1)S(1)}, bf16[784,128]{1,0:T(8,128)(2,1)S(1)}, u32[]{:S(2)}, u32[]{:S(2)}) %collective-permute-start.16) | collective-permute-done | bytes 200736 | tf_op jit(solution)/shard_map/ppermute | solution.py:51
  20.2 4.3 %collective-permute-start.8 = (bf16[1568,128]{1,0:T(8,128)(2,1)S(1)}, bf16[1568,128]{1,0:T(8,128)(2,1)S(1)}, u32[]{:S(2)}, u32[]{:S(2)}) collective-permute-start(bf16[1568,128]{1,0:T(8,128)(2,1)S(1)} %concatenate.19.arrays_5_), channel_id=1, source_target_pairs={{0,64},{16,464},{32,96},{48,496},{64,128},{80,16},{96,160},{112,48... | collective-permute-start | bytes 1204232 | tf_op jit(solution)/shard_map/ppermute | solution.py:58
  24.6 4.3 %collective-permute-start.18 = (bf16[1568,128]{1,0:T(8,128)(2,1)S(1)}, bf16[1568,128]{1,0:T(8,128)(2,1)S(1)}, u32[]{:S(2)}, u32[]{:S(2)}) collective-permute-start(bf16[1568,128]{1,0:T(8,128)(2,1)S(1)} %constant_dynamic-update-slice_fusion.arrays_14_), channel_id=1, source_target_pairs={{0,64},{16,464},{32,96},{48,496},{64,128},{80,16},{96,160},{112,48... | collective-permute-start | bytes 1204232 | tf_op jit(solution)/shard_map/ppermute | solution.py:58
  28.9 4.3 %collective-permute-start.2 = (bf16[784,128]{1,0:T(8,128)(2,1)S(1)}, bf16[784,128]{1,0:T(8,128)(2,1)S(1)}, u32[]{:S(2)}, u32[]{:S(2)}) collective-permute-start(bf16[784,128]{1,0:T(8,128)(2,1)S(1)} %pad_maximum_fusion), channel_id=1, source_target_pairs={{0,2},{1,3},{2,0},{3,1},{4,6},{5,7},{6,4},{7,5},{8,10},{9,11},{10,... | collective-permute-start | bytes 602120 | tf_op jit(solution)/shard_map/ppermute | solution.py:32
  33.2 4.2 %collective-permute-start.1 = (bf16[784,128]{1,0:T(8,128)(2,1)S(1)}, bf16[784,128]{1,0:T(8,128)(2,1)S(1)}, u32[]{:S(2)}, u32[]{:S(2)}) collective-permute-start(bf16[784,128]{1,0:T(8,128)(2,1)S(1)} %pad_maximum_fusion), channel_id=1, source_target_pairs={{0,3},{1,0},{2,1},{3,2},{4,7},{5,4},{6,5},{7,6},{8,11},{9,8},{10,9... | collective-permute-start | bytes 602120 | tf_op jit(solution)/shard_map/ppermute | solution.py:32
  42.6 7.8 %collective-permute-done.1 = bf16[784,128]{1,0:T(8,128)(2,1)S(1)} collective-permute-done((bf16[784,128]{1,0:T(8,128)(2,1)S(1)}, bf16[784,128]{1,0:T(8,128)(2,1)S(1)}, u32[]{:S(2)}, u32[]{:S(2)}) %collective-permute-start.1) | collective-permute-done | bytes 200736 | tf_op jit(solution)/shard_map/ppermute | solution.py:32
  51.8 4.7 %collective-permute-start.4 = (bf16[3136,128]{1,0:T(8,128)(2,1)S(1)}, bf16[3136,128]{1,0:T(8,128)(2,1)S(1)}, u32[]{:S(2)}, u32[]{:S(2)}) collective-permute-start(bf16[3136,128]{1,0:T(8,128)(2,1)S(1)} %concatenate.18.arrays_0_), channel_id=1, source_target_pairs={{0,12},{1,13},{2,14},{3,15},{4,0},{5,1},{6,2},{7,3},{8,4},{9,5},{1... | collective-permute-start | bytes 2408456 | tf_op jit(solution)/shard_map/ppermute | solution.py:35
  58.5 5.4 %collective-permute-start.9 = (bf16[1568,128]{1,0:T(8,128)(2,1)S(1)}, bf16[1568,128]{1,0:T(8,128)(2,1)S(1)}, u32[]{:S(2)}, u32[]{:S(2)}) collective-permute-start(bf16[1568,128]{1,0:T(8,128)(2,1)S(1)} %collective-permute-done.8.arrays_6_), channel_id=1, source_target_pairs={{0,64},{16,464},{32,96},{48,496},{64,128},{80,16},{96,160},{112,48... | collective-permute-start | bytes 1204232 | tf_op jit(solution)/shard_map/ppermute | solution.py:58
  65.8 6.7 %collective-permute-done.9.arrays_7_ = bf16[1568,128]{1,0:T(8,128)(2,1)S(1)} collective-permute-done((bf16[1568,128]{1,0:T(8,128)(2,1)S(1)}, bf16[1568,128]{1,0:T(8,128)(2,1)S(1)}, u32[]{:S(2)}, u32[]{:S(2)}) %collective-permute-start.9) | collective-permute-done | bytes 401440 | tf_op jit(solution)/shard_map/ppermute | solution.py:58
  78.9 3.7 %collective-permute-start.12 = (bf16[1568,128]{1,0:T(8,128)(2,1)S(1)}, bf16[1568,128]{1,0:T(8,128)(2,1)S(1)}, u32[]{:S(2)}, u32[]{:S(2)}) collective-permute-start(bf16[1568,128]{1,0:T(8,128)(2,1)S(1)} %collective-permute-done.8.arrays_6_), channel_id=1, source_target_pairs={{0,16},{16,0},{32,48},{48,32},{64,80},{80,64},{96,112},{112,96},{1... | collective-permute-start | bytes 1204232 | tf_op jit(solution)/shard_map/ppermute | solution.py:61
  88.0 4.8 %collective-permute-start.6 = (bf16[1568,128]{1,0:T(8,128)(2,1)S(1)}, bf16[1568,128]{1,0:T(8,128)(2,1)S(1)}, u32[]{:S(2)}, u32[]{:S(2)}) collective-permute-start(bf16[1568,128]{1,0:T(8,128)(2,1)S(1)} %slice.25), channel_id=1, source_target_pairs={{0,12},{1,13},{2,14},{3,15},{4,0},{5,1},{6,2},{7,3},{8,4},{9,5},{1... | collective-permute-start | bytes 1204232 | tf_op jit(solution)/shard_map/ppermute | solution.py:37
  104.3 3.7 %collective-permute-start.14 = (bf16[1568,128]{1,0:T(8,128)(2,1)S(1)}, bf16[1568,128]{1,0:T(8,128)(2,1)}, u32[]{:S(2)}, u32[]{:S(2)}) collective-permute-start(bf16[1568,128]{1,0:T(8,128)(2,1)S(1)} %collective-permute-done.10.arrays_8_), channel_id=1, source_target_pairs={{0,16},{16,0},{32,48},{48,32},{64,80},{80,64},{96,112},{112,96},{1... | collective-permute-start | bytes 1204232 | tf_op jit(solution)/shard_map/ppermute | solution.py:61
  129.0 6.3 %square.1 = (f32[768,128]{1,0:T(8,128)S(1)}, bf16[768,128]{1,0:T(8,128)(2,1)S(1)}, bf16[8192,512]{1,0:T(8,128)(2,1)S(1)}, bf16[256,128]{1,0:T(8,128)(2,1)S(1)}) custom-call(s32[5]{0:T(128)S(1)} %stack.23.pos, bf16[3136,128]{1,0:T(8,128)(2,1)S(1)} %concatenate.18.arrays_0_, bf16[3136,128]{1,0:T(8,128)(2,1)S(1)} %copy-done.1, ...), custom_call_target="tpu_custom_call" | custom-call | tf_op jit(solution)/shard_map/square/pallas_call | solution.py:186
  135.3 3.4 %collective-permute-start.26 = (bf16[768,128]{1,0:T(8,128)(2,1)S(1)}, bf16[768,128]{1,0:T(8,128)(2,1)S(1)}, u32[]{:S(2)}, u32[]{:S(2)}) collective-permute-start(bf16[768,128]{1,0:T(8,128)(2,1)S(1)} %get-tuple-element.12), channel_id=1, source_target_pairs={{0,1},{1,2},{2,3},{3,0},{4,5},{5,6},{6,7},{7,4},{8,9},{9,10},{10,1... | collective-permute-start | bytes 589832 | tf_op jit(solution)/shard_map/ppermute | solution.py:32
  138.6 3.9 %collective-permute-start.28 = (bf16[768,128]{1,0:T(8,128)(2,1)S(1)}, bf16[768,128]{1,0:T(8,128)(2,1)S(1)}, u32[]{:S(2)}, u32[]{:S(2)}) collective-permute-start(bf16[768,128]{1,0:T(8,128)(2,1)S(1)} %get-tuple-element.12), channel_id=1, source_target_pairs={{0,2},{1,3},{2,0},{3,1},{4,6},{5,7},{6,4},{7,5},{8,10},{9,11},{10,... | collective-permute-start | bytes 589832 | tf_op jit(solution)/shard_map/ppermute | solution.py:32
  144.5 7.5 %collective-permute-done.26 = bf16[768,128]{1,0:T(8,128)(2,1)S(1)} collective-permute-done((bf16[768,128]{1,0:T(8,128)(2,1)S(1)}, bf16[768,128]{1,0:T(8,128)(2,1)S(1)}, u32[]{:S(2)}, u32[]{:S(2)}) %collective-permute-start.26) | collective-permute-done | bytes 196640 | tf_op jit(solution)/shard_map/ppermute | solution.py:32
  152.0 6.1 %collective-permute-done.27 = bf16[768,128]{1,0:T(8,128)(2,1)S(1)} collective-permute-done((bf16[768,128]{1,0:T(8,128)(2,1)S(1)}, bf16[768,128]{1,0:T(8,128)(2,1)S(1)}, u32[]{:S(2)}, u32[]{:S(2)}) %collective-permute-start.27) | collective-permute-done | bytes 196640 | tf_op jit(solution)/shard_map/ppermute | solution.py:32
  158.2 5.1 %collective-permute-start.30 = (bf16[3072,128]{1,0:T(8,128)(2,1)S(1)}, bf16[3072,128]{1,0:T(8,128)(2,1)S(1)}, u32[]{:S(2)}, u32[]{:S(2)}) collective-permute-start(bf16[3072,128]{1,0:T(8,128)(2,1)S(1)} %constant_dynamic-update-slice_fusion.2.refs_0_), channel_id=1, source_target_pairs={{0,12},{1,13},{2,14},{3,15},{4,0},{5,1},{6,2},{7,3},{8,4},{9,5},{1... | collective-permute-start | bytes 2359304 | tf_op jit(solution)/shard_map/ppermute | solution.py:35
  165.3 15.0 %collective-permute-done.30.refs_2_ = bf16[3072,128]{1,0:T(8,128)(2,1)S(1)} collective-permute-done((bf16[3072,128]{1,0:T(8,128)(2,1)S(1)}, bf16[3072,128]{1,0:T(8,128)(2,1)S(1)}, u32[]{:S(2)}, u32[]{:S(2)}) %collective-permute-start.30) | collective-permute-done | bytes 786464 | tf_op jit(solution)/shard_map/ppermute | solution.py:35
  180.4 5.6 %collective-permute-start.32 = (bf16[1536,128]{1,0:T(8,128)(2,1)S(1)}, bf16[1536,128]{1,0:T(8,128)(2,1)S(1)}, u32[]{:S(2)}, u32[]{:S(2)}) collective-permute-start(bf16[1536,128]{1,0:T(8,128)(2,1)S(1)} %slice.29), channel_id=1, source_target_pairs={{0,12},{1,13},{2,14},{3,15},{4,0},{5,1},{6,2},{7,3},{8,4},{9,5},{1... | collective-permute-start | bytes 1179656 | tf_op jit(solution)/shard_map/ppermute | solution.py:37
  188.0 5.7 %collective-permute-done.32.refs_4_ = bf16[1536,128]{1,0:T(8,128)(2,1)S(1)} collective-permute-done((bf16[1536,128]{1,0:T(8,128)(2,1)S(1)}, bf16[1536,128]{1,0:T(8,128)(2,1)S(1)}, u32[]{:S(2)}, u32[]{:S(2)}) %collective-permute-start.32) | collective-permute-done | bytes 393248 | tf_op jit(solution)/shard_map/ppermute | solution.py:37
  193.7 5.4 %collective-permute-done.31.refs_3_ = bf16[1536,128]{1,0:T(8,128)(2,1)S(1)} collective-permute-done((bf16[1536,128]{1,0:T(8,128)(2,1)S(1)}, bf16[1536,128]{1,0:T(8,128)(2,1)S(1)}, u32[]{:S(2)}, u32[]{:S(2)}) %collective-permute-start.31) | collective-permute-done | bytes 393248 | tf_op jit(solution)/shard_map/ppermute | solution.py:36
  199.1 4.4 %cube.1 = bf16[768,128]{1,0:T(8,128)(2,1)} custom-call(s32[5]{0:T(128)S(1)} %stack.23.pos, bf16[256,128]{1,0:T(8,128)(2,1)S(1)} %get-tuple-element.9.meta_ref, bf16[8192,512]{1,0:T(8,128)(2,1)S(1)} %get-tuple-element.10.b_ref, f32[768,128]{1,0:T(8,128)S(1)} %get-tuple-element.11.square_ref, ...), custom_call_target="tpu_custom_call" | custom-call | tf_op jit(solution)/shard_map/cube/pallas_call | solution.py:201
  (112 shorter events, 67.0 us)
Async XLA Ops:
  1.9 15.2 %collective-permute-start.16 = (bf16[784,128]{1,0:T(8,128)(2,1)S(1)}, bf16[784,128]{1,0:T(8,128)(2,1)S(1)}, u32[]{:S(2)}, u32[]{:S(2)}) collective-permute-start(bf16[784,128]{1,0:T(8,128)(2,1)S(1)} %pad_maximum_fusion), channel_id=1, source_target_pairs={{0,32},{16,48},{32,0},{48,16},{64,96},{80,112},{96,64},{112,80},{1... | collective-permute-start | bytes 602120 | tf_op jit(solution)/shard_map/ppermute | solution.py:51
  20.2 38.2 %collective-permute-start.8 = (bf16[1568,128]{1,0:T(8,128)(2,1)S(1)}, bf16[1568,128]{1,0:T(8,128)(2,1)S(1)}, u32[]{:S(2)}, u32[]{:S(2)}) collective-permute-start(bf16[1568,128]{1,0:T(8,128)(2,1)S(1)} %concatenate.19.arrays_5_), channel_id=1, source_target_pairs={{0,64},{16,464},{32,96},{48,496},{64,128},{80,16},{96,160},{112,48... | collective-permute-start | bytes 1204232 | tf_op jit(solution)/shard_map/ppermute | solution.py:58
  24.6 39.3 %collective-permute-start.18 = (bf16[1568,128]{1,0:T(8,128)(2,1)S(1)}, bf16[1568,128]{1,0:T(8,128)(2,1)S(1)}, u32[]{:S(2)}, u32[]{:S(2)}) collective-permute-start(bf16[1568,128]{1,0:T(8,128)(2,1)S(1)} %constant_dynamic-update-slice_fusion.arrays_14_), channel_id=1, source_target_pairs={{0,64},{16,464},{32,96},{48,496},{64,128},{80,16},{96,160},{112,48... | collective-permute-start | bytes 1204232 | tf_op jit(solution)/shard_map/ppermute | solution.py:58
  28.9 13.7 %collective-permute-start.2 = (bf16[784,128]{1,0:T(8,128)(2,1)S(1)}, bf16[784,128]{1,0:T(8,128)(2,1)S(1)}, u32[]{:S(2)}, u32[]{:S(2)}) collective-permute-start(bf16[784,128]{1,0:T(8,128)(2,1)S(1)} %pad_maximum_fusion), channel_id=1, source_target_pairs={{0,2},{1,3},{2,0},{3,1},{4,6},{5,7},{6,4},{7,5},{8,10},{9,11},{10,... | collective-permute-start | bytes 602120 | tf_op jit(solution)/shard_map/ppermute | solution.py:32
  33.2 17.2 %collective-permute-start.1 = (bf16[784,128]{1,0:T(8,128)(2,1)S(1)}, bf16[784,128]{1,0:T(8,128)(2,1)S(1)}, u32[]{:S(2)}, u32[]{:S(2)}) collective-permute-start(bf16[784,128]{1,0:T(8,128)(2,1)S(1)} %pad_maximum_fusion), channel_id=1, source_target_pairs={{0,3},{1,0},{2,1},{3,2},{4,7},{5,4},{6,5},{7,6},{8,11},{9,8},{10,9... | collective-permute-start | bytes 602120 | tf_op jit(solution)/shard_map/ppermute | solution.py:32
  51.8 30.8 %collective-permute-start.4 = (bf16[3136,128]{1,0:T(8,128)(2,1)S(1)}, bf16[3136,128]{1,0:T(8,128)(2,1)S(1)}, u32[]{:S(2)}, u32[]{:S(2)}) collective-permute-start(bf16[3136,128]{1,0:T(8,128)(2,1)S(1)} %concatenate.18.arrays_0_), channel_id=1, source_target_pairs={{0,12},{1,13},{2,14},{3,15},{4,0},{5,1},{6,2},{7,3},{8,4},{9,5},{1... | collective-permute-start | bytes 2408456 | tf_op jit(solution)/shard_map/ppermute | solution.py:35
  56.5 28.1 %collective-permute-start.3 = (bf16[3136,128]{1,0:T(8,128)(2,1)S(1)}, bf16[3136,128]{1,0:T(8,128)(2,1)S(1)}, u32[]{:S(2)}, u32[]{:S(2)}) collective-permute-start(bf16[3136,128]{1,0:T(8,128)(2,1)S(1)} %concatenate.18.arrays_0_), channel_id=1, source_target_pairs={{0,4},{1,5},{2,6},{3,7},{4,8},{5,9},{6,10},{7,11},{8,12},{9,13},{1... | collective-permute-start | bytes 2408456 | tf_op jit(solution)/shard_map/ppermute | solution.py:34
  58.5 14.1 %collective-permute-start.9 = (bf16[1568,128]{1,0:T(8,128)(2,1)S(1)}, bf16[1568,128]{1,0:T(8,128)(2,1)S(1)}, u32[]{:S(2)}, u32[]{:S(2)}) collective-permute-start(bf16[1568,128]{1,0:T(8,128)(2,1)S(1)} %collective-permute-done.8.arrays_6_), channel_id=1, source_target_pairs={{0,64},{16,464},{32,96},{48,496},{64,128},{80,16},{96,160},{112,48... | collective-permute-start | bytes 1204232 | tf_op jit(solution)/shard_map/ppermute | solution.py:58
  63.9 13.1 %collective-permute-start.19 = (bf16[1568,128]{1,0:T(8,128)(2,1)S(1)}, bf16[1568,128]{1,0:T(8,128)(2,1)}, u32[]{:S(2)}, u32[]{:S(2)}) collective-permute-start(bf16[1568,128]{1,0:T(8,128)(2,1)S(1)} %collective-permute-done.18.arrays_15_), channel_id=1, source_target_pairs={{0,64},{16,464},{32,96},{48,496},{64,128},{80,16},{96,160},{112,48... | collective-permute-start | bytes 1204232 | tf_op jit(solution)/shard_map/ppermute | solution.py:58
  72.6 15.4 %collective-permute-start.10 = (bf16[1568,128]{1,0:T(8,128)(2,1)S(1)}, bf16[1568,128]{1,0:T(8,128)(2,1)S(1)}, u32[]{:S(2)}, u32[]{:S(2)}) collective-permute-start(bf16[1568,128]{1,0:T(8,128)(2,1)S(1)} %collective-permute-done.9.arrays_7_), channel_id=1, source_target_pairs={{0,64},{16,464},{32,96},{48,496},{64,128},{80,16},{96,160},{112,48... | collective-permute-start | bytes 1204232 | tf_op jit(solution)/shard_map/ppermute | solution.py:58
  77.0 15.9 %collective-permute-start.20 = (bf16[1568,128]{1,0:T(8,128)(2,1)}, bf16[1568,128]{1,0:T(8,128)(2,1)S(1)}, u32[]{:S(2)}, u32[]{:S(2)}) collective-permute-start(bf16[1568,128]{1,0:T(8,128)(2,1)} %collective-permute-done.19.arrays_16_), channel_id=1, source_target_pairs={{0,64},{16,464},{32,96},{48,496},{64,128},{80,16},{96,160},{112,48... | collective-permute-start | bytes 1204232 | tf_op jit(solution)/shard_map/ppermute | solution.py:58
  78.9 15.9 %collective-permute-start.12 = (bf16[1568,128]{1,0:T(8,128)(2,1)S(1)}, bf16[1568,128]{1,0:T(8,128)(2,1)S(1)}, u32[]{:S(2)}, u32[]{:S(2)}) collective-permute-start(bf16[1568,128]{1,0:T(8,128)(2,1)S(1)} %collective-permute-done.8.arrays_6_), channel_id=1, source_target_pairs={{0,16},{16,0},{32,48},{48,32},{64,80},{80,64},{96,112},{112,96},{1... | collective-permute-start | bytes 1204232 | tf_op jit(solution)/shard_map/ppermute | solution.py:61
  82.6 14.9 %collective-permute-start.22 = (bf16[1568,128]{1,0:T(8,128)(2,1)}, bf16[1568,128]{1,0:T(8,128)(2,1)S(1)}, u32[]{:S(2)}, u32[]{:S(2)}) collective-permute-start(bf16[1568,128]{1,0:T(8,128)(2,1)} %copy-done.10), channel_id=1, source_target_pairs={{0,16},{16,0},{32,48},{48,32},{64,80},{80,64},{96,112},{112,96},{1... | collective-permute-start | bytes 1204232 | tf_op jit(solution)/shard_map/ppermute | solution.py:61
  84.6 15.6 %collective-permute-start.13 = (bf16[1568,128]{1,0:T(8,128)(2,1)S(1)}, bf16[1568,128]{1,0:T(8,128)(2,1)S(1)}, u32[]{:S(2)}, u32[]{:S(2)}) collective-permute-start(bf16[1568,128]{1,0:T(8,128)(2,1)S(1)} %collective-permute-done.9.arrays_7_), channel_id=1, source_target_pairs={{0,16},{16,0},{32,48},{48,32},{64,80},{80,64},{96,112},{112,96},{1... | collective-permute-start | bytes 1204232 | tf_op jit(solution)/shard_map/ppermute | solution.py:61
  88.0 15.5 %collective-permute-start.6 = (bf16[1568,128]{1,0:T(8,128)(2,1)S(1)}, bf16[1568,128]{1,0:T(8,128)(2,1)S(1)}, u32[]{:S(2)}, u32[]{:S(2)}) collective-permute-start(bf16[1568,128]{1,0:T(8,128)(2,1)S(1)} %slice.25), channel_id=1, source_target_pairs={{0,12},{1,13},{2,14},{3,15},{4,0},{5,1},{6,2},{7,3},{8,4},{9,5},{1... | collective-permute-start | bytes 1204232 | tf_op jit(solution)/shard_map/ppermute | solution.py:37
  92.8 15.2 %collective-permute-start.5 = (bf16[1568,128]{1,0:T(8,128)(2,1)S(1)}, bf16[1568,128]{1,0:T(8,128)(2,1)S(1)}, u32[]{:S(2)}, u32[]{:S(2)}) collective-permute-start(bf16[1568,128]{1,0:T(8,128)(2,1)S(1)} %slice.24), channel_id=1, source_target_pairs={{0,4},{1,5},{2,6},{3,7},{4,8},{5,9},{6,10},{7,11},{8,12},{9,13},{1... | collective-permute-start | bytes 1204232 | tf_op jit(solution)/shard_map/ppermute | solution.py:36
  95.6 19.6 %collective-permute-start.23 = (bf16[1568,128]{1,0:T(8,128)(2,1)}, bf16[1568,128]{1,0:T(8,128)(2,1)}, u32[]{:S(2)}, u32[]{:S(2)}) collective-permute-start(bf16[1568,128]{1,0:T(8,128)(2,1)} %collective-permute-done.19.arrays_16_), channel_id=1, source_target_pairs={{0,16},{16,0},{32,48},{48,32},{64,80},{80,64},{96,112},{112,96},{1... | collective-permute-start | bytes 1204232 | tf_op jit(solution)/shard_map/ppermute | solution.py:61
  135.3 16.7 %collective-permute-start.26 = (bf16[768,128]{1,0:T(8,128)(2,1)S(1)}, bf16[768,128]{1,0:T(8,128)(2,1)S(1)}, u32[]{:S(2)}, u32[]{:S(2)}) collective-permute-start(bf16[768,128]{1,0:T(8,128)(2,1)S(1)} %get-tuple-element.12), channel_id=1, source_target_pairs={{0,1},{1,2},{2,3},{3,0},{4,5},{5,6},{6,7},{7,4},{8,9},{9,10},{10,1... | collective-permute-start | bytes 589832 | tf_op jit(solution)/shard_map/ppermute | solution.py:32
  138.6 19.6 %collective-permute-start.28 = (bf16[768,128]{1,0:T(8,128)(2,1)S(1)}, bf16[768,128]{1,0:T(8,128)(2,1)S(1)}, u32[]{:S(2)}, u32[]{:S(2)}) collective-permute-start(bf16[768,128]{1,0:T(8,128)(2,1)S(1)} %get-tuple-element.12), channel_id=1, source_target_pairs={{0,2},{1,3},{2,0},{3,1},{4,6},{5,7},{6,4},{7,5},{8,10},{9,11},{10,... | collective-permute-start | bytes 589832 | tf_op jit(solution)/shard_map/ppermute | solution.py:32
  142.5 15.7 %collective-permute-start.27 = (bf16[768,128]{1,0:T(8,128)(2,1)S(1)}, bf16[768,128]{1,0:T(8,128)(2,1)S(1)}, u32[]{:S(2)}, u32[]{:S(2)}) collective-permute-start(bf16[768,128]{1,0:T(8,128)(2,1)S(1)} %get-tuple-element.12), channel_id=1, source_target_pairs={{0,3},{1,0},{2,1},{3,2},{4,7},{5,4},{6,5},{7,6},{8,11},{9,8},{10,9... | collective-permute-start | bytes 589832 | tf_op jit(solution)/shard_map/ppermute | solution.py:32
  158.2 22.1 %collective-permute-start.30 = (bf16[3072,128]{1,0:T(8,128)(2,1)S(1)}, bf16[3072,128]{1,0:T(8,128)(2,1)S(1)}, u32[]{:S(2)}, u32[]{:S(2)}) collective-permute-start(bf16[3072,128]{1,0:T(8,128)(2,1)S(1)} %constant_dynamic-update-slice_fusion.2.refs_0_), channel_id=1, source_target_pairs={{0,12},{1,13},{2,14},{3,15},{4,0},{5,1},{6,2},{7,3},{8,4},{9,5},{1... | collective-permute-start | bytes 2359304 | tf_op jit(solution)/shard_map/ppermute | solution.py:35
  163.4 22.6 %collective-permute-start.29 = (bf16[3072,128]{1,0:T(8,128)(2,1)S(1)}, bf16[3072,128]{1,0:T(8,128)(2,1)S(1)}, u32[]{:S(2)}, u32[]{:S(2)}) collective-permute-start(bf16[3072,128]{1,0:T(8,128)(2,1)S(1)} %constant_dynamic-update-slice_fusion.2.refs_0_), channel_id=1, source_target_pairs={{0,4},{1,5},{2,6},{3,7},{4,8},{5,9},{6,10},{7,11},{8,12},{9,13},{1... | collective-permute-start | bytes 2359304 | tf_op jit(solution)/shard_map/ppermute | solution.py:34
  180.4 13.3 %collective-permute-start.32 = (bf16[1536,128]{1,0:T(8,128)(2,1)S(1)}, bf16[1536,128]{1,0:T(8,128)(2,1)S(1)}, u32[]{:S(2)}, u32[]{:S(2)}) collective-permute-start(bf16[1536,128]{1,0:T(8,128)(2,1)S(1)} %slice.29), channel_id=1, source_target_pairs={{0,12},{1,13},{2,14},{3,15},{4,0},{5,1},{6,2},{7,3},{8,4},{9,5},{1... | collective-permute-start | bytes 1179656 | tf_op jit(solution)/shard_map/ppermute | solution.py:37
  186.0 13.0 %collective-permute-start.31 = (bf16[1536,128]{1,0:T(8,128)(2,1)S(1)}, bf16[1536,128]{1,0:T(8,128)(2,1)S(1)}, u32[]{:S(2)}, u32[]{:S(2)}) collective-permute-start(bf16[1536,128]{1,0:T(8,128)(2,1)S(1)} %slice.28), channel_id=1, source_target_pairs={{0,4},{1,5},{2,6},{3,7},{4,8},{5,9},{6,10},{7,11},{8,12},{9,13},{1... | collective-permute-start | bytes 1179656 | tf_op jit(solution)/shard_map/ppermute | solution.py:36
  (33 other events, 297.9 us)

commit v2 on v1

v2 whole, which is shorter than its diff:
```python
import jax
import jax.numpy as jnp
from jax import lax
from jax.experimental import pallas as pl
from jax.experimental.pallas import tpu as pltpu
from jax.sharding import PartitionSpec as P

BS = 128
KD = 3
CG = 4
ROWS = 2
NG = 16
BLK = ROWS * KD * BS
PAY = BLK + 16
BF = jnp.bfloat16
F32 = jnp.float32

VM = pl.BlockSpec(memory_space=pltpu.VMEM)
SM = pl.BlockSpec(memory_space=pltpu.SMEM)

CORE_SWAP = [(r, r ^ 1) for r in range(32)]
YH_SWAP = [(r, r ^ 2) for r in range(32)]
Z_STEP = [(r, (r + (4 if r % 2 == 0 else 28)) % 32) for r in range(32)]


def yl_shift(s):
    return [(c, c // 4 * 4 + (c + s) % 4) for c in range(16)]


def x_shift(s):
    return [(c, (c + 4 * s) % 16) for c in range(16)]


Z_FAR = [(r, (r + 16) % 32) for r in range(32)]


def fence(token, *values):
    token, *values = lax.optimization_barrier((token, *values))

    def body(in_ref, out_ref):
        out_ref[...] = in_ref[...]

    token = pl.pallas_call(
        body,
        out_shape=jax.ShapeDtypeStruct(token.shape, token.dtype),
        in_specs=[VM],
        out_specs=VM,
        compiler_params=pltpu.CompilerParams(vmem_limit_bytes=1024 * 1024),
        cost_estimate=pl.CostEstimate(flops=50 * 10**9, bytes_accessed=0, transcendentals=0),
        name="fence",
    )(token)
    return lax.optimization_barrier((token, *values))


def cat(*arrays):
    rows = [a.shape[0] for a in arrays]

    def body(*refs):
        at = 0
        for n, ref in zip(rows, refs):
            refs[-1][at : at + n] = ref[...]
            at += n

    return pl.pallas_call(
        body,
        out_shape=jax.ShapeDtypeStruct((sum(rows), BS), BF),
        in_specs=[VM] * len(arrays),
        out_specs=VM,
        compiler_params=pltpu.CompilerParams(vmem_limit_bytes=2 * 1024 * 1024),
        name="cat",
    )(*arrays)


def gather_all(own):
    def row(a, perm):
        return lax.ppermute(a, "row", perm)

    def col(a, perm):
        return lax.ppermute(a, "col", perm)

    tok = jnp.zeros((8, BS), F32)
    other = row(own, CORE_SWAP)
    own_y = row(own, YH_SWAP)
    line1 = col(own, yl_shift(1))
    w0 = cat(own, other)
    tok, w0, own = fence(tok, w0, own)
    w1 = row(w0, Z_STEP)
    line3 = col(own, yl_shift(3))
    line2 = col(own, yl_shift(2))
    one = cat(own, line1)
    other_y = row(own_y, CORE_SWAP)
    v0 = cat(own_y, other_y)
    tok, v0, one, own_y = fence(tok, v0, one, own_y)
    v1 = row(v0, Z_STEP)
    left1, right1 = col(one, x_shift(1)), col(one, x_shift(3))
    w2 = row(w1, Z_STEP)
    two = cat(line3, line2)
    tok, two, w1, w2, own_y = fence(tok, two, w1, w2, own_y)
    far_y = row(own_y, Z_FAR)
    left2, right2 = col(two, x_shift(1)), col(two, x_shift(3))
    v2 = row(v1, Z_STEP)
    w3 = row(w2, Z_STEP)
    tok, left1, right1, v1, v2 = fence(tok, left1, right1, v1, v2)
    far1, far2 = col(left1[:PAY], x_shift(1)), col(right1[PAY:], x_shift(3))
    v3 = row(v2, Z_STEP)
    w4 = row(w3[:PAY], Z_STEP)
    tok, left2, right2, far_y, w3 = fence(tok, left2, right2, far_y, w3)
    far3, far4 = col(left2[:PAY], x_shift(1)), col(right2[PAY:], x_shift(3))
    ws = cat(w1, w2, w3, w4)
    ws_other = row(ws, CORE_SWAP)
    vs = cat(v1, v2, far_y, v3)
    vs_other = row(vs, CORE_SWAP)
    rows = [w0, v0, ws, ws_other, vs, vs_other]
    pieces = [(yh, n, 0, yh, n) for yh in range(2) for n in range(2)]
    for n, (step, c) in enumerate(((1, 0), (1, 1), (2, 0), (2, 1), (3, 0), (3, 1), (4, 0))):
        pieces += [(2, n, step, 0, c), (3, n, -step, 0, 1 - c)]
    for n, (step, c) in enumerate(((1, 0), (1, 1), (2, 0), (2, 1), (4, 0), (3, 0), (3, 1))):
        pieces += [(4, n, step, 1, c), (5, n, -step, 1, 1 - c)]
    return [one, left1, right1, two, left2, right2, far1, far2, far3, far4], rows, pieces


def col_gather(own, rows):
    near = [lax.ppermute(own, "col", yl_shift(s)) for s in (1, 3, 2)]
    one = jnp.concatenate([own, near[0]], axis=0)
    left1 = lax.ppermute(one, "col", x_shift(1))
    right1 = lax.ppermute(one, "col", x_shift(3))
    two = jnp.concatenate(near[1:], axis=0)
    left2 = lax.ppermute(two, "col", x_shift(1))
    right2 = lax.ppermute(two, "col", x_shift(3))
    far1 = lax.ppermute(left1[:rows], "col", x_shift(1))
    far2 = lax.ppermute(right1[rows:], "col", x_shift(3))
    far3 = lax.ppermute(left2[:rows], "col", x_shift(1))
    far4 = lax.ppermute(right2[rows:], "col", x_shift(3))
    return [one, left1, right1, two, left2, right2, far1, far2, far3, far4]


COL_PIECES = (
    [(a, n, dx, dy) for a, dx in ((0, 0), (1, 3), (2, 1)) for n, dy in ((0, 0), (1, 3))]
    + [(a, n, dx, dy) for a, dx in ((3, 0), (4, 3), (5, 1)) for n, dy in ((0, 1), (1, 2))]
    + [(6, 0, 2, 0), (7, 0, 2, 3), (8, 0, 2, 1), (9, 0, 2, 2)]
)


def meta_rows(meta):
    wide = meta.astype(F32)
    return [
        jnp.broadcast_to(wide[s : s + 1], (16, BS)).astype(BF) for s in range(ROWS * KD)
    ]


def spread(src, base, slots, store):
    masks = [[m == jnp.full((16, BS), q, BF) for q in range(CG)] for m in slots]

    def step(n, _):
        r = pl.multiple_of(n * 16, 16)
        v = [src[pl.ds(base + t * BS + r, 16), :] for t in range(KD)]
        zero = jnp.zeros((16, BS), BF)
        for q in range(CG):
            d = zero
            for t in range(KD):
                d = jnp.where(masks[t][q], v[t], d)
            store(r, q, d)
        return 0

    lax.fori_loop(0, BS // 16, step, 0, unroll=True)


def spread_strip(src, piece, rows, meta, group, a_ref):
    slots = meta_rows(meta)
    for i in range(ROWS):

        def store(r, q, d, i=i):
            col = pl.multiple_of(group * (CG * BS) + q * BS, BS)
            a_ref[pl.ds(i * BS + r, 16), pl.ds(col, BS)] = d

        spread(src, piece * rows + i * KD * BS, slots[i * KD : (i + 1) * KD], store)


def dot(a_ref, b_ref):
    return jnp.dot(a_ref[...], b_ref[...], preferred_element_type=F32)


def pick(acc, slots):
    out = []
    for i in range(ROWS):
        for t in range(KD):
            m = slots[i * KD + t].astype(F32)[0:1]
            d = jnp.zeros((BS, BS), F32)
            for q in range(CG):
                d = jnp.where(m == float(q), acc[i * BS : (i + 1) * BS, q * BS : (q + 1) * BS], d)
            out.append(d)
    return out


def fetch(arrays, buffers, sems):
    copies = [pltpu.make_async_copy(a, b, sems.at[n]) for n, (a, b) in enumerate(zip(arrays, buffers))]
    for copy in copies:
        copy.start()
    return copies


def group_of(x, yl, dx, dy):
    return ((x + dx) & 3) * 4 + ((yl + dy) & 3)


def square_kernel(n_col, n_row, row_pieces, pos, *refs):
    arrays, rest = refs[: n_col + n_row], refs[n_col + n_row :]
    square_ref, low_ref, b_out, meta_ref, a_ref, b_ref = rest[:6]
    buffers, sems, b_sem = rest[6:-2], rest[-2], rest[-1]
    copies = fetch(arrays, buffers, sems)
    cols, rows = buffers[:n_col], buffers[n_col:]
    z, yh, core, x, yl = (pos[n] for n in range(5))
    sign = 1 - 2 * core
    for arr in range(n_row):
        copies[n_col + arr].wait()
        for piece, step, dyh, dcore in [p[1:] for p in row_pieces if p[0] == arr]:
            src = rows[arr]
            group = ((z - sign * step) & 7) * 2 + (yh ^ dyh)
            slots = meta_rows(src[piece * PAY + BLK : (piece + 1) * PAY])
            for i in range(ROWS):
                top = pl.multiple_of((group * CG + (core ^ dcore) * 2 + i) * BS, BS)

                def store(r, q, d, top=top):
                    b_ref[pl.ds(top + r, 16), q * BS : (q + 1) * BS] = d

                spread(src, piece * PAY + i * KD * BS, slots[i * KD : (i + 1) * KD], store)
    b_copy = pltpu.make_async_copy(b_ref, b_out, b_sem)
    b_copy.start()
    for arr in range(n_col):
        copies[arr].wait()
        for n, (a, piece, dx, dy) in enumerate(COL_PIECES):
            if a == arr:
                src = cols[arr]
                meta = src[piece * PAY + BLK : (piece + 1) * PAY]
                at = pl.multiple_of(group_of(x, yl, dx, dy) * 16, 16)
                meta_ref[pl.ds(at, 16), :] = meta
                spread_strip(src, piece, PAY, meta, group_of(x, yl, dx, dy), a_ref)
    own = meta_rows(cols[0][BLK:PAY])
    for s, d in enumerate(pick(dot(a_ref, b_ref), own)):
        square_ref[s * BS : (s + 1) * BS] = d
        low_ref[s * BS : (s + 1) * BS] = d.astype(BF)
    b_copy.wait()


def cube_kernel(n_col, pos, meta_ref, square_ref, b_in, *refs):
    arrays, rest = refs[:n_col], refs[n_col:]
    out_ref, a_ref, b_ref, buffers, sems = rest[0], rest[1], rest[2], rest[3:-1], rest[-1]
    copies = fetch((b_in, *arrays), (b_ref, *buffers), sems)
    x, yl = pos[3], pos[4]
    for arr in range(n_col):
        copies[1 + arr].wait()
        for a, piece, dx, dy in COL_PIECES:
            if a == arr:
                group = group_of(x, yl, dx, dy)
                meta = meta_ref[pl.ds(pl.multiple_of(group * 16, 16), 16), :]
                spread_strip(buffers[arr], piece, BLK, meta, group, a_ref)
    copies[0].wait()
    at = pl.multiple_of(group_of(x, yl, 0, 0) * 16, 16)
    own = meta_rows(meta_ref[pl.ds(at, 16), :])
    for s, d in enumerate(pick(dot(a_ref, b_ref), own)):
        square = square_ref[s * BS : (s + 1) * BS]
        out_ref[s * BS : (s + 1) * BS] = (3.0 * square - 2.0 * d).astype(BF)


HB = pl.BlockSpec(memory_space=pl.ANY)
PARAMS = pltpu.CompilerParams(vmem_limit_bytes=56 * 1024 * 1024)
A_SCRATCH = pltpu.VMEM((ROWS * BS, NG * CG * BS), BF)
B_SHAPE = (NG * CG * BS, CG * BS)


def local(density, block_cols, block_counts):
    slot = lax.broadcasted_iota(jnp.int32, (ROWS, KD), 1)
    where = jnp.where(slot < block_counts, block_cols % CG, -1).reshape(ROWS * KD, 1)
    meta = jnp.broadcast_to(where, (ROWS * KD, BS)).astype(BF)
    own = jnp.concatenate(
        [density.reshape(BLK, BS), meta, jnp.zeros((16 - ROWS * KD, BS), BF)], axis=0
    )
    r, c = lax.axis_index("row"), lax.axis_index("col")
    pos = jnp.stack([r // 4, r // 2 % 2, r % 2, c // 4, c % 4]).astype(jnp.int32)
    cols, rows, row_pieces = gather_all(own)

    def square_call(pos, *refs):
        square_kernel(len(cols), len(rows), row_pieces, pos, *refs)

    square, low, b, metas = pl.pallas_call(
        square_call,
        out_shape=[
            jax.ShapeDtypeStruct((BLK, BS), F32),
            jax.ShapeDtypeStruct((BLK, BS), BF),
            jax.ShapeDtypeStruct(B_SHAPE, BF),
            jax.ShapeDtypeStruct((NG * 16, BS), BF),
        ],
        in_specs=[SM] + [HB] * (len(cols) + len(rows)),
        out_specs=[VM, VM, HB, VM],
        scratch_shapes=[A_SCRATCH, pltpu.VMEM(B_SHAPE, BF)]
        + [pltpu.VMEM(a.shape, BF) for a in cols + rows]
        + [pltpu.SemaphoreType.DMA((len(cols) + len(rows),)), pltpu.SemaphoreType.DMA(())],
        compiler_params=PARAMS,
        name="square",
    )(pos, *cols, *rows)
    lows = col_gather(low, BLK)

    def cube_call(pos, *refs):
        cube_kernel(len(lows), pos, *refs)

    out = pl.pallas_call(
        cube_call,
        out_shape=jax.ShapeDtypeStruct((BLK, BS), BF),
        in_specs=[SM, VM, VM, HB] + [HB] * len(lows),
        out_specs=VM,
        scratch_shapes=[A_SCRATCH, pltpu.VMEM(B_SHAPE, BF)]
        + [pltpu.VMEM(a.shape, BF) for a in lows]
        + [pltpu.SemaphoreType.DMA((1 + len(lows),))],
        compiler_params=PARAMS,
        name="cube",
    )(pos, metas, square, b, *lows)
    return out.reshape(density.shape)


def solution(mesh):
    return jax.shard_map(
        local,
        mesh=mesh,
        in_specs=(P("row", "col", None, None), P("row", "col"), P("row", "col")),
        out_specs=P("row", "col", None, None),
        check_vma=False,
    )
```

time: 205 us -> 185 us (0.902)
  the two profiles are of different devices: /device:TPU:8 before, /device:TPU:48 now
where the time goes in v2:
time: 185 us; the launch traced here: 184 us
  starting transfers between devices  111 us (60%)
  waiting for transfers between devices  49.6 us (27%)
  Pallas kernels  18.1 us (10%)
  local copies, waits for them, and re-layouts  2.67 us (1%)
  other arithmetic  1.95 us (1%)
    ppermute x13, starting transfers between devices, row(): return lax.ppermute(a, 'row', perm)  40.5 us
    ppermute x11, starting transfers between devices, col(): return lax.ppermute(a, 'col', perm)  37 us
    ppermute x13, waiting for transfers between devices, row(): return lax.ppermute(a, 'row', perm)  21.3 us
    ppermute x11, waiting for transfers between devices, col(): return lax.ppermute(a, 'col', perm)  13.7 us
    ppermute x3, starting transfers between devices, col_gather(): near = [lax.ppermute(own, 'col', yl_shift(s)) for s in (1, 3, 2)]  9.76 us
    pallas_call x1, Pallas kernels, local(): pl.pallas_call(square_call, out_shape=[jax.ShapeDtypeStruct((BLK, BS), F3...  9.18 us
    pallas_call x1, Pallas kernels, local(): pl.pallas_call(cube_call, out_shape=jax.ShapeDtypeStruct((BLK, BS), BF),...  8.6 us
    ppermute x3, waiting for transfers between devices, col_gather(): near = [lax.ppermute(own, 'col', yl_shift(s)) for s in (1, 3, 2)]  6.42 us
  transfers between devices with their start and end apart: 35, of which 15 were waited for; matrix products, arithmetic and copies ran while one was open for 1% of the time, Pallas kernels for 0%

profile of v2, /device:TPU:48, one launch (start us, length us, event | category | flops | bytes accessed | tf_op | source)
XLA Modules:
  0.0 184.1 jit_solution(9032289434805121578)
XLA Ops:
  2.1 3.8 %collective-permute-start = (bf16[784,128]{1,0:T(8,128)(2,1)S(1)}, bf16[784,128]{1,0:T(8,128)(2,1)S(1)}, u32[]{:S(2)}, u32[]{:S(2)}) collective-permute-start(bf16[784,128]{1,0:T(8,128)(2,1)S(1)} %maximum_maximum_fusion.refs_0_), channel_id=1, source_target_pairs={{0,32},{16,48},{32,0},{48,16},{64,96},{80,112},{96,64},{112,80},{1... | collective-permute-start | bytes 602120 | tf_op jit(solution)/shard_map/ppermute | solution.py:76
  7.9 3.5 %collective-permute-start.3 = (bf16[784,128]{1,0:T(8,128)(2,1)S(1)}, bf16[784,128]{1,0:T(8,128)(2,1)S(1)}, u32[]{:S(2)}, u32[]{:S(2)}) collective-permute-start(bf16[784,128]{1,0:T(8,128)(2,1)S(1)} %maximum_maximum_fusion.refs_0_), channel_id=1, source_target_pairs={{0,1},{1,2},{2,3},{3,0},{4,5},{5,6},{6,7},{7,4},{8,9},{9,10},{10,1... | collective-permute-start | bytes 602120 | tf_op jit(solution)/shard_map/ppermute | solution.py:79
  11.4 6.3 %collective-permute-done.refs_0_ = bf16[784,128]{1,0:T(8,128)(2,1)S(1)} collective-permute-done((bf16[784,128]{1,0:T(8,128)(2,1)S(1)}, bf16[784,128]{1,0:T(8,128)(2,1)S(1)}, u32[]{:S(2)}, u32[]{:S(2)}) %collective-permute-start) | collective-permute-done | bytes 200736 | tf_op jit(solution)/shard_map/ppermute | solution.py:76
  19.7 6.2 %collective-permute-start.10 = (bf16[1568,128]{1,0:T(8,128)(2,1)S(1)}, bf16[1568,128]{1,0:T(8,128)(2,1)S(1)}, u32[]{:S(2)}, u32[]{:S(2)}) collective-permute-start(bf16[1568,128]{1,0:T(8,128)(2,1)S(1)} %cat.7.refs_10_), channel_id=1, source_target_pairs={{0,64},{16,464},{32,96},{48,496},{64,128},{80,16},{96,160},{112,48... | collective-permute-start | bytes 1204232 | tf_op jit(solution)/shard_map/ppermute | solution.py:76
  26.0 4.3 %collective-permute-start.6 = (bf16[1568,128]{1,0:T(8,128)(2,1)S(1)}, bf16[1568,128]{1,0:T(8,128)(2,1)S(1)}, u32[]{:S(2)}, u32[]{:S(2)}) collective-permute-start(bf16[1568,128]{1,0:T(8,128)(2,1)S(1)} %cat.6.refs_11_), channel_id=1, source_target_pairs={{0,64},{16,464},{32,96},{48,496},{64,128},{80,16},{96,160},{112,48... | collective-permute-start | bytes 1204232 | tf_op jit(solution)/shard_map/ppermute | solution.py:76
  30.3 4.1 %collective-permute-start.9 = (bf16[784,128]{1,0:T(8,128)(2,1)S(1)}, bf16[784,128]{1,0:T(8,128)(2,1)S(1)}, u32[]{:S(2)}, u32[]{:S(2)}) collective-permute-start(bf16[784,128]{1,0:T(8,128)(2,1)S(1)} %maximum_maximum_fusion.refs_0_), channel_id=1, source_target_pairs={{0,2},{1,3},{2,0},{3,1},{4,6},{5,7},{6,4},{7,5},{8,10},{9,11},{10,... | collective-permute-start | bytes 602120 | tf_op jit(solution)/shard_map/ppermute | solution.py:79
  34.4 4.0 %collective-permute-done.10.refs_0_ = bf16[1568,128]{1,0:T(8,128)(2,1)S(1)} collective-permute-done((bf16[1568,128]{1,0:T(8,128)(2,1)S(1)}, bf16[1568,128]{1,0:T(8,128)(2,1)S(1)}, u32[]{:S(2)}, u32[]{:S(2)}) %collective-permute-start.10) | collective-permute-done | bytes 401440 | tf_op jit(solution)/shard_map/ppermute | solution.py:76
  40.3 4.7 %collective-permute-start.5 = (bf16[1568,128]{1,0:T(8,128)(2,1)S(1)}, bf16[1568,128]{1,0:T(8,128)(2,1)S(1)}, u32[]{:S(2)}, u32[]{:S(2)}) collective-permute-start(bf16[1568,128]{1,0:T(8,128)(2,1)S(1)} %cat.8.refs_0_), channel_id=1, source_target_pairs={{0,12},{1,13},{2,14},{3,15},{4,0},{5,1},{6,2},{7,3},{8,4},{9,5},{1... | collective-permute-start | bytes 1204232 | tf_op jit(solution)/shard_map/ppermute | solution.py:79
  46.9 3.9 %collective-permute-start.7 = (bf16[1568,128]{1,0:T(8,128)(2,1)S(1)}, bf16[1568,128]{1,0:T(8,128)(2,1)S(1)}, u32[]{:S(2)}, u32[]{:S(2)}) collective-permute-start(bf16[1568,128]{1,0:T(8,128)(2,1)S(1)} %collective-permute-done.6.refs_0_), channel_id=1, source_target_pairs={{0,64},{16,464},{32,96},{48,496},{64,128},{80,16},{96,160},{112,48... | collective-permute-start | bytes 1204232 | tf_op jit(solution)/shard_map/ppermute | solution.py:76
  52.8 7.0 %collective-permute-done.8.refs_0_ = bf16[784,128]{1,0:T(8,128)(2,1)S(1)} collective-permute-done((bf16[784,128]{1,0:T(8,128)(2,1)S(1)}, bf16[784,128]{1,0:T(8,128)(2,1)S(1)}, u32[]{:S(2)}, u32[]{:S(2)}) %collective-permute-start.8) | collective-permute-done | bytes 200736 | tf_op jit(solution)/shard_map/ppermute | solution.py:79
  59.9 3.7 %collective-permute-start.15 = (bf16[1568,128]{1,0:T(8,128)(2,1)S(1)}, bf16[1568,128]{1,0:T(8,128)(2,1)S(1)}, u32[]{:S(2)}, u32[]{:S(2)}) collective-permute-start(bf16[1568,128]{1,0:T(8,128)(2,1)S(1)} %collective-permute-done.11.refs_1_), channel_id=1, source_target_pairs={{0,64},{16,464},{32,96},{48,496},{64,128},{80,16},{96,160},{112,48... | collective-permute-start | bytes 1204232 | tf_op jit(solution)/shard_map/ppermute | solution.py:76
  63.5 4.8 %collective-permute-start.13 = (bf16[1568,128]{1,0:T(8,128)(2,1)S(1)}, bf16[1568,128]{1,0:T(8,128)(2,1)S(1)}, u32[]{:S(2)}, u32[]{:S(2)}) collective-permute-start(bf16[1568,128]{1,0:T(8,128)(2,1)S(1)} %cat.9.refs_3_), channel_id=1, source_target_pairs={{0,12},{1,13},{2,14},{3,15},{4,0},{5,1},{6,2},{7,3},{8,4},{9,5},{1... | collective-permute-start | bytes 1204232 | tf_op jit(solution)/shard_map/ppermute | solution.py:79
  72.4 4.6 %collective-permute-start.14 = (bf16[784,128]{1,0:T(8,128)(2,1)S(1)}, bf16[784,128]{1,0:T(8,128)(2,1)S(1)}, u32[]{:S(2)}, u32[]{:S(2)}) collective-permute-start(bf16[784,128]{1,0:T(8,128)(2,1)S(1)} %collective-permute-done.refs_0_), channel_id=1, source_target_pairs={{0,256},{16,272},{32,288},{48,304},{64,320},{80,336},{96,352},{112... | collective-permute-start | bytes 602120 | tf_op jit(solution)/shard_map/ppermute | solution.py:76
  79.1 9.1 %collective-permute-done.14.refs_2_ = bf16[784,128]{1,0:T(8,128)(2,1)S(1)} collective-permute-done((bf16[784,128]{1,0:T(8,128)(2,1)S(1)}, bf16[784,128]{1,0:T(8,128)(2,1)S(1)}, u32[]{:S(2)}, u32[]{:S(2)}) %collective-permute-start.14) | collective-permute-done | bytes 200736 | tf_op jit(solution)/shard_map/ppermute | solution.py:76
  94.6 5.1 %collective-permute-start.17 = (bf16[784,128]{1,0:T(8,128)(2,1)S(1)}, bf16[784,128]{1,0:T(8,128)(2,1)S(1)}, u32[]{:S(2)}, u32[]{:S(2)}) collective-permute-start(bf16[784,128]{1,0:T(8,128)(2,1)S(1)} %slice.28), channel_id=1, source_target_pairs={{0,12},{1,13},{2,14},{3,15},{4,0},{5,1},{6,2},{7,3},{8,4},{9,5},{1... | collective-permute-start | bytes 602120 | tf_op jit(solution)/shard_map/ppermute | solution.py:79
  101.7 5.1 %collective-permute-start.19 = (bf16[784,128]{1,0:T(8,128)(2,1)S(1)}, bf16[784,128]{1,0:T(8,128)(2,1)}, u32[]{:S(2)}, u32[]{:S(2)}) collective-permute-start(bf16[784,128]{1,0:T(8,128)(2,1)S(1)} %slice.30), channel_id=1, source_target_pairs={{0,12},{1,13},{2,14},{3,15},{4,0},{5,1},{6,2},{7,3},{8,4},{9,5},{1... | collective-permute-start | bytes 602120 | tf_op jit(solution)/shard_map/ppermute | solution.py:79
  110.8 5.5 %collective-permute-done.18.refs_8_ = bf16[784,128]{1,0:T(8,128)(2,1)} collective-permute-done((bf16[784,128]{1,0:T(8,128)(2,1)S(1)}, bf16[784,128]{1,0:T(8,128)(2,1)}, u32[]{:S(2)}, u32[]{:S(2)}) %collective-permute-start.18) | collective-permute-done | bytes 200736 | tf_op jit(solution)/shard_map/ppermute | solution.py:79
  116.3 9.2 %square.1 = (f32[768,128]{1,0:T(8,128)}, bf16[768,128]{1,0:T(8,128)(2,1)}, bf16[8192,512]{1,0:T(8,128)(2,1)}, bf16[256,128]{1,0:T(8,128)(2,1)}) custom-call(s32[5]{0:T(128)} %stack.23.pos, bf16[1568,128]{1,0:T(8,128)(2,1)} %copy-done.3, bf16[1568,128]{1,0:T(8,128)(2,1)} %copy-done.7, bf16[1568,128]{1,0:T(8,128)(2,1)} %copy-done.6, ...), custom_call_target="tpu_custom_call" | custom-call | tf_op jit(solution)/shard_map/square/pallas_call | solution.py:285
  131.0 4.2 %collective-permute-start.27 = (bf16[768,128]{1,0:T(8,128)(2,1)}, bf16[768,128]{1,0:T(8,128)(2,1)S(1)}, u32[]{:S(2)}, u32[]{:S(2)}) collective-permute-start(bf16[768,128]{1,0:T(8,128)(2,1)} %get-tuple-element.46), channel_id=1, source_target_pairs={{0,3},{1,0},{2,1},{3,2},{4,7},{5,4},{6,5},{7,6},{8,11},{9,8},{10,9... | collective-permute-start | bytes 589832 | tf_op jit(solution)/shard_map/ppermute | solution.py:123
  136.2 6.4 %collective-permute-done.24 = bf16[768,128]{1,0:T(8,128)(2,1)S(1)} collective-permute-done((bf16[768,128]{1,0:T(8,128)(2,1)}, bf16[768,128]{1,0:T(8,128)(2,1)S(1)}, u32[]{:S(2)}, u32[]{:S(2)}) %collective-permute-start.24) | collective-permute-done | bytes 196640 | tf_op jit(solution)/shard_map/ppermute | solution.py:123
  144.6 3.9 %collective-permute-start.25 = (bf16[1536,128]{1,0:T(8,128)(2,1)S(1)}, bf16[1536,128]{1,0:T(8,128)(2,1)S(1)}, u32[]{:S(2)}, u32[]{:S(2)}) collective-permute-start(bf16[1536,128]{1,0:T(8,128)(2,1)S(1)} %constant_dynamic-update-slice_fusion.refs_3_), channel_id=1, source_target_pairs={{0,4},{1,5},{2,6},{3,7},{4,8},{5,9},{6,10},{7,11},{8,12},{9,13},{1... | collective-permute-start | bytes 1179656 | tf_op jit(solution)/shard_map/ppermute | solution.py:125
  154.6 4.2 %collective-permute-start.32 = (bf16[768,128]{1,0:T(8,128)(2,1)S(1)}, bf16[768,128]{1,0:T(8,128)(2,1)S(1)}, u32[]{:S(2)}, u32[]{:S(2)}) collective-permute-start(bf16[768,128]{1,0:T(8,128)(2,1)S(1)} %slice.38), channel_id=1, source_target_pairs={{0,12},{1,13},{2,14},{3,15},{4,0},{5,1},{6,2},{7,3},{8,4},{9,5},{1... | collective-permute-start | bytes 589832 | tf_op jit(solution)/shard_map/ppermute | solution.py:131
  170.4 4.4 %collective-permute-done.33.refs_11_ = bf16[768,128]{1,0:T(8,128)(2,1)S(1)} collective-permute-done((bf16[768,128]{1,0:T(8,128)(2,1)S(1)}, bf16[768,128]{1,0:T(8,128)(2,1)S(1)}, u32[]{:S(2)}, u32[]{:S(2)}) %collective-permute-start.33) | collective-permute-done | bytes 196640 | tf_op jit(solution)/shard_map/ppermute | solution.py:132
  175.5 8.6 %cube.1 = bf16[768,128]{1,0:T(8,128)(2,1)} custom-call(s32[5]{0:T(128)} %stack.23.pos, bf16[256,128]{1,0:T(8,128)(2,1)} %get-tuple-element.43.refs_0_, f32[768,128]{1,0:T(8,128)} %get-tuple-element.44.refs_1_, bf16[8192,512]{1,0:T(8,128)(2,1)} %get-tuple-element.45.refs_2_, bf16[1536,128]{1,0:T(8,128)(2,1)} %copy-done.15, bf16[1536,128]{1,0:T(8,128)(2,1)} %copy-done.11, ...), custom_call_target="tpu_custom_call" | custom-call | tf_op jit(solution)/shard_map/cube/pallas_call | solution.py:306
  (116 shorter events, 56.6 us)
Async XLA Ops:
  2.1 15.6 %collective-permute-start = (bf16[784,128]{1,0:T(8,128)(2,1)S(1)}, bf16[784,128]{1,0:T(8,128)(2,1)S(1)}, u32[]{:S(2)}, u32[]{:S(2)}) collective-permute-start(bf16[784,128]{1,0:T(8,128)(2,1)S(1)} %maximum_maximum_fusion.refs_0_), channel_id=1, source_target_pairs={{0,32},{16,48},{32,0},{48,16},{64,96},{80,112},{96,64},{112,80},{1... | collective-permute-start | bytes 602120 | tf_op jit(solution)/shard_map/ppermute | solution.py:76
  7.9 18.0 %collective-permute-start.3 = (bf16[784,128]{1,0:T(8,128)(2,1)S(1)}, bf16[784,128]{1,0:T(8,128)(2,1)S(1)}, u32[]{:S(2)}, u32[]{:S(2)}) collective-permute-start(bf16[784,128]{1,0:T(8,128)(2,1)S(1)} %maximum_maximum_fusion.refs_0_), channel_id=1, source_target_pairs={{0,1},{1,2},{2,3},{3,0},{4,5},{5,6},{6,7},{7,4},{8,9},{9,10},{10,1... | collective-permute-start | bytes 602120 | tf_op jit(solution)/shard_map/ppermute | solution.py:79
  19.7 18.7 %collective-permute-start.10 = (bf16[1568,128]{1,0:T(8,128)(2,1)S(1)}, bf16[1568,128]{1,0:T(8,128)(2,1)S(1)}, u32[]{:S(2)}, u32[]{:S(2)}) collective-permute-start(bf16[1568,128]{1,0:T(8,128)(2,1)S(1)} %cat.7.refs_10_), channel_id=1, source_target_pairs={{0,64},{16,464},{32,96},{48,496},{64,128},{80,16},{96,160},{112,48... | collective-permute-start | bytes 1204232 | tf_op jit(solution)/shard_map/ppermute | solution.py:76
  26.0 20.9 %collective-permute-start.6 = (bf16[1568,128]{1,0:T(8,128)(2,1)S(1)}, bf16[1568,128]{1,0:T(8,128)(2,1)S(1)}, u32[]{:S(2)}, u32[]{:S(2)}) collective-permute-start(bf16[1568,128]{1,0:T(8,128)(2,1)S(1)} %cat.6.refs_11_), channel_id=1, source_target_pairs={{0,64},{16,464},{32,96},{48,496},{64,128},{80,16},{96,160},{112,48... | collective-permute-start | bytes 1204232 | tf_op jit(solution)/shard_map/ppermute | solution.py:76
  30.3 20.5 %collective-permute-start.9 = (bf16[784,128]{1,0:T(8,128)(2,1)S(1)}, bf16[784,128]{1,0:T(8,128)(2,1)S(1)}, u32[]{:S(2)}, u32[]{:S(2)}) collective-permute-start(bf16[784,128]{1,0:T(8,128)(2,1)S(1)} %maximum_maximum_fusion.refs_0_), channel_id=1, source_target_pairs={{0,2},{1,3},{2,0},{3,1},{4,6},{5,7},{6,4},{7,5},{8,10},{9,11},{10,... | collective-permute-start | bytes 602120 | tf_op jit(solution)/shard_map/ppermute | solution.py:79
  38.4 21.4 %collective-permute-start.11 = (bf16[1568,128]{1,0:T(8,128)(2,1)S(1)}, bf16[1568,128]{1,0:T(8,128)(2,1)S(1)}, u32[]{:S(2)}, u32[]{:S(2)}) collective-permute-start(bf16[1568,128]{1,0:T(8,128)(2,1)S(1)} %collective-permute-done.10.refs_0_), channel_id=1, source_target_pairs={{0,64},{16,464},{32,96},{48,496},{64,128},{80,16},{96,160},{112,48... | collective-permute-start | bytes 1204232 | tf_op jit(solution)/shard_map/ppermute | solution.py:76
  40.3 28.0 %collective-permute-start.5 = (bf16[1568,128]{1,0:T(8,128)(2,1)S(1)}, bf16[1568,128]{1,0:T(8,128)(2,1)S(1)}, u32[]{:S(2)}, u32[]{:S(2)}) collective-permute-start(bf16[1568,128]{1,0:T(8,128)(2,1)S(1)} %cat.8.refs_0_), channel_id=1, source_target_pairs={{0,12},{1,13},{2,14},{3,15},{4,0},{5,1},{6,2},{7,3},{8,4},{9,5},{1... | collective-permute-start | bytes 1204232 | tf_op jit(solution)/shard_map/ppermute | solution.py:79
  45.0 25.3 %collective-permute-start.4 = (bf16[1568,128]{1,0:T(8,128)(2,1)S(1)}, bf16[1568,128]{1,0:T(8,128)(2,1)S(1)}, u32[]{:S(2)}, u32[]{:S(2)}) collective-permute-start(bf16[1568,128]{1,0:T(8,128)(2,1)S(1)} %cat.8.refs_0_), channel_id=1, source_target_pairs={{0,4},{1,5},{2,6},{3,7},{4,8},{5,9},{6,10},{7,11},{8,12},{9,13},{1... | collective-permute-start | bytes 1204232 | tf_op jit(solution)/shard_map/ppermute | solution.py:79
  46.9 23.4 %collective-permute-start.7 = (bf16[1568,128]{1,0:T(8,128)(2,1)S(1)}, bf16[1568,128]{1,0:T(8,128)(2,1)S(1)}, u32[]{:S(2)}, u32[]{:S(2)}) collective-permute-start(bf16[1568,128]{1,0:T(8,128)(2,1)S(1)} %collective-permute-done.6.refs_0_), channel_id=1, source_target_pairs={{0,64},{16,464},{32,96},{48,496},{64,128},{80,16},{96,160},{112,48... | collective-permute-start | bytes 1204232 | tf_op jit(solution)/shard_map/ppermute | solution.py:76
  59.9 17.2 %collective-permute-start.15 = (bf16[1568,128]{1,0:T(8,128)(2,1)S(1)}, bf16[1568,128]{1,0:T(8,128)(2,1)S(1)}, u32[]{:S(2)}, u32[]{:S(2)}) collective-permute-start(bf16[1568,128]{1,0:T(8,128)(2,1)S(1)} %collective-permute-done.11.refs_1_), channel_id=1, source_target_pairs={{0,64},{16,464},{32,96},{48,496},{64,128},{80,16},{96,160},{112,48... | collective-permute-start | bytes 1204232 | tf_op jit(solution)/shard_map/ppermute | solution.py:76
  63.5 24.7 %collective-permute-start.13 = (bf16[1568,128]{1,0:T(8,128)(2,1)S(1)}, bf16[1568,128]{1,0:T(8,128)(2,1)S(1)}, u32[]{:S(2)}, u32[]{:S(2)}) collective-permute-start(bf16[1568,128]{1,0:T(8,128)(2,1)S(1)} %cat.9.refs_3_), channel_id=1, source_target_pairs={{0,12},{1,13},{2,14},{3,15},{4,0},{5,1},{6,2},{7,3},{8,4},{9,5},{1... | collective-permute-start | bytes 1204232 | tf_op jit(solution)/shard_map/ppermute | solution.py:79
  68.4 19.8 %collective-permute-start.12 = (bf16[1568,128]{1,0:T(8,128)(2,1)S(1)}, bf16[1568,128]{1,0:T(8,128)(2,1)S(1)}, u32[]{:S(2)}, u32[]{:S(2)}) collective-permute-start(bf16[1568,128]{1,0:T(8,128)(2,1)S(1)} %cat.9.refs_3_), channel_id=1, source_target_pairs={{0,4},{1,5},{2,6},{3,7},{4,8},{5,9},{6,10},{7,11},{8,12},{9,13},{1... | collective-permute-start | bytes 1204232 | tf_op jit(solution)/shard_map/ppermute | solution.py:79
  70.4 19.6 %collective-permute-start.22 = (bf16[1568,128]{1,0:T(8,128)(2,1)S(1)}, bf16[1568,128]{1,0:T(8,128)(2,1)S(1)}, u32[]{:S(2)}, u32[]{:S(2)}) collective-permute-start(bf16[1568,128]{1,0:T(8,128)(2,1)S(1)} %collective-permute-done.7.refs_1_), channel_id=1, source_target_pairs={{0,64},{16,464},{32,96},{48,496},{64,128},{80,16},{96,160},{112,48... | collective-permute-start | bytes 1204232 | tf_op jit(solution)/shard_map/ppermute | solution.py:76
  72.4 15.8 %collective-permute-start.14 = (bf16[784,128]{1,0:T(8,128)(2,1)S(1)}, bf16[784,128]{1,0:T(8,128)(2,1)S(1)}, u32[]{:S(2)}, u32[]{:S(2)}) collective-permute-start(bf16[784,128]{1,0:T(8,128)(2,1)S(1)} %collective-permute-done.refs_0_), channel_id=1, source_target_pairs={{0,256},{16,272},{32,288},{48,304},{64,320},{80,336},{96,352},{112... | collective-permute-start | bytes 602120 | tf_op jit(solution)/shard_map/ppermute | solution.py:76
  77.1 15.0 %collective-permute-start.20 = (bf16[784,128]{1,0:T(8,128)(2,1)S(1)}, bf16[784,128]{1,0:T(8,128)(2,1)S(1)}, u32[]{:S(2)}, u32[]{:S(2)}) collective-permute-start(bf16[784,128]{1,0:T(8,128)(2,1)S(1)} %slice.36), channel_id=1, source_target_pairs={{0,64},{16,464},{32,96},{48,496},{64,128},{80,16},{96,160},{112,48... | collective-permute-start | bytes 602120 | tf_op jit(solution)/shard_map/ppermute | solution.py:76
  90.0 26.2 %collective-permute-start.23 = (bf16[5488,128]{1,0:T(8,128)(2,1)S(1)}, bf16[5488,128]{1,0:T(8,128)(2,1)}, u32[]{:S(2)}, u32[]{:S(2)}) collective-permute-start(bf16[5488,128]{1,0:T(8,128)(2,1)S(1)} %cat.11.refs_14_), channel_id=1, source_target_pairs={{0,16},{16,0},{32,48},{48,32},{64,80},{80,64},{96,112},{112,96},{1... | collective-permute-start | bytes 4214792 | tf_op jit(solution)/shard_map/ppermute | solution.py:76
  92.2 24.1 %collective-permute-start.21 = (bf16[5488,128]{1,0:T(8,128)(2,1)S(1)}, bf16[5488,128]{1,0:T(8,128)(2,1)}, u32[]{:S(2)}, u32[]{:S(2)}) collective-permute-start(bf16[5488,128]{1,0:T(8,128)(2,1)S(1)} %cat.10.refs_12_), channel_id=1, source_target_pairs={{0,16},{16,0},{32,48},{48,32},{64,80},{80,64},{96,112},{112,96},{1... | collective-permute-start | bytes 4214792 | tf_op jit(solution)/shard_map/ppermute | solution.py:76
  125.4 17.1 %collective-permute-start.24 = (bf16[768,128]{1,0:T(8,128)(2,1)}, bf16[768,128]{1,0:T(8,128)(2,1)S(1)}, u32[]{:S(2)}, u32[]{:S(2)}) collective-permute-start(bf16[768,128]{1,0:T(8,128)(2,1)} %get-tuple-element.46), channel_id=1, source_target_pairs={{0,1},{1,2},{2,3},{3,0},{4,5},{5,6},{6,7},{7,4},{8,9},{9,10},{10,1... | collective-permute-start | bytes 589832 | tf_op jit(solution)/shard_map/ppermute | solution.py:123
  127.9 20.7 %collective-permute-start.28 = (bf16[768,128]{1,0:T(8,128)(2,1)}, bf16[768,128]{1,0:T(8,128)(2,1)S(1)}, u32[]{:S(2)}, u32[]{:S(2)}) collective-permute-start(bf16[768,128]{1,0:T(8,128)(2,1)} %get-tuple-element.46), channel_id=1, source_target_pairs={{0,2},{1,3},{2,0},{3,1},{4,6},{5,7},{6,4},{7,5},{8,10},{9,11},{10,... | collective-permute-start | bytes 589832 | tf_op jit(solution)/shard_map/ppermute | solution.py:123
  131.0 17.5 %collective-permute-start.27 = (bf16[768,128]{1,0:T(8,128)(2,1)}, bf16[768,128]{1,0:T(8,128)(2,1)S(1)}, u32[]{:S(2)}, u32[]{:S(2)}) collective-permute-start(bf16[768,128]{1,0:T(8,128)(2,1)} %get-tuple-element.46), channel_id=1, source_target_pairs={{0,3},{1,0},{2,1},{3,2},{4,7},{5,4},{6,5},{7,6},{8,11},{9,8},{10,9... | collective-permute-start | bytes 589832 | tf_op jit(solution)/shard_map/ppermute | solution.py:123
  144.6 14.3 %collective-permute-start.25 = (bf16[1536,128]{1,0:T(8,128)(2,1)S(1)}, bf16[1536,128]{1,0:T(8,128)(2,1)S(1)}, u32[]{:S(2)}, u32[]{:S(2)}) collective-permute-start(bf16[1536,128]{1,0:T(8,128)(2,1)S(1)} %constant_dynamic-update-slice_fusion.refs_3_), channel_id=1, source_target_pairs={{0,4},{1,5},{2,6},{3,7},{4,8},{5,9},{6,10},{7,11},{8,12},{9,13},{1... | collective-permute-start | bytes 1179656 | tf_op jit(solution)/shard_map/ppermute | solution.py:125
  148.6 14.3 %collective-permute-start.30 = (bf16[1536,128]{1,0:T(8,128)(2,1)S(1)}, bf16[1536,128]{1,0:T(8,128)(2,1)S(1)}, u32[]{:S(2)}, u32[]{:S(2)}) collective-permute-start(bf16[1536,128]{1,0:T(8,128)(2,1)S(1)} %constant_dynamic-update-slice_fusion.2.refs_6_), channel_id=1, source_target_pairs={{0,12},{1,13},{2,14},{3,15},{4,0},{5,1},{6,2},{7,3},{8,4},{9,5},{1... | collective-permute-start | bytes 1179656 | tf_op jit(solution)/shard_map/ppermute | solution.py:129
  151.7 14.3 %collective-permute-start.29 = (bf16[1536,128]{1,0:T(8,128)(2,1)S(1)}, bf16[1536,128]{1,0:T(8,128)(2,1)S(1)}, u32[]{:S(2)}, u32[]{:S(2)}) collective-permute-start(bf16[1536,128]{1,0:T(8,128)(2,1)S(1)} %constant_dynamic-update-slice_fusion.2.refs_6_), channel_id=1, source_target_pairs={{0,4},{1,5},{2,6},{3,7},{4,8},{5,9},{6,10},{7,11},{8,12},{9,13},{1... | collective-permute-start | bytes 1179656 | tf_op jit(solution)/shard_map/ppermute | solution.py:128
  154.6 14.2 %collective-permute-start.32 = (bf16[768,128]{1,0:T(8,128)(2,1)S(1)}, bf16[768,128]{1,0:T(8,128)(2,1)S(1)}, u32[]{:S(2)}, u32[]{:S(2)}) collective-permute-start(bf16[768,128]{1,0:T(8,128)(2,1)S(1)} %slice.38), channel_id=1, source_target_pairs={{0,12},{1,13},{2,14},{3,15},{4,0},{5,1},{6,2},{7,3},{8,4},{9,5},{1... | collective-permute-start | bytes 589832 | tf_op jit(solution)/shard_map/ppermute | solution.py:131
  (32 other events, 503.6 us)

commit v3 on v0

v3 whole, which is shorter than its diff:
```python
import jax
import jax.numpy as jnp
from jax import lax
from jax.experimental import pallas as pl
from jax.experimental.pallas import tpu as pltpu
from jax.sharding import PartitionSpec as P

BS = 128
KD = 3
CG = 4
ROWS = 2
NG = 16
NZ = 8
BLK = ROWS * KD * BS
PAY = BLK + 16
HALF = NG * ROWS * BS
BF = jnp.bfloat16
F32 = jnp.float32
VM = pl.BlockSpec(memory_space=pltpu.VMEM)
SM = pl.BlockSpec(memory_space=pltpu.SMEM)
HBM = pl.BlockSpec(memory_space=pltpu.HBM)

CORE_SWAP = [(r, r ^ 1) for r in range(32)]
YH_SWAP = [(r, r ^ 2) for r in range(32)]
Z_GROUPS = [[z * 4 + n for z in range(NZ)] for n in range(4)]


def yl_shift(s):
    return [(c, c // 4 * 4 + (c + s) % 4) for c in range(16)]


def x_shift(s):
    return [(c, (c + 4 * s) % 16) for c in range(16)]


def col(a, perm):
    return lax.ppermute(a, "col", perm)


def row(a, perm):
    return lax.ppermute(a, "row", perm)


def shape(*dims, dtype=BF):
    return jax.ShapeDtypeStruct(dims, dtype)


def params(mib):
    return pltpu.CompilerParams(vmem_limit_bytes=mib * 1024 * 1024)


def fence(token, *values):
    token, *values = lax.optimization_barrier((token, *values))

    def body(in_ref, out_ref):
        out_ref[...] = in_ref[...]

    token = pl.pallas_call(
        body,
        out_shape=shape(*token.shape, dtype=token.dtype),
        in_specs=[VM],
        out_specs=VM,
        compiler_params=params(1),
        cost_estimate=pl.CostEstimate(flops=4 * 10**9, bytes_accessed=0, transcendentals=0),
        name="fence",
    )(token)
    return lax.optimization_barrier((token, *values))


def cat(*arrays):
    rows = [a.shape[0] for a in arrays]

    def body(*refs):
        at = 0
        for n, ref in zip(rows, refs):
            refs[-1][at : at + n] = ref[...]
            at += n

    return pl.pallas_call(
        body,
        out_shape=shape(sum(rows), BS),
        in_specs=[VM] * len(arrays),
        out_specs=VM,
        compiler_params=params(2),
        name="cat",
    )(*arrays)


X_FAR = x_shift(2)

ALL_PIECES = [
    (g * 4 + a, n, dx, dy)
    for g, dys in enumerate(((0, 3), (1, 2)))
    for a, dx in enumerate((0, 3, 1, 2))
    for n, dy in enumerate(dys)
]
NEAR_PIECES = [
    (g * 3 + a, n, dx, dy)
    for g, dys in enumerate(((0, 3), (1, 2)))
    for a, dx in enumerate((0, 3, 1))
    for n, dy in enumerate(dys)
]
FAR_PIECES = [(0, 0, 2, 0), (1, 0, 2, 3), (2, 0, 2, 1), (3, 0, 2, 2)]


def gather(own):
    token = jnp.zeros((8, BS), F32)
    own_y = row(own, YH_SWAP)
    one = cat(own, col(own, yl_shift(1)))
    token, one, own = fence(token, one, own)
    ones = [col(one, p) for p in (x_shift(1), x_shift(3), X_FAR)]
    token, both, own = fence(token, cat(own, own_y), own)
    column = lax.all_gather(both, "row", axis_index_groups=Z_GROUPS, axis=0, tiled=True)
    token, two = fence(token, cat(col(own, yl_shift(3)), col(own, yl_shift(2))))
    twos = [col(two, p) for p in (x_shift(1), x_shift(3), X_FAR)]
    return [one, *ones, two, *twos], column, token


def col_gather(own, rows):
    line1, line3, line2 = [col(own, yl_shift(s)) for s in (1, 3, 2)]
    one = cat(own, line1)
    left1, right1 = col(one, x_shift(1)), col(one, x_shift(3))
    two = cat(line3, line2)
    left2, right2 = col(two, x_shift(1)), col(two, x_shift(3))
    far1, far2 = col(left1[:rows], x_shift(1)), col(right1[rows:], x_shift(3))
    far3, far4 = col(left2[:rows], x_shift(1)), col(right2[rows:], x_shift(3))
    return [one, left1, right1, two, left2, right2], [far1, far2, far3, far4]


def meta_rows(meta):
    wide = meta.astype(F32)
    return [
        jnp.broadcast_to(wide[s : s + 1], (16, BS)).astype(BF) for s in range(ROWS * KD)
    ]


def spread(src, base, slots, store):
    masks = [[m == jnp.full((16, BS), q, BF) for q in range(CG)] for m in slots]

    def step(n, _):
        r = pl.multiple_of(n * 16, 16)
        v = [src[pl.ds(base + t * BS + r, 16), :] for t in range(KD)]
        zero = jnp.zeros((16, BS), BF)
        for q in range(CG):
            d = zero
            for t in range(KD):
                d = jnp.where(masks[t][q], v[t], d)
            store(r, q, d)
        return 0

    lax.fori_loop(0, BS // 16, step, 0, unroll=True)


def group_of(pos, dx, dy):
    return ((pos[3] + dx) & 3) * 4 + ((pos[4] + dy) & 3)


def spread_row(pos, src, base, i, slots, group, a_ref):
    def store(r, q, d):
        half = (q >> 1) ^ pos[2]
        at = pl.multiple_of(half * HALF + group * (ROWS * BS) + (q & 1) * BS, BS)
        a_ref[pl.ds(i * BS + r, 16), pl.ds(at, BS)] = d

    spread(src, base + i * KD * BS, slots[i * KD : (i + 1) * KD], store)


def pick(acc, slots):
    out = []
    for i in range(ROWS):
        for t in range(KD):
            m = slots[i * KD + t].astype(F32)[0:1]
            d = jnp.zeros((BS, BS), F32)
            for q in range(CG):
                d = jnp.where(m == float(q), acc[i * BS : (i + 1) * BS, q * BS : (q + 1) * BS], d)
            out.append(d)
    return out


def strip_kernel(pos, token, *refs):
    cols, (a_out, meta_ref, a_ref, sems) = refs[:-4], refs[-4:]
    copies = []
    for i in range(ROWS):
        for a, n, dx, dy in ALL_PIECES:
            src, group = cols[a], group_of(pos, dx, dy)
            meta = src[n * PAY + BLK : (n + 1) * PAY]
            if i == 0:
                meta_ref[pl.ds(pl.multiple_of(group * 16, 16), 16), :] = meta
            spread_row(pos, src, n * PAY, i, meta_rows(meta), group, a_ref)
        here = pl.ds(i * BS, BS)
        copies.append(pltpu.make_async_copy(a_ref.at[here], a_out.at[here], sems.at[i]))
        copies[-1].start()
    for copy in copies:
        copy.wait()


def fetch(src, buffer, sems):
    copies = []
    for z in range(NZ):
        part = pl.ds(z * 2 * PAY, 2 * PAY)
        copies.append(pltpu.make_async_copy(src.at[part], buffer.at[part], sems.at[z]))
        copies[-1].start()
    return copies


def half_kernel(pos, v_ref, b_ref, buffer, sems):
    copies = fetch(v_ref, buffer, sems)
    for z in range(NZ):
        copies[z].wait()
        for n in range(2):
            base = (z * 2 + n) * PAY
            slots = meta_rows(buffer[base + BLK : base + PAY])
            top = pl.multiple_of((z * 2 + (pos[1] ^ n)) * (ROWS * BS), ROWS * BS)
            for i in range(ROWS):

                def store(r, q, d, top=top + i * BS):
                    b_ref[pl.ds(top + r, 16), q * BS : (q + 1) * BS] = d

                spread(buffer, base + i * KD * BS, slots[i * KD : (i + 1) * KD], store)


def own_half_kernel(pos, a_in, v_ref, acc_ref, b_ref, buffer, sems, a_ref, a_sem):
    copy = pltpu.make_async_copy(a_in.at[:, pl.ds(0, HALF)], a_ref, a_sem)
    copy.start()
    half_kernel(pos, v_ref, b_ref, buffer, sems)
    copy.wait()
    acc_ref[...] = jnp.dot(a_ref[...], b_ref[...], preferred_element_type=F32)


def square_kernel(pos, meta_ref, acc_ref, a_in, v_ref, square_ref, low_ref, b_ref, buffer, sems, a_ref, a_sem):
    copy = pltpu.make_async_copy(a_in.at[:, pl.ds(HALF, HALF)], a_ref, a_sem)
    copy.start()
    half_kernel(pos, v_ref, b_ref, buffer, sems)
    copy.wait()
    acc = acc_ref[...] + jnp.dot(a_ref[...], b_ref[...], preferred_element_type=F32)
    at = pl.multiple_of(group_of(pos, 0, 0) * 16, 16)
    for s, d in enumerate(pick(acc, meta_rows(meta_ref[pl.ds(at, 16), :]))):
        square_ref[s * BS : (s + 1) * BS] = d
        low_ref[s * BS : (s + 1) * BS] = d.astype(BF)


def near_kernel(pos, meta_ref, b_own, b_other, *refs):
    lows, acc_ref, a_ref = refs[:-2], refs[-2], refs[-1]
    for _, _, dx, dy in FAR_PIECES:
        for half in range(2):
            at = pl.multiple_of(half * HALF + group_of(pos, dx, dy) * (ROWS * BS), ROWS * BS)
            a_ref[:, pl.ds(at, ROWS * BS)] = jnp.zeros((ROWS * BS, ROWS * BS), BF)
    for a, n, dx, dy in NEAR_PIECES:
        group = group_of(pos, dx, dy)
        meta = meta_ref[pl.ds(pl.multiple_of(group * 16, 16), 16), :]
        for i in range(ROWS):
            spread_row(pos, lows[a], n * BLK, i, meta_rows(meta), group, a_ref)
    acc_ref[...] = jnp.dot(a_ref[:, :HALF], b_own[...], preferred_element_type=F32) + jnp.dot(
        a_ref[:, HALF:], b_other[...], preferred_element_type=F32
    )


def far_kernel(pos, meta_ref, b_own, b_other, acc_ref, square_ref, *refs):
    lows, (out_ref, a_ref, b_ref) = refs[:-3], refs[-3:]
    width = ROWS * BS
    for m, (a, n, dx, dy) in enumerate(FAR_PIECES):
        group = group_of(pos, dx, dy)
        at = pl.multiple_of(group * width, width)
        for half, b in enumerate((b_own, b_other)):
            b_ref[(2 * m + half) * width : (2 * m + half + 1) * width] = b[pl.ds(at, width), :]
        slots = meta_rows(meta_ref[pl.ds(pl.multiple_of(group * 16, 16), 16), :])
        for i in range(ROWS):

            def store(r, q, d, i=i, m=m):
                half = (q >> 1) ^ pos[2]
                at = pl.multiple_of((2 * m + half) * width + (q & 1) * BS, BS)
                a_ref[pl.ds(i * BS + r, 16), pl.ds(at, BS)] = d

            spread(lows[a], n * BLK + i * KD * BS, slots[i * KD : (i + 1) * KD], store)
    acc = acc_ref[...] + jnp.dot(a_ref[...], b_ref[...], preferred_element_type=F32)
    at = pl.multiple_of(group_of(pos, 0, 0) * 16, 16)
    for s, d in enumerate(pick(acc, meta_rows(meta_ref[pl.ds(at, 16), :]))):
        square = square_ref[s * BS : (s + 1) * BS]
        out_ref[s * BS : (s + 1) * BS] = (3.0 * square - 2.0 * d).astype(BF)


def local(density, block_cols, block_counts):
    slot = lax.broadcasted_iota(jnp.int32, (ROWS, KD), 1)
    where = jnp.where(slot < block_counts, block_cols % CG, -1).reshape(ROWS * KD, 1)
    meta = jnp.broadcast_to(where, (ROWS * KD, BS)).astype(BF)
    meta = jnp.pad(meta, ((0, 16 - ROWS * KD), (0, 0)))
    density = density.reshape(BLK, BS)
    own = cat(density, meta)
    r, c = lax.axis_index("row"), lax.axis_index("col")
    pos = jnp.stack([r // 4, r // 2 % 2, r % 2, c // 4, c % 4]).astype(jnp.int32)
    strips, column, token = gather(own)
    acc_shape = shape(ROWS * BS, CG * BS, dtype=F32)
    b_shape = shape(HALF, CG * BS)
    a, metas = pl.pallas_call(
        strip_kernel,
        out_shape=[shape(ROWS * BS, 2 * HALF), shape(NG * 16, BS)],
        in_specs=[SM, VM] + [VM] * len(strips),
        out_specs=[HBM, VM],
        scratch_shapes=[pltpu.VMEM((ROWS * BS, 2 * HALF), BF), pltpu.SemaphoreType.DMA((ROWS,))],
        compiler_params=params(58),
        name="strips",
    )(pos, token, *strips)
    v, a, metas = lax.optimization_barrier((column, a, metas))
    v_other = row(v, CORE_SWAP)
    block_scratch = [
        pltpu.VMEM((2 * NZ * PAY, BS), BF),
        pltpu.SemaphoreType.DMA((NZ,)),
        pltpu.VMEM((ROWS * BS, HALF), BF),
        pltpu.SemaphoreType.DMA(()),
    ]
    acc, b_own = pl.pallas_call(
        own_half_kernel,
        out_shape=[acc_shape, b_shape],
        in_specs=[SM, HBM, HBM],
        out_specs=[VM, VM],
        scratch_shapes=block_scratch,
        compiler_params=params(57),
        name="own_half",
    )(pos, a, v)
    square, low, b_other = pl.pallas_call(
        square_kernel,
        out_shape=[shape(BLK, BS, dtype=F32), shape(BLK, BS), b_shape],
        in_specs=[SM, VM, VM, HBM, pl.BlockSpec(memory_space=pl.ANY)],
        out_specs=[VM, VM, VM],
        scratch_shapes=block_scratch,
        compiler_params=params(16),
        name="square",
    )(pos, metas, acc, a, v_other)

    near, far = col_gather(low, BLK)
    acc = pl.pallas_call(
        near_kernel,
        out_shape=acc_shape,
        in_specs=[SM] + [VM] * 9,
        out_specs=VM,
        scratch_shapes=[pltpu.VMEM((ROWS * BS, 2 * HALF), BF)],
        compiler_params=params(16),
        name="near",
    )(pos, metas, b_own, b_other, *near)
    out = pl.pallas_call(
        far_kernel,
        out_shape=shape(BLK, BS),
        in_specs=[SM] + [VM] * (5 + len(far)),
        out_specs=VM,
        scratch_shapes=[pltpu.VMEM((ROWS * BS, 4 * CG * BS), BF), pltpu.VMEM((4 * CG * BS, CG * BS), BF)],
        compiler_params=params(16),
        name="far",
    )(pos, metas, b_own, b_other, acc, square, *far)
    return out.reshape(ROWS, KD, BS, BS)


def solution(mesh):
    return jax.shard_map(
        local,
        mesh=mesh,
        in_specs=(P("row", "col", None, None), P("row", "col"), P("row", "col")),
        out_specs=P("row", "col", None, None),
        check_vma=False,
    )
```

time: 347 us -> 160 us (0.46)
  the two profiles are of different devices: /device:TPU:128 before, /device:TPU:72 now
where the time goes in v3:
time: 160 us; the launch traced here: 159 us
  starting transfers between devices  77 us (48%)
  waiting for transfers between devices  41 us (26%)
  Pallas kernels  21.6 us (14%)
  between operations  13.9 us (9%)
  local copies, waits for them, and re-layouts  4.72 us (3%)
    ppermute x20, starting transfers between devices, col(): return lax.ppermute(a, 'col', perm)  68.9 us
    ppermute x20, waiting for transfers between devices, col(): return lax.ppermute(a, 'col', perm)  28 us
    ppermute x2, waiting for transfers between devices, row(): return lax.ppermute(a, 'row', perm)  12.9 us
    ppermute x2, starting transfers between devices, row(): return lax.ppermute(a, 'row', perm)  8.12 us
    pallas_call x1, Pallas kernels, local(): pl.pallas_call(own_half_kernel, out_shape=[acc_shape, b_shape], in_specs=...  5.56 us
    pallas_call x1, Pallas kernels, local(): pl.pallas_call(strip_kernel, out_shape=[shape(ROWS * BS, 2 * HALF), shape...  4.89 us
    pallas_call x1, Pallas kernels, local(): pl.pallas_call(square_kernel, out_shape=[shape(BLK, BS, dtype=F32), shape...  4.5 us
    unnamed x30, local copies, waits for them, and re-layouts  3.82 us
  transfers between devices with their start and end apart: 23, of which 11 were waited for; matrix products, arithmetic and copies ran while one was open for 0% of the time, Pallas kernels for 9%

profile of v3, /device:TPU:72, one launch (start us, length us, event | category | flops | bytes accessed | tf_op | source)
XLA Modules:
  0.0 159.0 jit_solution(1376905677379161232)
XLA Ops:
  8.4 3.5 %collective-permute-start = (bf16[784,128]{1,0:T(8,128)(2,1)S(1)}, bf16[784,128]{1,0:T(8,128)(2,1)S(1)}, u32[]{:S(2)}, u32[]{:S(2)}) collective-permute-start(bf16[784,128]{1,0:T(8,128)(2,1)S(1)} %cat.6.refs_0_), channel_id=1, source_target_pairs={{0,1},{1,2},{2,3},{3,0},{4,5},{5,6},{6,7},{7,4},{8,9},{9,10},{10,1... | collective-permute-start | bytes 602120 | tf_op jit(solution)/shard_map/ppermute | solution.py:37
  11.9 5.9 %collective-permute-start.1 = (bf16[784,128]{1,0:T(8,128)(2,1)S(1)}, bf16[784,128]{1,0:T(8,128)(2,1)S(1)}, u32[]{:S(2)}, u32[]{:S(2)}) collective-permute-start(bf16[784,128]{1,0:T(8,128)(2,1)S(1)} %cat.6.refs_0_), channel_id=1, source_target_pairs={{0,32},{16,48},{32,0},{48,16},{64,96},{80,112},{96,64},{112,80},{1... | collective-permute-start | bytes 602120 | tf_op jit(solution)/shard_map/ppermute | solution.py:41
  17.9 12.4 %collective-permute-done.1.refs_1_ = bf16[784,128]{1,0:T(8,128)(2,1)S(1)} collective-permute-done((bf16[784,128]{1,0:T(8,128)(2,1)S(1)}, bf16[784,128]{1,0:T(8,128)(2,1)S(1)}, u32[]{:S(2)}, u32[]{:S(2)}) %collective-permute-start.1) | collective-permute-done | bytes 200736 | tf_op jit(solution)/shard_map/ppermute | solution.py:41
  31.2 3.9 %collective-permute-start.3 = (bf16[784,128]{1,0:T(8,128)(2,1)S(1)}, bf16[784,128]{1,0:T(8,128)(2,1)S(1)}, u32[]{:S(2)}, u32[]{:S(2)}) collective-permute-start(bf16[784,128]{1,0:T(8,128)(2,1)S(1)} %cat.6.refs_0_), channel_id=1, source_target_pairs={{0,2},{1,3},{2,0},{3,1},{4,6},{5,7},{6,4},{7,5},{8,10},{9,11},{10,... | collective-permute-start | bytes 602120 | tf_op jit(solution)/shard_map/ppermute | solution.py:37
  37.0 4.9 %collective-permute-start.6 = (bf16[1568,128]{1,0:T(8,128)(2,1)S(1)}, bf16[1568,128]{1,0:T(8,128)(2,1)S(1)}, u32[]{:S(2)}, u32[]{:S(2)}) collective-permute-start(bf16[1568,128]{1,0:T(8,128)(2,1)S(1)} %cat.7.refs_0_), channel_id=1, source_target_pairs={{0,8},{1,9},{2,10},{3,11},{4,12},{5,13},{6,14},{7,15},{8,0},{9,1},... | collective-permute-start | bytes 1204232 | tf_op jit(solution)/shard_map/ppermute | solution.py:37
  41.9 3.0 %collective-permute-start.5 = (bf16[1568,128]{1,0:T(8,128)(2,1)S(1)}, bf16[1568,128]{1,0:T(8,128)(2,1)S(1)}, u32[]{:S(2)}, u32[]{:S(2)}) collective-permute-start(bf16[1568,128]{1,0:T(8,128)(2,1)S(1)} %cat.7.refs_0_), channel_id=1, source_target_pairs={{0,12},{1,13},{2,14},{3,15},{4,0},{5,1},{6,2},{7,3},{8,4},{9,5},{1... | collective-permute-start | bytes 1204232 | tf_op jit(solution)/shard_map/ppermute | solution.py:37
  45.0 2.8 %collective-permute-start.4 = (bf16[1568,128]{1,0:T(8,128)(2,1)S(1)}, bf16[1568,128]{1,0:T(8,128)(2,1)S(1)}, u32[]{:S(2)}, u32[]{:S(2)}) collective-permute-start(bf16[1568,128]{1,0:T(8,128)(2,1)S(1)} %cat.7.refs_0_), channel_id=1, source_target_pairs={{0,4},{1,5},{2,6},{3,7},{4,8},{5,9},{6,10},{7,11},{8,12},{9,13},{1... | collective-permute-start | bytes 1204232 | tf_op jit(solution)/shard_map/ppermute | solution.py:37
  48.5 4.3 %collective-permute-start.9 = (bf16[1568,128]{1,0:T(8,128)(2,1)S(1)}, bf16[1568,128]{1,0:T(8,128)(2,1)S(1)}, u32[]{:S(2)}, u32[]{:S(2)}) collective-permute-start(bf16[1568,128]{1,0:T(8,128)(2,1)S(1)} %cat.9.refs_4_), channel_id=1, source_target_pairs={{0,8},{1,9},{2,10},{3,11},{4,12},{5,13},{6,14},{7,15},{8,0},{9,1},... | collective-permute-start | bytes 1204232 | tf_op jit(solution)/shard_map/ppermute | solution.py:37
  52.8 3.0 %collective-permute-start.8 = (bf16[1568,128]{1,0:T(8,128)(2,1)S(1)}, bf16[1568,128]{1,0:T(8,128)(2,1)S(1)}, u32[]{:S(2)}, u32[]{:S(2)}) collective-permute-start(bf16[1568,128]{1,0:T(8,128)(2,1)S(1)} %cat.9.refs_4_), channel_id=1, source_target_pairs={{0,12},{1,13},{2,14},{3,15},{4,0},{5,1},{6,2},{7,3},{8,4},{9,5},{1... | collective-permute-start | bytes 1204232 | tf_op jit(solution)/shard_map/ppermute | solution.py:37
  61.4 7.4 %collective-permute-done.4.refs_1_ = bf16[1568,128]{1,0:T(8,128)(2,1)S(1)} collective-permute-done((bf16[1568,128]{1,0:T(8,128)(2,1)S(1)}, bf16[1568,128]{1,0:T(8,128)(2,1)S(1)}, u32[]{:S(2)}, u32[]{:S(2)}) %collective-permute-start.4) | collective-permute-done | bytes 401440 | tf_op jit(solution)/shard_map/ppermute | solution.py:37
  69.9 6.3 %collective-permute-done.8.refs_6_ = bf16[1568,128]{1,0:T(8,128)(2,1)S(1)} collective-permute-done((bf16[1568,128]{1,0:T(8,128)(2,1)S(1)}, bf16[1568,128]{1,0:T(8,128)(2,1)S(1)}, u32[]{:S(2)}, u32[]{:S(2)}) %collective-permute-start.8) | collective-permute-done | bytes 401440 | tf_op jit(solution)/shard_map/ppermute | solution.py:37
  77.7 4.9 %strips.1 = (bf16[256,8192]{1,0:T(8,128)(2,1)}, bf16[256,128]{1,0:T(8,128)(2,1)}) custom-call(s32[5]{0:T(128)} %stack.23.pos, f32[8,128]{1,0:T(8,128)} %copy-done.8, bf16[1568,128]{1,0:T(8,128)(2,1)} %copy-done.2, bf16[1568,128]{1,0:T(8,128)(2,1)} %copy-done.11, bf16[1568,128]{1,0:T(8,128)(2,1)} %copy-done.10, bf16[1568,128]{1,0:T(8,128)(2,1)} %copy-done.9, ...), custom_call_target="tpu_custom_call" | custom-call | tf_op jit(solution)/shard_map/strips/pallas_call | solution.py:293
  84.9 5.6 %own_half.1 = (f32[256,512]{1,0:T(8,128)}, bf16[4096,512]{1,0:T(8,128)(2,1)}) custom-call(s32[5]{0:T(128)} %stack.23.pos, bf16[256,8192]{1,0:T(8,128)(2,1)} %get-tuple-element.50.a_in, bf16[12544,128]{1,0:T(8,128)(2,1)} %all-gather.2.cloned.1.call-done.v_ref), custom_call_target="tpu_custom_call" | custom-call | tf_op jit(solution)/shard_map/own_half/pallas_call | solution.py:310
  92.0 4.5 %square.1 = (f32[768,128]{1,0:T(8,128)S(1)}, bf16[768,128]{1,0:T(8,128)(2,1)S(1)}, bf16[4096,512]{1,0:T(8,128)(2,1)S(1)}) custom-call(s32[5]{0:T(128)S(1)} %copy-done.7, bf16[256,128]{1,0:T(8,128)(2,1)S(1)} %copy-done.4, f32[256,512]{1,0:T(8,128)S(1)} %copy-done.5, bf16[256,8192]{1,0:T(8,128)(2,1)S(1)} %copy-done.1, ...), custom_call_target="tpu_custom_call" | custom-call | tf_op jit(solution)/shard_map/square/pallas_call | solution.py:319
  96.5 3.6 %collective-permute-start.11 = (bf16[768,128]{1,0:T(8,128)(2,1)S(1)}, bf16[768,128]{1,0:T(8,128)(2,1)S(1)}, u32[]{:S(2)}, u32[]{:S(2)}) collective-permute-start(bf16[768,128]{1,0:T(8,128)(2,1)S(1)} %get-tuple-element.55.refs_0_), channel_id=1, source_target_pairs={{0,1},{1,2},{2,3},{3,0},{4,5},{5,6},{6,7},{7,4},{8,9},{9,10},{10,1... | collective-permute-start | bytes 589832 | tf_op jit(solution)/shard_map/ppermute | solution.py:37
  100.1 5.8 %collective-permute-start.15 = (bf16[768,128]{1,0:T(8,128)(2,1)S(1)}, bf16[768,128]{1,0:T(8,128)(2,1)S(1)}, u32[]{:S(2)}, u32[]{:S(2)}) collective-permute-start(bf16[768,128]{1,0:T(8,128)(2,1)S(1)} %get-tuple-element.55.refs_0_), channel_id=1, source_target_pairs={{0,2},{1,3},{2,0},{3,1},{4,6},{5,7},{6,4},{7,5},{8,10},{9,11},{10,... | collective-permute-start | bytes 589832 | tf_op jit(solution)/shard_map/ppermute | solution.py:37
  107.9 4.5 %collective-permute-start.13 = (bf16[1536,128]{1,0:T(8,128)(2,1)S(1)}, bf16[1536,128]{1,0:T(8,128)(2,1)S(1)}, u32[]{:S(2)}, u32[]{:S(2)}) collective-permute-start(bf16[1536,128]{1,0:T(8,128)(2,1)S(1)} %cat.10.refs_0_), channel_id=1, source_target_pairs={{0,12},{1,13},{2,14},{3,15},{4,0},{5,1},{6,2},{7,3},{8,4},{9,5},{1... | collective-permute-start | bytes 1179656 | tf_op jit(solution)/shard_map/ppermute | solution.py:37
  114.3 3.9 %collective-permute-done.15.refs_1_ = bf16[768,128]{1,0:T(8,128)(2,1)S(1)} collective-permute-done((bf16[768,128]{1,0:T(8,128)(2,1)S(1)}, bf16[768,128]{1,0:T(8,128)(2,1)S(1)}, u32[]{:S(2)}, u32[]{:S(2)}) %collective-permute-start.15) | collective-permute-done | bytes 196640 | tf_op jit(solution)/shard_map/ppermute | solution.py:37
  118.2 3.3 %collective-permute-done.14.refs_0_ = bf16[768,128]{1,0:T(8,128)(2,1)S(1)} collective-permute-done((bf16[768,128]{1,0:T(8,128)(2,1)S(1)}, bf16[768,128]{1,0:T(8,128)(2,1)S(1)}, u32[]{:S(2)}, u32[]{:S(2)}) %collective-permute-start.14) | collective-permute-done | bytes 196640 | tf_op jit(solution)/shard_map/ppermute | solution.py:37
  121.6 4.5 %collective-permute-start.17 = (bf16[1536,128]{1,0:T(8,128)(2,1)S(1)}, bf16[1536,128]{1,0:T(8,128)(2,1)S(1)}, u32[]{:S(2)}, u32[]{:S(2)}) collective-permute-start(bf16[1536,128]{1,0:T(8,128)(2,1)S(1)} %cat.11.refs_3_), channel_id=1, source_target_pairs={{0,12},{1,13},{2,14},{3,15},{4,0},{5,1},{6,2},{7,3},{8,4},{9,5},{1... | collective-permute-start | bytes 1179656 | tf_op jit(solution)/shard_map/ppermute | solution.py:37
  128.1 5.1 %collective-permute-start.19 = (bf16[768,128]{1,0:T(8,128)(2,1)S(1)}, bf16[768,128]{1,0:T(8,128)(2,1)S(1)}, u32[]{:S(2)}, u32[]{:S(2)}) collective-permute-start(bf16[768,128]{1,0:T(8,128)(2,1)S(1)} %slice.17), channel_id=1, source_target_pairs={{0,12},{1,13},{2,14},{3,15},{4,0},{5,1},{6,2},{7,3},{8,4},{9,5},{1... | collective-permute-start | bytes 589832 | tf_op jit(solution)/shard_map/ppermute | solution.py:37
  135.6 5.6 %collective-permute-start.21 = (bf16[768,128]{1,0:T(8,128)(2,1)S(1)}, bf16[768,128]{1,0:T(8,128)(2,1)S(1)}, u32[]{:S(2)}, u32[]{:S(2)}) collective-permute-start(bf16[768,128]{1,0:T(8,128)(2,1)S(1)} %slice.19), channel_id=1, source_target_pairs={{0,12},{1,13},{2,14},{3,15},{4,0},{5,1},{6,2},{7,3},{8,4},{9,5},{1... | collective-permute-start | bytes 589832 | tf_op jit(solution)/shard_map/ppermute | solution.py:37
  143.2 3.6 %near.1.acc_ref = f32[256,512]{1,0:T(8,128)S(1)} custom-call(s32[5]{0:T(128)S(1)} %copy-done.7, bf16[256,128]{1,0:T(8,128)(2,1)S(1)} %copy-done.4, bf16[4096,512]{1,0:T(8,128)(2,1)S(1)} %copy-done, bf16[4096,512]{1,0:T(8,128)(2,1)S(1)} %get-tuple-element.54.b_other, bf16[1536,128]{1,0:T(8,128)(2,1)S(1)} %cat.10.refs_0_, ...), custom_call_target="tpu_custom_call" | custom-call | tf_op jit(solution)/shard_map/near/pallas_call | solution.py:330
  146.8 3.2 %collective-permute-done.20.refs_2_ = bf16[768,128]{1,0:T(8,128)(2,1)S(1)} collective-permute-done((bf16[768,128]{1,0:T(8,128)(2,1)S(1)}, bf16[768,128]{1,0:T(8,128)(2,1)S(1)}, u32[]{:S(2)}, u32[]{:S(2)}) %collective-permute-start.20) | collective-permute-done | bytes 196640 | tf_op jit(solution)/shard_map/ppermute | solution.py:37
  (77 shorter events, 29.5 us)
Async XLA Ops:
  6.5 76.1 %all-gather.2.cloned.1.call-start = ((), (), s32[]{:S(2)}) async-start(), calls=%async_computation | async-start | bytes 3612672 | tf_op jit(solution)/shard_map/all_gather | solution.py:113
  8.4 9.4 %collective-permute-start = (bf16[784,128]{1,0:T(8,128)(2,1)S(1)}, bf16[784,128]{1,0:T(8,128)(2,1)S(1)}, u32[]{:S(2)}, u32[]{:S(2)}) collective-permute-start(bf16[784,128]{1,0:T(8,128)(2,1)S(1)} %cat.6.refs_0_), channel_id=1, source_target_pairs={{0,1},{1,2},{2,3},{3,0},{4,5},{5,6},{6,7},{7,4},{8,9},{9,10},{10,1... | collective-permute-start | bytes 602120 | tf_op jit(solution)/shard_map/ppermute | solution.py:37
  11.9 18.5 %collective-permute-start.1 = (bf16[784,128]{1,0:T(8,128)(2,1)S(1)}, bf16[784,128]{1,0:T(8,128)(2,1)S(1)}, u32[]{:S(2)}, u32[]{:S(2)}) collective-permute-start(bf16[784,128]{1,0:T(8,128)(2,1)S(1)} %cat.6.refs_0_), channel_id=1, source_target_pairs={{0,32},{16,48},{32,0},{48,16},{64,96},{80,112},{96,64},{112,80},{1... | collective-permute-start | bytes 602120 | tf_op jit(solution)/shard_map/ppermute | solution.py:41
  31.2 16.6 %collective-permute-start.3 = (bf16[784,128]{1,0:T(8,128)(2,1)S(1)}, bf16[784,128]{1,0:T(8,128)(2,1)S(1)}, u32[]{:S(2)}, u32[]{:S(2)}) collective-permute-start(bf16[784,128]{1,0:T(8,128)(2,1)S(1)} %cat.6.refs_0_), channel_id=1, source_target_pairs={{0,2},{1,3},{2,0},{3,1},{4,6},{5,7},{6,4},{7,5},{8,10},{9,11},{10,... | collective-permute-start | bytes 602120 | tf_op jit(solution)/shard_map/ppermute | solution.py:37
  35.1 12.8 %collective-permute-start.2 = (bf16[784,128]{1,0:T(8,128)(2,1)S(1)}, bf16[784,128]{1,0:T(8,128)(2,1)S(1)}, u32[]{:S(2)}, u32[]{:S(2)}) collective-permute-start(bf16[784,128]{1,0:T(8,128)(2,1)S(1)} %cat.6.refs_0_), channel_id=1, source_target_pairs={{0,3},{1,0},{2,1},{3,2},{4,7},{5,4},{6,5},{7,6},{8,11},{9,8},{10,9... | collective-permute-start | bytes 602120 | tf_op jit(solution)/shard_map/ppermute | solution.py:37
  37.0 18.9 %collective-permute-start.6 = (bf16[1568,128]{1,0:T(8,128)(2,1)S(1)}, bf16[1568,128]{1,0:T(8,128)(2,1)S(1)}, u32[]{:S(2)}, u32[]{:S(2)}) collective-permute-start(bf16[1568,128]{1,0:T(8,128)(2,1)S(1)} %cat.7.refs_0_), channel_id=1, source_target_pairs={{0,8},{1,9},{2,10},{3,11},{4,12},{5,13},{6,14},{7,15},{8,0},{9,1},... | collective-permute-start | bytes 1204232 | tf_op jit(solution)/shard_map/ppermute | solution.py:37
  41.9 19.4 %collective-permute-start.5 = (bf16[1568,128]{1,0:T(8,128)(2,1)S(1)}, bf16[1568,128]{1,0:T(8,128)(2,1)S(1)}, u32[]{:S(2)}, u32[]{:S(2)}) collective-permute-start(bf16[1568,128]{1,0:T(8,128)(2,1)S(1)} %cat.7.refs_0_), channel_id=1, source_target_pairs={{0,12},{1,13},{2,14},{3,15},{4,0},{5,1},{6,2},{7,3},{8,4},{9,5},{1... | collective-permute-start | bytes 1204232 | tf_op jit(solution)/shard_map/ppermute | solution.py:37
  45.0 23.7 %collective-permute-start.4 = (bf16[1568,128]{1,0:T(8,128)(2,1)S(1)}, bf16[1568,128]{1,0:T(8,128)(2,1)S(1)}, u32[]{:S(2)}, u32[]{:S(2)}) collective-permute-start(bf16[1568,128]{1,0:T(8,128)(2,1)S(1)} %cat.7.refs_0_), channel_id=1, source_target_pairs={{0,4},{1,5},{2,6},{3,7},{4,8},{5,9},{6,10},{7,11},{8,12},{9,13},{1... | collective-permute-start | bytes 1204232 | tf_op jit(solution)/shard_map/ppermute | solution.py:37
  48.5 21.3 %collective-permute-start.9 = (bf16[1568,128]{1,0:T(8,128)(2,1)S(1)}, bf16[1568,128]{1,0:T(8,128)(2,1)S(1)}, u32[]{:S(2)}, u32[]{:S(2)}) collective-permute-start(bf16[1568,128]{1,0:T(8,128)(2,1)S(1)} %cat.9.refs_4_), channel_id=1, source_target_pairs={{0,8},{1,9},{2,10},{3,11},{4,12},{5,13},{6,14},{7,15},{8,0},{9,1},... | collective-permute-start | bytes 1204232 | tf_op jit(solution)/shard_map/ppermute | solution.py:37
  52.8 23.4 %collective-permute-start.8 = (bf16[1568,128]{1,0:T(8,128)(2,1)S(1)}, bf16[1568,128]{1,0:T(8,128)(2,1)S(1)}, u32[]{:S(2)}, u32[]{:S(2)}) collective-permute-start(bf16[1568,128]{1,0:T(8,128)(2,1)S(1)} %cat.9.refs_4_), channel_id=1, source_target_pairs={{0,12},{1,13},{2,14},{3,15},{4,0},{5,1},{6,2},{7,3},{8,4},{9,5},{1... | collective-permute-start | bytes 1204232 | tf_op jit(solution)/shard_map/ppermute | solution.py:37
  55.9 20.6 %collective-permute-start.7 = (bf16[1568,128]{1,0:T(8,128)(2,1)S(1)}, bf16[1568,128]{1,0:T(8,128)(2,1)S(1)}, u32[]{:S(2)}, u32[]{:S(2)}) collective-permute-start(bf16[1568,128]{1,0:T(8,128)(2,1)S(1)} %cat.9.refs_4_), channel_id=1, source_target_pairs={{0,4},{1,5},{2,6},{3,7},{4,8},{5,9},{6,10},{7,11},{8,12},{9,13},{1... | collective-permute-start | bytes 1204232 | tf_op jit(solution)/shard_map/ppermute | solution.py:37
  82.7 8.3 %collective-permute-start.10 = (bf16[12544,128]{1,0:T(8,128)(2,1)}, bf16[12544,128]{1,0:T(8,128)(2,1)}, u32[]{:S(2)}, u32[]{:S(2)}) collective-permute-start(bf16[12544,128]{1,0:T(8,128)(2,1)} %all-gather.2.cloned.1.call-done.v_ref), channel_id=1, source_target_pairs={{0,16},{16,0},{32,48},{48,32},{64,80},{80,64},{96,112},{112,96},{1... | collective-permute-start | bytes 9633800 | tf_op jit(solution)/shard_map/ppermute | solution.py:41
  92.0 51.2 %copy-start = (bf16[4096,512]{1,0:T(8,128)(2,1)S(1)}, bf16[4096,512]{1,0:T(8,128)(2,1)}, u32[]{:S(2)}) copy-start(bf16[4096,512]{1,0:T(8,128)(2,1)} %get-tuple-element.52.b_own) | copy-start | bytes 12582916
  96.5 11.4 %collective-permute-start.11 = (bf16[768,128]{1,0:T(8,128)(2,1)S(1)}, bf16[768,128]{1,0:T(8,128)(2,1)S(1)}, u32[]{:S(2)}, u32[]{:S(2)}) collective-permute-start(bf16[768,128]{1,0:T(8,128)(2,1)S(1)} %get-tuple-element.55.refs_0_), channel_id=1, source_target_pairs={{0,1},{1,2},{2,3},{3,0},{4,5},{5,6},{6,7},{7,4},{8,9},{9,10},{10,1... | collective-permute-start | bytes 589832 | tf_op jit(solution)/shard_map/ppermute | solution.py:37
  100.1 18.1 %collective-permute-start.15 = (bf16[768,128]{1,0:T(8,128)(2,1)S(1)}, bf16[768,128]{1,0:T(8,128)(2,1)S(1)}, u32[]{:S(2)}, u32[]{:S(2)}) collective-permute-start(bf16[768,128]{1,0:T(8,128)(2,1)S(1)} %get-tuple-element.55.refs_0_), channel_id=1, source_target_pairs={{0,2},{1,3},{2,0},{3,1},{4,6},{5,7},{6,4},{7,5},{8,10},{9,11},{10,... | collective-permute-start | bytes 589832 | tf_op jit(solution)/shard_map/ppermute | solution.py:37
  105.9 15.7 %collective-permute-start.14 = (bf16[768,128]{1,0:T(8,128)(2,1)S(1)}, bf16[768,128]{1,0:T(8,128)(2,1)S(1)}, u32[]{:S(2)}, u32[]{:S(2)}) collective-permute-start(bf16[768,128]{1,0:T(8,128)(2,1)S(1)} %get-tuple-element.55.refs_0_), channel_id=1, source_target_pairs={{0,3},{1,0},{2,1},{3,2},{4,7},{5,4},{6,5},{7,6},{8,11},{9,8},{10,9... | collective-permute-start | bytes 589832 | tf_op jit(solution)/shard_map/ppermute | solution.py:37
  107.9 20.1 %collective-permute-start.13 = (bf16[1536,128]{1,0:T(8,128)(2,1)S(1)}, bf16[1536,128]{1,0:T(8,128)(2,1)S(1)}, u32[]{:S(2)}, u32[]{:S(2)}) collective-permute-start(bf16[1536,128]{1,0:T(8,128)(2,1)S(1)} %cat.10.refs_0_), channel_id=1, source_target_pairs={{0,12},{1,13},{2,14},{3,15},{4,0},{5,1},{6,2},{7,3},{8,4},{9,5},{1... | collective-permute-start | bytes 1179656 | tf_op jit(solution)/shard_map/ppermute | solution.py:37
  112.4 20.8 %collective-permute-start.12 = (bf16[1536,128]{1,0:T(8,128)(2,1)S(1)}, bf16[1536,128]{1,0:T(8,128)(2,1)S(1)}, u32[]{:S(2)}, u32[]{:S(2)}) collective-permute-start(bf16[1536,128]{1,0:T(8,128)(2,1)S(1)} %cat.10.refs_0_), channel_id=1, source_target_pairs={{0,4},{1,5},{2,6},{3,7},{4,8},{5,9},{6,10},{7,11},{8,12},{9,13},{1... | collective-permute-start | bytes 1179656 | tf_op jit(solution)/shard_map/ppermute | solution.py:37
  121.6 14.0 %collective-permute-start.17 = (bf16[1536,128]{1,0:T(8,128)(2,1)S(1)}, bf16[1536,128]{1,0:T(8,128)(2,1)S(1)}, u32[]{:S(2)}, u32[]{:S(2)}) collective-permute-start(bf16[1536,128]{1,0:T(8,128)(2,1)S(1)} %cat.11.refs_3_), channel_id=1, source_target_pairs={{0,12},{1,13},{2,14},{3,15},{4,0},{5,1},{6,2},{7,3},{8,4},{9,5},{1... | collective-permute-start | bytes 1179656 | tf_op jit(solution)/shard_map/ppermute | solution.py:37
  126.1 15.1 %collective-permute-start.16 = (bf16[1536,128]{1,0:T(8,128)(2,1)S(1)}, bf16[1536,128]{1,0:T(8,128)(2,1)S(1)}, u32[]{:S(2)}, u32[]{:S(2)}) collective-permute-start(bf16[1536,128]{1,0:T(8,128)(2,1)S(1)} %cat.11.refs_3_), channel_id=1, source_target_pairs={{0,4},{1,5},{2,6},{3,7},{4,8},{5,9},{6,10},{7,11},{8,12},{9,13},{1... | collective-permute-start | bytes 1179656 | tf_op jit(solution)/shard_map/ppermute | solution.py:37
  128.1 18.7 %collective-permute-start.19 = (bf16[768,128]{1,0:T(8,128)(2,1)S(1)}, bf16[768,128]{1,0:T(8,128)(2,1)S(1)}, u32[]{:S(2)}, u32[]{:S(2)}) collective-permute-start(bf16[768,128]{1,0:T(8,128)(2,1)S(1)} %slice.17), channel_id=1, source_target_pairs={{0,12},{1,13},{2,14},{3,15},{4,0},{5,1},{6,2},{7,3},{8,4},{9,5},{1... | collective-permute-start | bytes 589832 | tf_op jit(solution)/shard_map/ppermute | solution.py:37
  133.2 13.5 %collective-permute-start.18 = (bf16[768,128]{1,0:T(8,128)(2,1)S(1)}, bf16[768,128]{1,0:T(8,128)(2,1)S(1)}, u32[]{:S(2)}, u32[]{:S(2)}) collective-permute-start(bf16[768,128]{1,0:T(8,128)(2,1)S(1)} %slice.16), channel_id=1, source_target_pairs={{0,4},{1,5},{2,6},{3,7},{4,8},{5,9},{6,10},{7,11},{8,12},{9,13},{1... | collective-permute-start | bytes 589832 | tf_op jit(solution)/shard_map/ppermute | solution.py:37
  135.6 11.2 %collective-permute-start.21 = (bf16[768,128]{1,0:T(8,128)(2,1)S(1)}, bf16[768,128]{1,0:T(8,128)(2,1)S(1)}, u32[]{:S(2)}, u32[]{:S(2)}) collective-permute-start(bf16[768,128]{1,0:T(8,128)(2,1)S(1)} %slice.19), channel_id=1, source_target_pairs={{0,12},{1,13},{2,14},{3,15},{4,0},{5,1},{6,2},{7,3},{8,4},{9,5},{1... | collective-permute-start | bytes 589832 | tf_op jit(solution)/shard_map/ppermute | solution.py:37
  141.2 8.8 %collective-permute-start.20 = (bf16[768,128]{1,0:T(8,128)(2,1)S(1)}, bf16[768,128]{1,0:T(8,128)(2,1)S(1)}, u32[]{:S(2)}, u32[]{:S(2)}) collective-permute-start(bf16[768,128]{1,0:T(8,128)(2,1)S(1)} %slice.18), channel_id=1, source_target_pairs={{0,4},{1,5},{2,6},{3,7},{4,8},{5,9},{6,10},{7,11},{8,12},{9,13},{1... | collective-permute-start | bytes 589832 | tf_op jit(solution)/shard_map/ppermute | solution.py:37
  (14 other events, 114.4 us)
Sparse Core Ops, SparseCore 0:
  31.3 49.2 all-gather.1

commit v4 on v3

--- a/solution.py
+++ b/solution.py
@@ -86,14 +86,6 @@
     )(*arrays)
 
 
-X_FAR = x_shift(2)
-
-ALL_PIECES = [
-    (g * 4 + a, n, dx, dy)
-    for g, dys in enumerate(((0, 3), (1, 2)))
-    for a, dx in enumerate((0, 3, 1, 2))
-    for n, dy in enumerate(dys)
-]
 NEAR_PIECES = [
     (g * 3 + a, n, dx, dy)
     for g, dys in enumerate(((0, 3), (1, 2)))
@@ -101,6 +93,7 @@
     for n, dy in enumerate(dys)
 ]
 FAR_PIECES = [(0, 0, 2, 0), (1, 0, 2, 3), (2, 0, 2, 1), (3, 0, 2, 2)]
+ALL_PIECES = NEAR_PIECES + [(6 + a, n, dx, dy) for a, n, dx, dy in FAR_PIECES]
 
 
 def gather(own):
@@ -108,12 +101,14 @@
     own_y = row(own, YH_SWAP)
     one = cat(own, col(own, yl_shift(1)))
     token, one, own = fence(token, one, own)
-    ones = [col(one, p) for p in (x_shift(1), x_shift(3), X_FAR)]
+    left1, right1 = [col(one, x_shift(s)) for s in (1, 3)]
     token, both, own = fence(token, cat(own, own_y), own)
     column = lax.all_gather(both, "row", axis_index_groups=Z_GROUPS, axis=0, tiled=True)
     token, two = fence(token, cat(col(own, yl_shift(3)), col(own, yl_shift(2))))
-    twos = [col(two, p) for p in (x_shift(1), x_shift(3), X_FAR)]
-    return [one, *ones, two, *twos], column, token
+    left2, right2 = [col(two, x_shift(s)) for s in (1, 3)]
+    far = [col(left1[:PAY], x_shift(1)), col(right1[PAY:], x_shift(3))]
+    far += [col(left2[:PAY], x_shift(1)), col(right2[PAY:], x_shift(3))]
+    return [one, left1, right1, two, left2, right2, *far], column, token
 
 
 def col_gather(own, rows):
@@ -122,9 +117,9 @@
     left1, right1 = col(one, x_shift(1)), col(one, x_shift(3))
     two = cat(line3, line2)
     left2, right2 = col(two, x_shift(1)), col(two, x_shift(3))
-    far1, far2 = col(left1[:rows], x_shift(1)), col(right1[rows:], x_shift(3))
-    far3, far4 = col(left2[:rows], x_shift(1)), col(right2[rows:], x_shift(3))
-    return [one, left1, right1, two, left2, right2], [far1, far2, far3, far4]
+    far = [col(left1[:rows], x_shift(1)), col(right1[rows:], x_shift(3))]
+    far += [col(left2[:rows], x_shift(1)), col(right2[rows:], x_shift(3))]
+    return [one, left1, right1, two, left2, right2], far
 
 
 def meta_rows(meta):
@@ -202,36 +197,34 @@
     return copies
 
 
-def half_kernel(pos, v_ref, b_ref, buffer, sems):
-    copies = fetch(v_ref, buffer, sems)
+def spread_half(pos, copies, src, b_ref):
     for z in range(NZ):
-        copies[z].wait()
+        if copies:
+            copies[z].wait()
         for n in range(2):
             base = (z * 2 + n) * PAY
-            slots = meta_rows(buffer[base + BLK : base + PAY])
+            slots = meta_rows(src[base + BLK : base + PAY])
             top = pl.multiple_of((z * 2 + (pos[1] ^ n)) * (ROWS * BS), ROWS * BS)
             for i in range(ROWS):
 
                 def store(r, q, d, top=top + i * BS):
                     b_ref[pl.ds(top + r, 16), q * BS : (q + 1) * BS] = d
 
-                spread(buffer, base + i * KD * BS, slots[i * KD : (i + 1) * KD], store)
-
-
-def own_half_kernel(pos, a_in, v_ref, acc_ref, b_ref, buffer, sems, a_ref, a_sem):
+                spread(src, base + i * KD * BS, slots[i * KD : (i + 1) * KD], store)
+
+
+def own_half_kernel(pos, a_in, v_in, acc_ref, b_ref, buffer, sems, a_ref, a_sem):
+    copies = fetch(v_in, buffer, sems)
     copy = pltpu.make_async_copy(a_in.at[:, pl.ds(0, HALF)], a_ref, a_sem)
     copy.start()
-    half_kernel(pos, v_ref, b_ref, buffer, sems)
+    spread_half(pos, copies, buffer, b_ref)
     copy.wait()
     acc_ref[...] = jnp.dot(a_ref[...], b_ref[...], preferred_element_type=F32)
 
 
-def square_kernel(pos, meta_ref, acc_ref, a_in, v_ref, square_ref, low_ref, b_ref, buffer, sems, a_ref, a_sem):
-    copy = pltpu.make_async_copy(a_in.at[:, pl.ds(HALF, HALF)], a_ref, a_sem)
-    copy.start()
-    half_kernel(pos, v_ref, b_ref, buffer, sems)
-    copy.wait()
-    acc = acc_ref[...] + jnp.dot(a_ref[...], b_ref[...], preferred_element_type=F32)
+def square_kernel(pos, meta_ref, acc_ref, a_ref, v_ref, square_ref, low_ref, b_ref):
+    spread_half(pos, None, v_ref, b_ref)
+    acc = acc_ref[...] + jnp.dot(a_ref[:, HALF:], b_ref[...], preferred_element_type=F32)
     at = pl.multiple_of(group_of(pos, 0, 0) * 16, 16)
     for s, d in enumerate(pick(acc, meta_rows(meta_ref[pl.ds(at, 16), :]))):
         square_ref[s * BS : (s + 1) * BS] = d
@@ -301,28 +294,26 @@
     )(pos, token, *strips)
     v, a, metas = lax.optimization_barrier((column, a, metas))
     v_other = row(v, CORE_SWAP)
-    block_scratch = [
-        pltpu.VMEM((2 * NZ * PAY, BS), BF),
-        pltpu.SemaphoreType.DMA((NZ,)),
-        pltpu.VMEM((ROWS * BS, HALF), BF),
-        pltpu.SemaphoreType.DMA(()),
-    ]
     acc, b_own = pl.pallas_call(
         own_half_kernel,
         out_shape=[acc_shape, b_shape],
         in_specs=[SM, HBM, HBM],
         out_specs=[VM, VM],
-        scratch_shapes=block_scratch,
-        compiler_params=params(57),
+        scratch_shapes=[
+            pltpu.VMEM((2 * NZ * PAY, BS), BF),
+            pltpu.SemaphoreType.DMA((NZ,)),
+            pltpu.VMEM((ROWS * BS, HALF), BF),
+            pltpu.SemaphoreType.DMA(()),
+        ],
+        compiler_params=params(53),
         name="own_half",
     )(pos, a, v)
     square, low, b_other = pl.pallas_call(
         square_kernel,
         out_shape=[shape(BLK, BS, dtype=F32), shape(BLK, BS), b_shape],
-        in_specs=[SM, VM, VM, HBM, pl.BlockSpec(memory_space=pl.ANY)],
-        out_specs=[VM, VM, VM],
-        scratch_shapes=block_scratch,
-        compiler_params=params(16),
+        in_specs=[SM] + [VM] * 4,
+        out_specs=[VM] * 3,
+        compiler_params=params(12),
         name="square",
     )(pos, metas, acc, a, v_other)
 

time: 160 us -> 156 us (0.975)
  the two profiles are of different devices: /device:TPU:72 before, /device:TPU:16 now
where the time goes in v4:
time: 156 us; the launch traced here: 155 us
  starting transfers between devices  85.2 us (55%)
  waiting for transfers between devices  31.4 us (20%)
  Pallas kernels  19.5 us (12%)
  between operations  14 us (9%)
  local copies, waits for them, and re-layouts  3.82 us (2%)
    ppermute x22, starting transfers between devices, col(): return lax.ppermute(a, 'col', perm)  78 us
    ppermute x22, waiting for transfers between devices, col(): return lax.ppermute(a, 'col', perm)  20.5 us
    ppermute x2, waiting for transfers between devices, row(): return lax.ppermute(a, 'row', perm)  8.91 us
    ppermute x2, starting transfers between devices, row(): return lax.ppermute(a, 'row', perm)  7.21 us
    pallas_call x1, Pallas kernels, local(): pl.pallas_call(own_half_kernel, out_shape=[acc_shape, b_shape], in_specs=...  5.22 us
    pallas_call x1, Pallas kernels, local(): pl.pallas_call(strip_kernel, out_shape=[shape(ROWS * BS, 2 * HALF), shape...  4.92 us
    pallas_call x1, Pallas kernels, local(): pl.pallas_call(near_kernel, out_shape=acc_shape, in_specs=[SM] + [VM] * 9...  3.66 us
  transfers between devices with their start and end apart: 25, of which 10 were waited for; matrix products, arithmetic and copies ran while one was open for 0% of the time, Pallas kernels for 9%

profile of v4, /device:TPU:16, one launch (start us, length us, event | category | flops | bytes accessed | tf_op | source)
XLA Modules:
  0.0 154.7 jit_solution(8723157063346817982)
XLA Ops:
  8.4 3.5 %collective-permute-start = (bf16[784,128]{1,0:T(8,128)(2,1)S(1)}, bf16[784,128]{1,0:T(8,128)(2,1)S(1)}, u32[]{:S(2)}, u32[]{:S(2)}) collective-permute-start(bf16[784,128]{1,0:T(8,128)(2,1)S(1)} %cat.6.refs_0_), channel_id=1, source_target_pairs={{0,1},{1,2},{2,3},{3,0},{4,5},{5,6},{6,7},{7,4},{8,9},{9,10},{10,1... | collective-permute-start | bytes 602120 | tf_op jit(solution)/shard_map/ppermute | solution.py:37
  11.9 5.0 %collective-permute-start.1 = (bf16[784,128]{1,0:T(8,128)(2,1)S(1)}, bf16[784,128]{1,0:T(8,128)(2,1)S(1)}, u32[]{:S(2)}, u32[]{:S(2)}) collective-permute-start(bf16[784,128]{1,0:T(8,128)(2,1)S(1)} %cat.6.refs_0_), channel_id=1, source_target_pairs={{0,32},{16,48},{32,0},{48,16},{64,96},{80,112},{96,64},{112,80},{1... | collective-permute-start | bytes 602120 | tf_op jit(solution)/shard_map/ppermute | solution.py:41
  17.1 8.8 %collective-permute-done.1.refs_1_ = bf16[784,128]{1,0:T(8,128)(2,1)S(1)} collective-permute-done((bf16[784,128]{1,0:T(8,128)(2,1)S(1)}, bf16[784,128]{1,0:T(8,128)(2,1)S(1)}, u32[]{:S(2)}, u32[]{:S(2)}) %collective-permute-start.1) | collective-permute-done | bytes 200736 | tf_op jit(solution)/shard_map/ppermute | solution.py:41
  26.7 6.4 %collective-permute-start.3 = (bf16[784,128]{1,0:T(8,128)(2,1)S(1)}, bf16[784,128]{1,0:T(8,128)(2,1)S(1)}, u32[]{:S(2)}, u32[]{:S(2)}) collective-permute-start(bf16[784,128]{1,0:T(8,128)(2,1)S(1)} %cat.6.refs_0_), channel_id=1, source_target_pairs={{0,2},{1,3},{2,0},{3,1},{4,6},{5,7},{6,4},{7,5},{8,10},{9,11},{10,... | collective-permute-start | bytes 602120 | tf_op jit(solution)/shard_map/ppermute | solution.py:37
  33.2 3.8 %collective-permute-start.2 = (bf16[784,128]{1,0:T(8,128)(2,1)S(1)}, bf16[784,128]{1,0:T(8,128)(2,1)S(1)}, u32[]{:S(2)}, u32[]{:S(2)}) collective-permute-start(bf16[784,128]{1,0:T(8,128)(2,1)S(1)} %cat.6.refs_0_), channel_id=1, source_target_pairs={{0,3},{1,0},{2,1},{3,2},{4,7},{5,4},{6,5},{7,6},{8,11},{9,8},{10,9... | collective-permute-start | bytes 602120 | tf_op jit(solution)/shard_map/ppermute | solution.py:37
  37.0 5.1 %collective-permute-start.5 = (bf16[1568,128]{1,0:T(8,128)(2,1)S(1)}, bf16[1568,128]{1,0:T(8,128)(2,1)S(1)}, u32[]{:S(2)}, u32[]{:S(2)}) collective-permute-start(bf16[1568,128]{1,0:T(8,128)(2,1)S(1)} %cat.7.refs_0_), channel_id=1, source_target_pairs={{0,12},{1,13},{2,14},{3,15},{4,0},{5,1},{6,2},{7,3},{8,4},{9,5},{1... | collective-permute-start | bytes 1204232 | tf_op jit(solution)/shard_map/ppermute | solution.py:37
  46.2 4.3 %collective-permute-start.7 = (bf16[1568,128]{1,0:T(8,128)(2,1)S(1)}, bf16[1568,128]{1,0:T(8,128)(2,1)S(1)}, u32[]{:S(2)}, u32[]{:S(2)}) collective-permute-start(bf16[1568,128]{1,0:T(8,128)(2,1)S(1)} %cat.9.refs_3_), channel_id=1, source_target_pairs={{0,12},{1,13},{2,14},{3,15},{4,0},{5,1},{6,2},{7,3},{8,4},{9,5},{1... | collective-permute-start | bytes 1204232 | tf_op jit(solution)/shard_map/ppermute | solution.py:37
  52.5 5.1 %collective-permute-start.9 = (bf16[784,128]{1,0:T(8,128)(2,1)S(1)}, bf16[784,128]{1,0:T(8,128)(2,1)S(1)}, u32[]{:S(2)}, u32[]{:S(2)}) collective-permute-start(bf16[784,128]{1,0:T(8,128)(2,1)S(1)} %slice.33), channel_id=1, source_target_pairs={{0,12},{1,13},{2,14},{3,15},{4,0},{5,1},{6,2},{7,3},{8,4},{9,5},{1... | collective-permute-start | bytes 602120 | tf_op jit(solution)/shard_map/ppermute | solution.py:37
  60.4 5.1 %collective-permute-start.11 = (bf16[784,128]{1,0:T(8,128)(2,1)S(1)}, bf16[784,128]{1,0:T(8,128)(2,1)S(1)}, u32[]{:S(2)}, u32[]{:S(2)}) collective-permute-start(bf16[784,128]{1,0:T(8,128)(2,1)S(1)} %slice.35), channel_id=1, source_target_pairs={{0,12},{1,13},{2,14},{3,15},{4,0},{5,1},{6,2},{7,3},{8,4},{9,5},{1... | collective-permute-start | bytes 602120 | tf_op jit(solution)/shard_map/ppermute | solution.py:37
  68.7 5.6 %collective-permute-done.10.refs_8_ = bf16[784,128]{1,0:T(8,128)(2,1)S(1)} collective-permute-done((bf16[784,128]{1,0:T(8,128)(2,1)S(1)}, bf16[784,128]{1,0:T(8,128)(2,1)S(1)}, u32[]{:S(2)}, u32[]{:S(2)}) %collective-permute-start.10) | collective-permute-done | bytes 200736 | tf_op jit(solution)/shard_map/ppermute | solution.py:37
  75.1 4.9 %strips.1 = (bf16[256,8192]{1,0:T(8,128)(2,1)}, bf16[256,128]{1,0:T(8,128)(2,1)}) custom-call(s32[5]{0:T(128)} %stack.23.pos, f32[8,128]{1,0:T(8,128)} %copy-done.7, bf16[1568,128]{1,0:T(8,128)(2,1)} %copy-done.2, bf16[1568,128]{1,0:T(8,128)(2,1)} %copy-done.9, bf16[1568,128]{1,0:T(8,128)(2,1)} %copy-done.8, bf16[1568,128]{1,0:T(8,128)(2,1)} %copy-done.3, ...), custom_call_target="tpu_custom_call" | custom-call | tf_op jit(solution)/shard_map/strips/pallas_call | solution.py:286
  84.8 5.2 %own_half.1 = (f32[256,512]{1,0:T(8,128)S(1)}, bf16[4096,512]{1,0:T(8,128)(2,1)}) custom-call(s32[5]{0:T(128)S(1)} %copy-done.6, bf16[256,8192]{1,0:T(8,128)(2,1)} %get-tuple-element.50.a_in.a_ref, bf16[12544,128]{1,0:T(8,128)(2,1)} %all-gather.2.cloned.1.call-done.v_in), custom_call_target="tpu_custom_call" | custom-call | tf_op jit(solution)/shard_map/own_half/pallas_call | solution.py:297
  90.1 2.6 %square.1 = (f32[768,128]{1,0:T(8,128)S(1)}, bf16[768,128]{1,0:T(8,128)(2,1)S(1)}, bf16[4096,512]{1,0:T(8,128)(2,1)S(1)}) custom-call(s32[5]{0:T(128)S(1)} %copy-done.6, bf16[256,128]{1,0:T(8,128)(2,1)S(1)} %copy-done.4, f32[256,512]{1,0:T(8,128)S(1)} %get-tuple-element.53.acc_ref, bf16[256,8192]{1,0:T(8,128)(2,1)S(1)} %copy-done.1, ...), custom_call_target="tpu_custom_call" | custom-call | tf_op jit(solution)/shard_map/square/pallas_call | solution.py:311
  92.8 3.4 %collective-permute-start.13 = (bf16[768,128]{1,0:T(8,128)(2,1)S(1)}, bf16[768,128]{1,0:T(8,128)(2,1)S(1)}, u32[]{:S(2)}, u32[]{:S(2)}) collective-permute-start(bf16[768,128]{1,0:T(8,128)(2,1)S(1)} %get-tuple-element.55.refs_0_), channel_id=1, source_target_pairs={{0,1},{1,2},{2,3},{3,0},{4,5},{5,6},{6,7},{7,4},{8,9},{9,10},{10,1... | collective-permute-start | bytes 589832 | tf_op jit(solution)/shard_map/ppermute | solution.py:37
  96.2 2.4 %collective-permute-start.17 = (bf16[768,128]{1,0:T(8,128)(2,1)S(1)}, bf16[768,128]{1,0:T(8,128)(2,1)S(1)}, u32[]{:S(2)}, u32[]{:S(2)}) collective-permute-start(bf16[768,128]{1,0:T(8,128)(2,1)S(1)} %get-tuple-element.55.refs_0_), channel_id=1, source_target_pairs={{0,2},{1,3},{2,0},{3,1},{4,6},{5,7},{6,4},{7,5},{8,10},{9,11},{10,... | collective-permute-start | bytes 589832 | tf_op jit(solution)/shard_map/ppermute | solution.py:37
  98.6 3.3 %collective-permute-start.16 = (bf16[768,128]{1,0:T(8,128)(2,1)S(1)}, bf16[768,128]{1,0:T(8,128)(2,1)S(1)}, u32[]{:S(2)}, u32[]{:S(2)}) collective-permute-start(bf16[768,128]{1,0:T(8,128)(2,1)S(1)} %get-tuple-element.55.refs_0_), channel_id=1, source_target_pairs={{0,3},{1,0},{2,1},{3,2},{4,7},{5,4},{6,5},{7,6},{8,11},{9,8},{10,9... | collective-permute-start | bytes 589832 | tf_op jit(solution)/shard_map/ppermute | solution.py:37
  102.0 8.8 %collective-permute-done.13.refs_1_ = bf16[768,128]{1,0:T(8,128)(2,1)S(1)} collective-permute-done((bf16[768,128]{1,0:T(8,128)(2,1)S(1)}, bf16[768,128]{1,0:T(8,128)(2,1)S(1)}, u32[]{:S(2)}, u32[]{:S(2)}) %collective-permute-start.13) | collective-permute-done | bytes 196640 | tf_op jit(solution)/shard_map/ppermute | solution.py:37
  110.8 4.6 %collective-permute-start.15 = (bf16[1536,128]{1,0:T(8,128)(2,1)S(1)}, bf16[1536,128]{1,0:T(8,128)(2,1)S(1)}, u32[]{:S(2)}, u32[]{:S(2)}) collective-permute-start(bf16[1536,128]{1,0:T(8,128)(2,1)S(1)} %cat.10.refs_0_), channel_id=1, source_target_pairs={{0,12},{1,13},{2,14},{3,15},{4,0},{5,1},{6,2},{7,3},{8,4},{9,5},{1... | collective-permute-start | bytes 1179656 | tf_op jit(solution)/shard_map/ppermute | solution.py:37
  117.4 5.1 %collective-permute-start.19 = (bf16[1536,128]{1,0:T(8,128)(2,1)S(1)}, bf16[1536,128]{1,0:T(8,128)(2,1)S(1)}, u32[]{:S(2)}, u32[]{:S(2)}) collective-permute-start(bf16[1536,128]{1,0:T(8,128)(2,1)S(1)} %cat.11.refs_3_), channel_id=1, source_target_pairs={{0,12},{1,13},{2,14},{3,15},{4,0},{5,1},{6,2},{7,3},{8,4},{9,5},{1... | collective-permute-start | bytes 1179656 | tf_op jit(solution)/shard_map/ppermute | solution.py:37
  124.5 5.1 %collective-permute-start.21 = (bf16[768,128]{1,0:T(8,128)(2,1)S(1)}, bf16[768,128]{1,0:T(8,128)(2,1)S(1)}, u32[]{:S(2)}, u32[]{:S(2)}) collective-permute-start(bf16[768,128]{1,0:T(8,128)(2,1)S(1)} %slice.37), channel_id=1, source_target_pairs={{0,12},{1,13},{2,14},{3,15},{4,0},{5,1},{6,2},{7,3},{8,4},{9,5},{1... | collective-permute-start | bytes 589832 | tf_op jit(solution)/shard_map/ppermute | solution.py:37
  131.7 5.2 %collective-permute-start.23 = (bf16[768,128]{1,0:T(8,128)(2,1)S(1)}, bf16[768,128]{1,0:T(8,128)(2,1)S(1)}, u32[]{:S(2)}, u32[]{:S(2)}) collective-permute-start(bf16[768,128]{1,0:T(8,128)(2,1)S(1)} %slice.39), channel_id=1, source_target_pairs={{0,12},{1,13},{2,14},{3,15},{4,0},{5,1},{6,2},{7,3},{8,4},{9,5},{1... | collective-permute-start | bytes 589832 | tf_op jit(solution)/shard_map/ppermute | solution.py:37
  138.8 3.7 %near.1.acc_ref = f32[256,512]{1,0:T(8,128)S(1)} custom-call(s32[5]{0:T(128)S(1)} %copy-done.6, bf16[256,128]{1,0:T(8,128)(2,1)S(1)} %copy-done.4, bf16[4096,512]{1,0:T(8,128)(2,1)S(1)} %copy-done, bf16[4096,512]{1,0:T(8,128)(2,1)S(1)} %get-tuple-element.54.b_other, bf16[1536,128]{1,0:T(8,128)(2,1)S(1)} %cat.10.refs_0_, ...), custom_call_target="tpu_custom_call" | custom-call | tf_op jit(solution)/shard_map/near/pallas_call | solution.py:321
  142.5 3.1 %collective-permute-done.22.refs_2_ = bf16[768,128]{1,0:T(8,128)(2,1)S(1)} collective-permute-done((bf16[768,128]{1,0:T(8,128)(2,1)S(1)}, bf16[768,128]{1,0:T(8,128)(2,1)S(1)}, u32[]{:S(2)}, u32[]{:S(2)}) %collective-permute-start.22) | collective-permute-done | bytes 196640 | tf_op jit(solution)/shard_map/ppermute | solution.py:37
  145.7 2.2 %far.1 = bf16[768,128]{1,0:T(8,128)(2,1)} custom-call(s32[5]{0:T(128)S(1)} %copy-done.6, bf16[256,128]{1,0:T(8,128)(2,1)S(1)} %copy-done.4, bf16[4096,512]{1,0:T(8,128)(2,1)S(1)} %copy-done, bf16[4096,512]{1,0:T(8,128)(2,1)S(1)} %get-tuple-element.54.b_other, f32[256,512]{1,0:T(8,128)S(1)} %near.1.acc_ref, f32[768,128]{1,0:T(8,128)S(1)} %get-tuple-element.56.square_ref, ...), custom_call_target="tpu_custom_call" | custom-call | tf_op jit(solution)/shard_map/far/pallas_call | solution.py:330
  (87 shorter events, 28.0 us)
Async XLA Ops:
  6.5 75.5 %all-gather.2.cloned.1.call-start = ((), (), s32[]{:S(2)}) async-start(), calls=%async_computation | async-start | bytes 3612672 | tf_op jit(solution)/shard_map/all_gather | solution.py:106
  8.4 8.6 %collective-permute-start = (bf16[784,128]{1,0:T(8,128)(2,1)S(1)}, bf16[784,128]{1,0:T(8,128)(2,1)S(1)}, u32[]{:S(2)}, u32[]{:S(2)}) collective-permute-start(bf16[784,128]{1,0:T(8,128)(2,1)S(1)} %cat.6.refs_0_), channel_id=1, source_target_pairs={{0,1},{1,2},{2,3},{3,0},{4,5},{5,6},{6,7},{7,4},{8,9},{9,10},{10,1... | collective-permute-start | bytes 602120 | tf_op jit(solution)/shard_map/ppermute | solution.py:37
  11.9 14.0 %collective-permute-start.1 = (bf16[784,128]{1,0:T(8,128)(2,1)S(1)}, bf16[784,128]{1,0:T(8,128)(2,1)S(1)}, u32[]{:S(2)}, u32[]{:S(2)}) collective-permute-start(bf16[784,128]{1,0:T(8,128)(2,1)S(1)} %cat.6.refs_0_), channel_id=1, source_target_pairs={{0,32},{16,48},{32,0},{48,16},{64,96},{80,112},{96,64},{112,80},{1... | collective-permute-start | bytes 602120 | tf_op jit(solution)/shard_map/ppermute | solution.py:41
  26.7 17.3 %collective-permute-start.3 = (bf16[784,128]{1,0:T(8,128)(2,1)S(1)}, bf16[784,128]{1,0:T(8,128)(2,1)S(1)}, u32[]{:S(2)}, u32[]{:S(2)}) collective-permute-start(bf16[784,128]{1,0:T(8,128)(2,1)S(1)} %cat.6.refs_0_), channel_id=1, source_target_pairs={{0,2},{1,3},{2,0},{3,1},{4,6},{5,7},{6,4},{7,5},{8,10},{9,11},{10,... | collective-permute-start | bytes 602120 | tf_op jit(solution)/shard_map/ppermute | solution.py:37
  33.2 12.4 %collective-permute-start.2 = (bf16[784,128]{1,0:T(8,128)(2,1)S(1)}, bf16[784,128]{1,0:T(8,128)(2,1)S(1)}, u32[]{:S(2)}, u32[]{:S(2)}) collective-permute-start(bf16[784,128]{1,0:T(8,128)(2,1)S(1)} %cat.6.refs_0_), channel_id=1, source_target_pairs={{0,3},{1,0},{2,1},{3,2},{4,7},{5,4},{6,5},{7,6},{8,11},{9,8},{10,9... | collective-permute-start | bytes 602120 | tf_op jit(solution)/shard_map/ppermute | solution.py:37
  37.0 15.5 %collective-permute-start.5 = (bf16[1568,128]{1,0:T(8,128)(2,1)S(1)}, bf16[1568,128]{1,0:T(8,128)(2,1)S(1)}, u32[]{:S(2)}, u32[]{:S(2)}) collective-permute-start(bf16[1568,128]{1,0:T(8,128)(2,1)S(1)} %cat.7.refs_0_), channel_id=1, source_target_pairs={{0,12},{1,13},{2,14},{3,15},{4,0},{5,1},{6,2},{7,3},{8,4},{9,5},{1... | collective-permute-start | bytes 1204232 | tf_op jit(solution)/shard_map/ppermute | solution.py:37
  42.1 15.5 %collective-permute-start.4 = (bf16[1568,128]{1,0:T(8,128)(2,1)S(1)}, bf16[1568,128]{1,0:T(8,128)(2,1)S(1)}, u32[]{:S(2)}, u32[]{:S(2)}) collective-permute-start(bf16[1568,128]{1,0:T(8,128)(2,1)S(1)} %cat.7.refs_0_), channel_id=1, source_target_pairs={{0,4},{1,5},{2,6},{3,7},{4,8},{5,9},{6,10},{7,11},{8,12},{9,13},{1... | collective-permute-start | bytes 1204232 | tf_op jit(solution)/shard_map/ppermute | solution.py:37
  46.2 14.1 %collective-permute-start.7 = (bf16[1568,128]{1,0:T(8,128)(2,1)S(1)}, bf16[1568,128]{1,0:T(8,128)(2,1)S(1)}, u32[]{:S(2)}, u32[]{:S(2)}) collective-permute-start(bf16[1568,128]{1,0:T(8,128)(2,1)S(1)} %cat.9.refs_3_), channel_id=1, source_target_pairs={{0,12},{1,13},{2,14},{3,15},{4,0},{5,1},{6,2},{7,3},{8,4},{9,5},{1... | collective-permute-start | bytes 1204232 | tf_op jit(solution)/shard_map/ppermute | solution.py:37
  50.5 15.0 %collective-permute-start.6 = (bf16[1568,128]{1,0:T(8,128)(2,1)S(1)}, bf16[1568,128]{1,0:T(8,128)(2,1)S(1)}, u32[]{:S(2)}, u32[]{:S(2)}) collective-permute-start(bf16[1568,128]{1,0:T(8,128)(2,1)S(1)} %cat.9.refs_3_), channel_id=1, source_target_pairs={{0,4},{1,5},{2,6},{3,7},{4,8},{5,9},{6,10},{7,11},{8,12},{9,13},{1... | collective-permute-start | bytes 1204232 | tf_op jit(solution)/shard_map/ppermute | solution.py:37
  52.5 15.7 %collective-permute-start.9 = (bf16[784,128]{1,0:T(8,128)(2,1)S(1)}, bf16[784,128]{1,0:T(8,128)(2,1)S(1)}, u32[]{:S(2)}, u32[]{:S(2)}) collective-permute-start(bf16[784,128]{1,0:T(8,128)(2,1)S(1)} %slice.33), channel_id=1, source_target_pairs={{0,12},{1,13},{2,14},{3,15},{4,0},{5,1},{6,2},{7,3},{8,4},{9,5},{1... | collective-permute-start | bytes 602120 | tf_op jit(solution)/shard_map/ppermute | solution.py:37
  57.7 10.5 %collective-permute-start.8 = (bf16[784,128]{1,0:T(8,128)(2,1)S(1)}, bf16[784,128]{1,0:T(8,128)(2,1)S(1)}, u32[]{:S(2)}, u32[]{:S(2)}) collective-permute-start(bf16[784,128]{1,0:T(8,128)(2,1)S(1)} %slice.32), channel_id=1, source_target_pairs={{0,4},{1,5},{2,6},{3,7},{4,8},{5,9},{6,10},{7,11},{8,12},{9,13},{1... | collective-permute-start | bytes 602120 | tf_op jit(solution)/shard_map/ppermute | solution.py:37
  60.4 8.4 %collective-permute-start.11 = (bf16[784,128]{1,0:T(8,128)(2,1)S(1)}, bf16[784,128]{1,0:T(8,128)(2,1)S(1)}, u32[]{:S(2)}, u32[]{:S(2)}) collective-permute-start(bf16[784,128]{1,0:T(8,128)(2,1)S(1)} %slice.35), channel_id=1, source_target_pairs={{0,12},{1,13},{2,14},{3,15},{4,0},{5,1},{6,2},{7,3},{8,4},{9,5},{1... | collective-permute-start | bytes 602120 | tf_op jit(solution)/shard_map/ppermute | solution.py:37
  65.6 8.8 %collective-permute-start.10 = (bf16[784,128]{1,0:T(8,128)(2,1)S(1)}, bf16[784,128]{1,0:T(8,128)(2,1)S(1)}, u32[]{:S(2)}, u32[]{:S(2)}) collective-permute-start(bf16[784,128]{1,0:T(8,128)(2,1)S(1)} %slice.34), channel_id=1, source_target_pairs={{0,4},{1,5},{2,6},{3,7},{4,8},{5,9},{6,10},{7,11},{8,12},{9,13},{1... | collective-permute-start | bytes 602120 | tf_op jit(solution)/shard_map/ppermute | solution.py:37
  92.8 18.0 %collective-permute-start.13 = (bf16[768,128]{1,0:T(8,128)(2,1)S(1)}, bf16[768,128]{1,0:T(8,128)(2,1)S(1)}, u32[]{:S(2)}, u32[]{:S(2)}) collective-permute-start(bf16[768,128]{1,0:T(8,128)(2,1)S(1)} %get-tuple-element.55.refs_0_), channel_id=1, source_target_pairs={{0,1},{1,2},{2,3},{3,0},{4,5},{5,6},{6,7},{7,4},{8,9},{9,10},{10,1... | collective-permute-start | bytes 589832 | tf_op jit(solution)/shard_map/ppermute | solution.py:37
  96.2 21.2 %collective-permute-start.17 = (bf16[768,128]{1,0:T(8,128)(2,1)S(1)}, bf16[768,128]{1,0:T(8,128)(2,1)S(1)}, u32[]{:S(2)}, u32[]{:S(2)}) collective-permute-start(bf16[768,128]{1,0:T(8,128)(2,1)S(1)} %get-tuple-element.55.refs_0_), channel_id=1, source_target_pairs={{0,2},{1,3},{2,0},{3,1},{4,6},{5,7},{6,4},{7,5},{8,10},{9,11},{10,... | collective-permute-start | bytes 589832 | tf_op jit(solution)/shard_map/ppermute | solution.py:37
  98.6 18.8 %collective-permute-start.16 = (bf16[768,128]{1,0:T(8,128)(2,1)S(1)}, bf16[768,128]{1,0:T(8,128)(2,1)S(1)}, u32[]{:S(2)}, u32[]{:S(2)}) collective-permute-start(bf16[768,128]{1,0:T(8,128)(2,1)S(1)} %get-tuple-element.55.refs_0_), channel_id=1, source_target_pairs={{0,3},{1,0},{2,1},{3,2},{4,7},{5,4},{6,5},{7,6},{8,11},{9,8},{10,9... | collective-permute-start | bytes 589832 | tf_op jit(solution)/shard_map/ppermute | solution.py:37
  110.8 13.7 %collective-permute-start.15 = (bf16[1536,128]{1,0:T(8,128)(2,1)S(1)}, bf16[1536,128]{1,0:T(8,128)(2,1)S(1)}, u32[]{:S(2)}, u32[]{:S(2)}) collective-permute-start(bf16[1536,128]{1,0:T(8,128)(2,1)S(1)} %cat.10.refs_0_), channel_id=1, source_target_pairs={{0,12},{1,13},{2,14},{3,15},{4,0},{5,1},{6,2},{7,3},{8,4},{9,5},{1... | collective-permute-start | bytes 1179656 | tf_op jit(solution)/shard_map/ppermute | solution.py:37
  115.4 14.2 %collective-permute-start.14 = (bf16[1536,128]{1,0:T(8,128)(2,1)S(1)}, bf16[1536,128]{1,0:T(8,128)(2,1)S(1)}, u32[]{:S(2)}, u32[]{:S(2)}) collective-permute-start(bf16[1536,128]{1,0:T(8,128)(2,1)S(1)} %cat.10.refs_0_), channel_id=1, source_target_pairs={{0,4},{1,5},{2,6},{3,7},{4,8},{5,9},{6,10},{7,11},{8,12},{9,13},{1... | collective-permute-start | bytes 1179656 | tf_op jit(solution)/shard_map/ppermute | solution.py:37
  117.4 14.2 %collective-permute-start.19 = (bf16[1536,128]{1,0:T(8,128)(2,1)S(1)}, bf16[1536,128]{1,0:T(8,128)(2,1)S(1)}, u32[]{:S(2)}, u32[]{:S(2)}) collective-permute-start(bf16[1536,128]{1,0:T(8,128)(2,1)S(1)} %cat.11.refs_3_), channel_id=1, source_target_pairs={{0,12},{1,13},{2,14},{3,15},{4,0},{5,1},{6,2},{7,3},{8,4},{9,5},{1... | collective-permute-start | bytes 1179656 | tf_op jit(solution)/shard_map/ppermute | solution.py:37
  122.6 14.3 %collective-permute-start.18 = (bf16[1536,128]{1,0:T(8,128)(2,1)S(1)}, bf16[1536,128]{1,0:T(8,128)(2,1)S(1)}, u32[]{:S(2)}, u32[]{:S(2)}) collective-permute-start(bf16[1536,128]{1,0:T(8,128)(2,1)S(1)} %cat.11.refs_3_), channel_id=1, source_target_pairs={{0,4},{1,5},{2,6},{3,7},{4,8},{5,9},{6,10},{7,11},{8,12},{9,13},{1... | collective-permute-start | bytes 1179656 | tf_op jit(solution)/shard_map/ppermute | solution.py:37
  124.5 18.0 %collective-permute-start.21 = (bf16[768,128]{1,0:T(8,128)(2,1)S(1)}, bf16[768,128]{1,0:T(8,128)(2,1)S(1)}, u32[]{:S(2)}, u32[]{:S(2)}) collective-permute-start(bf16[768,128]{1,0:T(8,128)(2,1)S(1)} %slice.37), channel_id=1, source_target_pairs={{0,12},{1,13},{2,14},{3,15},{4,0},{5,1},{6,2},{7,3},{8,4},{9,5},{1... | collective-permute-start | bytes 589832 | tf_op jit(solution)/shard_map/ppermute | solution.py:37
  129.7 12.8 %collective-permute-start.20 = (bf16[768,128]{1,0:T(8,128)(2,1)S(1)}, bf16[768,128]{1,0:T(8,128)(2,1)S(1)}, u32[]{:S(2)}, u32[]{:S(2)}) collective-permute-start(bf16[768,128]{1,0:T(8,128)(2,1)S(1)} %slice.36), channel_id=1, source_target_pairs={{0,4},{1,5},{2,6},{3,7},{4,8},{5,9},{6,10},{7,11},{8,12},{9,13},{1... | collective-permute-start | bytes 589832 | tf_op jit(solution)/shard_map/ppermute | solution.py:37
  131.7 10.9 %collective-permute-start.23 = (bf16[768,128]{1,0:T(8,128)(2,1)S(1)}, bf16[768,128]{1,0:T(8,128)(2,1)S(1)}, u32[]{:S(2)}, u32[]{:S(2)}) collective-permute-start(bf16[768,128]{1,0:T(8,128)(2,1)S(1)} %slice.39), channel_id=1, source_target_pairs={{0,12},{1,13},{2,14},{3,15},{4,0},{5,1},{6,2},{7,3},{8,4},{9,5},{1... | collective-permute-start | bytes 589832 | tf_op jit(solution)/shard_map/ppermute | solution.py:37
  136.9 8.8 %collective-permute-start.22 = (bf16[768,128]{1,0:T(8,128)(2,1)S(1)}, bf16[768,128]{1,0:T(8,128)(2,1)S(1)}, u32[]{:S(2)}, u32[]{:S(2)}) collective-permute-start(bf16[768,128]{1,0:T(8,128)(2,1)S(1)} %slice.38), channel_id=1, source_target_pairs={{0,4},{1,5},{2,6},{3,7},{4,8},{5,9},{6,10},{7,11},{8,12},{9,13},{1... | collective-permute-start | bytes 589832 | tf_op jit(solution)/shard_map/ppermute | solution.py:37
  (17 other events, 187.6 us)
Sparse Core Ops, SparseCore 0:
  26.8 55.1 all-gather.1

commit v5 on v4

--- a/solution.py
+++ b/solution.py
@@ -17,7 +17,6 @@
 BF = jnp.bfloat16
 F32 = jnp.float32
 VM = pl.BlockSpec(memory_space=pltpu.VMEM)
-SM = pl.BlockSpec(memory_space=pltpu.SMEM)
 HBM = pl.BlockSpec(memory_space=pltpu.HBM)
 
 CORE_SWAP = [(r, r ^ 1) for r in range(32)]
@@ -29,12 +28,21 @@
     return [(c, c // 4 * 4 + (c + s) % 4) for c in range(16)]
 
 
-def x_shift(s):
-    return [(c, (c + 4 * s) % 16) for c in range(16)]
+def x_step(s):
+    return [
+        (r * 16 + c, r * 16 + (c + 4 * s * (1 - 2 * (r % 2))) % 16) for r in range(32) for c in range(16)
+    ]
+
+
+AHEAD, BACK = x_step(1), x_step(-1)
 
 
 def col(a, perm):
     return lax.ppermute(a, "col", perm)
+
+
+def both_axes(a, perm):
+    return lax.ppermute(a, ("row", "col"), perm)
 
 
 def row(a, perm):
@@ -89,10 +97,10 @@
 NEAR_PIECES = [
     (g * 3 + a, n, dx, dy)
     for g, dys in enumerate(((0, 3), (1, 2)))
-    for a, dx in enumerate((0, 3, 1))
+    for a, dx in enumerate((0, -1, 1))
     for n, dy in enumerate(dys)
 ]
-FAR_PIECES = [(0, 0, 2, 0), (1, 0, 2, 3), (2, 0, 2, 1), (3, 0, 2, 2)]
+FAR_PIECES = [(0, 0, 2, 0), (0, 1, 2, 3), (1, 0, 2, 1), (1, 1, 2, 2)]
 ALL_PIECES = NEAR_PIECES + [(6 + a, n, dx, dy) for a, n, dx, dy in FAR_PIECES]
 
 
@@ -101,25 +109,27 @@
     own_y = row(own, YH_SWAP)
     one = cat(own, col(own, yl_shift(1)))
     token, one, own = fence(token, one, own)
-    left1, right1 = [col(one, x_shift(s)) for s in (1, 3)]
+    ahead1, back1 = both_axes(one, AHEAD), both_axes(one, BACK)
     token, both, own = fence(token, cat(own, own_y), own)
     column = lax.all_gather(both, "row", axis_index_groups=Z_GROUPS, axis=0, tiled=True)
     token, two = fence(token, cat(col(own, yl_shift(3)), col(own, yl_shift(2))))
-    left2, right2 = [col(two, x_shift(s)) for s in (1, 3)]
-    far = [col(left1[:PAY], x_shift(1)), col(right1[PAY:], x_shift(3))]
-    far += [col(left2[:PAY], x_shift(1)), col(right2[PAY:], x_shift(3))]
-    return [one, left1, right1, two, left2, right2, *far], column, token
-
-
-def col_gather(own, rows):
+    ahead2, back2 = both_axes(two, AHEAD), both_axes(two, BACK)
+    ahead1, back1 = lax.optimization_barrier((ahead1, back1))
+    ahead2, back2 = lax.optimization_barrier((ahead2, back2))
+    far = [both_axes(ahead1, AHEAD), both_axes(ahead2, AHEAD)]
+    return [one, ahead1, back1, two, ahead2, back2, *far], column, token
+
+
+def col_gather(own):
     line1, line3, line2 = [col(own, yl_shift(s)) for s in (1, 3, 2)]
     one = cat(own, line1)
-    left1, right1 = col(one, x_shift(1)), col(one, x_shift(3))
+    ahead1, back1 = both_axes(one, AHEAD), both_axes(one, BACK)
     two = cat(line3, line2)
-    left2, right2 = col(two, x_shift(1)), col(two, x_shift(3))
-    far = [col(left1[:rows], x_shift(1)), col(right1[rows:], x_shift(3))]
-    far += [col(left2[:rows], x_shift(1)), col(right2[rows:], x_shift(3))]
-    return [one, left1, right1, two, left2, right2], far
+    ahead2, back2 = both_axes(two, AHEAD), both_axes(two, BACK)
+    ahead1, back1 = lax.optimization_barrier((ahead1, back1))
+    ahead2, back2 = lax.optimization_barrier((ahead2, back2))
+    far = [both_axes(ahead1, AHEAD), both_axes(ahead2, AHEAD)]
+    return [one, ahead1, back1, two, ahead2, back2], far
 
 
 def meta_rows(meta):
@@ -146,8 +156,13 @@
     lax.fori_loop(0, BS // 16, step, 0, unroll=True)
 
 
+def position():
+    r, c = lax.axis_index("row"), lax.axis_index("col")
+    return r >> 2, (r >> 1) & 1, r & 1, c >> 2, c & 3
+
+
 def group_of(pos, dx, dy):
-    return ((pos[3] + dx) & 3) * 4 + ((pos[4] + dy) & 3)
+    return ((pos[3] + dx * (1 - 2 * pos[2])) & 3) * 4 + ((pos[4] + dy) & 3)
 
 
 def spread_row(pos, src, base, i, slots, group, a_ref):
@@ -171,7 +186,8 @@
     return out
 
 
-def strip_kernel(pos, token, *refs):
+def strip_kernel(token, *refs):
+    pos = position()
     cols, (a_out, meta_ref, a_ref, sems) = refs[:-4], refs[-4:]
     copies = []
     for i in range(ROWS):
@@ -213,7 +229,8 @@
                 spread(src, base + i * KD * BS, slots[i * KD : (i + 1) * KD], store)
 
 
-def own_half_kernel(pos, a_in, v_in, acc_ref, b_ref, buffer, sems, a_ref, a_sem):
+def own_half_kernel(a_in, v_in, acc_ref, b_ref, buffer, sems, a_ref, a_sem):
+    pos = position()
     copies = fetch(v_in, buffer, sems)
     copy = pltpu.make_async_copy(a_in.at[:, pl.ds(0, HALF)], a_ref, a_sem)
     copy.start()
@@ -222,7 +239,8 @@
     acc_ref[...] = jnp.dot(a_ref[...], b_ref[...], preferred_element_type=F32)
 
 
-def square_kernel(pos, meta_ref, acc_ref, a_ref, v_ref, square_ref, low_ref, b_ref):
+def square_kernel(meta_ref, acc_ref, a_ref, v_ref, square_ref, low_ref, b_ref):
+    pos = position()
     spread_half(pos, None, v_ref, b_ref)
     acc = acc_ref[...] + jnp.dot(a_ref[:, HALF:], b_ref[...], preferred_element_type=F32)
     at = pl.multiple_of(group_of(pos, 0, 0) * 16, 16)
@@ -231,7 +249,8 @@
         low_ref[s * BS : (s + 1) * BS] = d.astype(BF)
 
 
-def near_kernel(pos, meta_ref, b_own, b_other, *refs):
+def near_kernel(meta_ref, b_own, b_other, *refs):
+    pos = position()
     lows, acc_ref, a_ref = refs[:-2], refs[-2], refs[-1]
     for _, _, dx, dy in FAR_PIECES:
         for half in range(2):
@@ -247,7 +266,8 @@
     )
 
 
-def far_kernel(pos, meta_ref, b_own, b_other, acc_ref, square_ref, *refs):
+def far_kernel(meta_ref, b_own, b_other, acc_ref, square_ref, *refs):
+    pos = position()
     lows, (out_ref, a_ref, b_ref) = refs[:-3], refs[-3:]
     width = ROWS * BS
     for m, (a, n, dx, dy) in enumerate(FAR_PIECES):
@@ -278,26 +298,24 @@
     meta = jnp.pad(meta, ((0, 16 - ROWS * KD), (0, 0)))
     density = density.reshape(BLK, BS)
     own = cat(density, meta)
-    r, c = lax.axis_index("row"), lax.axis_index("col")
-    pos = jnp.stack([r // 4, r // 2 % 2, r % 2, c // 4, c % 4]).astype(jnp.int32)
     strips, column, token = gather(own)
     acc_shape = shape(ROWS * BS, CG * BS, dtype=F32)
     b_shape = shape(HALF, CG * BS)
     a, metas = pl.pallas_call(
         strip_kernel,
         out_shape=[shape(ROWS * BS, 2 * HALF), shape(NG * 16, BS)],
-        in_specs=[SM, VM] + [VM] * len(strips),
+        in_specs=[VM] * (1 + len(strips)),
         out_specs=[HBM, VM],
         scratch_shapes=[pltpu.VMEM((ROWS * BS, 2 * HALF), BF), pltpu.SemaphoreType.DMA((ROWS,))],
         compiler_params=params(58),
         name="strips",
-    )(pos, token, *strips)
+    )(token, *strips)
     v, a, metas = lax.optimization_barrier((column, a, metas))
     v_other = row(v, CORE_SWAP)
     acc, b_own = pl.pallas_call(
         own_half_kernel,
         out_shape=[acc_shape, b_shape],
-        in_specs=[SM, HBM, HBM],
+        in_specs=[HBM, HBM],
         out_specs=[VM, VM],
         scratch_shapes=[
             pltpu.VMEM((2 * NZ * PAY, BS), BF),
@@ -307,35 +325,35 @@
         ],
         compiler_params=params(53),
         name="own_half",
-    )(pos, a, v)
+    )(a, v)
     square, low, b_other = pl.pallas_call(
         square_kernel,
         out_shape=[shape(BLK, BS, dtype=F32), shape(BLK, BS), b_shape],
-        in_specs=[SM] + [VM] * 4,
+        in_specs=[VM] * 4,
         out_specs=[VM] * 3,
         compiler_params=params(12),
         name="square",
-    )(pos, metas, acc, a, v_other)
-
-    near, far = col_gather(low, BLK)
+    )(metas, acc, a, v_other)
+
+    near, far = col_gather(low)
     acc = pl.pallas_call(
         near_kernel,
         out_shape=acc_shape,
-        in_specs=[SM] + [VM] * 9,
+        in_specs=[VM] * 9,
         out_specs=VM,
         scratch_shapes=[pltpu.VMEM((ROWS * BS, 2 * HALF), BF)],
         compiler_params=params(16),
         name="near",
-    )(pos, metas, b_own, b_other, *near)
+    )(metas, b_own, b_other, *near)
     out = pl.pallas_call(
         far_kernel,
         out_shape=shape(BLK, BS),
-        in_specs=[SM] + [VM] * (5 + len(far)),
+        in_specs=[VM] * (5 + len(far)),
         out_specs=VM,
         scratch_shapes=[pltpu.VMEM((ROWS * BS, 4 * CG * BS), BF), pltpu.VMEM((4 * CG * BS, CG * BS), BF)],
         compiler_params=params(16),
         name="far",
-    )(pos, metas, b_own, b_other, acc, square, *far)
+    )(metas, b_own, b_other, acc, square, *far)
     return out.reshape(ROWS, KD, BS, BS)
 
 

time: 156 us -> 153 us (0.981)
  the two profiles are of different devices: /device:TPU:16 before, /device:TPU:8 now
where the time goes in v5:
time: 153 us; the launch traced here: 152 us
  starting transfers between devices  61.5 us (40%)
  waiting for transfers between devices  56.6 us (37%)
  Pallas kernels  17.3 us (11%)
  between operations  13.8 us (9%)
  local copies, waits for them, and re-layouts  2.56 us (2%)
    ppermute x12, starting transfers between devices, both_axes(): return lax.ppermute(a, ('row', 'col'), perm)  35.7 us
    ppermute x12, waiting for transfers between devices, both_axes(): return lax.ppermute(a, ('row', 'col'), perm)  29.5 us
    ppermute x6, starting transfers between devices, col(): return lax.ppermute(a, 'col', perm)  17.7 us
    ppermute x6, waiting for transfers between devices, col(): return lax.ppermute(a, 'col', perm)  13.2 us
    ppermute x2, waiting for transfers between devices, row(): return lax.ppermute(a, 'row', perm)  12 us
    ppermute x2, starting transfers between devices, row(): return lax.ppermute(a, 'row', perm)  8.11 us
    pallas_call x1, Pallas kernels, local(): pl.pallas_call(strip_kernel, out_shape=[shape(ROWS * BS, 2 * HALF), shape...  4.97 us
    pallas_call x1, Pallas kernels, local(): pl.pallas_call(own_half_kernel, out_shape=[acc_shape, b_shape], in_specs=...  4.68 us
  transfers between devices with their start and end apart: 21, of which 15 were waited for; matrix products, arithmetic and copies ran while one was open for 0% of the time, Pallas kernels for 8%

profile of v5, /device:TPU:8, one launch (start us, length us, event | category | flops | bytes accessed | tf_op | source)
XLA Modules:
  0.0 152.5 jit_solution(13311040068455463746)
XLA Ops:
  8.4 3.5 %collective-permute-start = (bf16[784,128]{1,0:T(8,128)(2,1)S(1)}, bf16[784,128]{1,0:T(8,128)(2,1)S(1)}, u32[]{:S(2)}, u32[]{:S(2)}) collective-permute-start(bf16[784,128]{1,0:T(8,128)(2,1)S(1)} %cat.6.refs_0_), channel_id=1, source_target_pairs={{0,1},{1,2},{2,3},{3,0},{4,5},{5,6},{6,7},{7,4},{8,9},{9,10},{10,1... | collective-permute-start | bytes 602120 | tf_op jit(solution)/shard_map/ppermute | solution.py:41
  11.9 5.9 %collective-permute-start.1 = (bf16[784,128]{1,0:T(8,128)(2,1)S(1)}, bf16[784,128]{1,0:T(8,128)(2,1)S(1)}, u32[]{:S(2)}, u32[]{:S(2)}) collective-permute-start(bf16[784,128]{1,0:T(8,128)(2,1)S(1)} %cat.6.refs_0_), channel_id=1, source_target_pairs={{0,32},{16,48},{32,0},{48,16},{64,96},{80,112},{96,64},{112,80},{1... | collective-permute-start | bytes 602120 | tf_op jit(solution)/shard_map/ppermute | solution.py:49
  17.8 3.1 %collective-permute-done.refs_1_ = bf16[784,128]{1,0:T(8,128)(2,1)S(1)} collective-permute-done((bf16[784,128]{1,0:T(8,128)(2,1)S(1)}, bf16[784,128]{1,0:T(8,128)(2,1)S(1)}, u32[]{:S(2)}, u32[]{:S(2)}) %collective-permute-start) | collective-permute-done | bytes 200736 | tf_op jit(solution)/shard_map/ppermute | solution.py:41
  21.0 10.7 %collective-permute-done.1.refs_1_ = bf16[784,128]{1,0:T(8,128)(2,1)S(1)} collective-permute-done((bf16[784,128]{1,0:T(8,128)(2,1)S(1)}, bf16[784,128]{1,0:T(8,128)(2,1)S(1)}, u32[]{:S(2)}, u32[]{:S(2)}) %collective-permute-start.1) | collective-permute-done | bytes 200736 | tf_op jit(solution)/shard_map/ppermute | solution.py:49
  36.6 5.1 %collective-permute-start.5 = (bf16[1568,128]{1,0:T(8,128)(2,1)S(1)}, bf16[1568,128]{1,0:T(8,128)(2,1)S(1)}, u32[]{:S(2)}, u32[]{:S(2)}) collective-permute-start(bf16[1568,128]{1,0:T(8,128)(2,1)S(1)} %cat.7.refs_0_), channel_id=1, source_target_pairs={{0,12},{1,13},{2,14},{3,15},{4,0},{5,1},{6,2},{7,3},{8,4},{9,5},{1... | collective-permute-start | bytes 1204232 | tf_op jit(solution)/shard_map/ppermute | solution.py:45
  44.6 2.4 %collective-permute-done.2.refs_0_ = bf16[784,128]{1,0:T(8,128)(2,1)S(1)} collective-permute-done((bf16[784,128]{1,0:T(8,128)(2,1)S(1)}, bf16[784,128]{1,0:T(8,128)(2,1)S(1)}, u32[]{:S(2)}, u32[]{:S(2)}) %collective-permute-start.2) | collective-permute-done | bytes 200736 | tf_op jit(solution)/shard_map/ppermute | solution.py:41
  47.7 4.8 %collective-permute-start.7 = (bf16[1568,128]{1,0:T(8,128)(2,1)S(1)}, bf16[1568,128]{1,0:T(8,128)(2,1)S(1)}, u32[]{:S(2)}, u32[]{:S(2)}) collective-permute-start(bf16[1568,128]{1,0:T(8,128)(2,1)S(1)} %cat.9.refs_3_), channel_id=1, source_target_pairs={{0,12},{1,13},{2,14},{3,15},{4,0},{5,1},{6,2},{7,3},{8,4},{9,5},{1... | collective-permute-start | bytes 1204232 | tf_op jit(solution)/shard_map/ppermute | solution.py:45
  54.5 2.7 %collective-permute-start.8 = (bf16[1568,128]{1,0:T(8,128)(2,1)S(1)}, bf16[1568,128]{1,0:T(8,128)(2,1)S(1)}, u32[]{:S(2)}, u32[]{:S(2)}) collective-permute-start(bf16[1568,128]{1,0:T(8,128)(2,1)S(1)} %collective-permute-done.4.refs_1_), channel_id=1, source_target_pairs={{0,4},{1,5},{2,6},{3,7},{4,8},{5,9},{6,10},{7,11},{8,12},{9,13},{1... | collective-permute-start | bytes 1204232 | tf_op jit(solution)/shard_map/ppermute | solution.py:45
  57.2 4.3 %collective-permute-done.7.refs_5_ = bf16[1568,128]{1,0:T(8,128)(2,1)S(1)} collective-permute-done((bf16[1568,128]{1,0:T(8,128)(2,1)S(1)}, bf16[1568,128]{1,0:T(8,128)(2,1)S(1)}, u32[]{:S(2)}, u32[]{:S(2)}) %collective-permute-start.7) | collective-permute-done | bytes 401440 | tf_op jit(solution)/shard_map/ppermute | solution.py:45
  65.4 2.4 %collective-permute-done.8.refs_6_ = bf16[1568,128]{1,0:T(8,128)(2,1)S(1)} collective-permute-done((bf16[1568,128]{1,0:T(8,128)(2,1)S(1)}, bf16[1568,128]{1,0:T(8,128)(2,1)S(1)}, u32[]{:S(2)}, u32[]{:S(2)}) %collective-permute-start.8) | collective-permute-done | bytes 401440 | tf_op jit(solution)/shard_map/ppermute | solution.py:45
  67.8 6.7 %collective-permute-done.9.refs_7_ = bf16[1568,128]{1,0:T(8,128)(2,1)S(1)} collective-permute-done((bf16[1568,128]{1,0:T(8,128)(2,1)S(1)}, bf16[1568,128]{1,0:T(8,128)(2,1)S(1)}, u32[]{:S(2)}, u32[]{:S(2)}) %collective-permute-start.9) | collective-permute-done | bytes 401440 | tf_op jit(solution)/shard_map/ppermute | solution.py:45
  75.3 5.0 %strips.1 = (bf16[256,8192]{1,0:T(8,128)(2,1)}, bf16[256,128]{1,0:T(8,128)(2,1)}) custom-call(f32[8,128]{1,0:T(8,128)} %copy-done.6, bf16[1568,128]{1,0:T(8,128)(2,1)} %copy-done.2, bf16[1568,128]{1,0:T(8,128)(2,1)} %copy-done.8, bf16[1568,128]{1,0:T(8,128)(2,1)} %copy-done.7, bf16[1568,128]{1,0:T(8,128)(2,1)} %copy-done.3, bf16[1568,128]{1,0:T(8,128)(2,1)} %copy-done.10, ...), custom_call_target="tpu_custom_call" | custom-call | tf_op jit(solution)/shard_map/strips/pallas_call | solution.py:304
  82.2 2.2 %collective-permute-start.10 = (bf16[12544,128]{1,0:T(8,128)(2,1)}, bf16[12544,128]{1,0:T(8,128)(2,1)S(1)}, u32[]{:S(2)}, u32[]{:S(2)}) collective-permute-start(bf16[12544,128]{1,0:T(8,128)(2,1)} %all-gather.2.cloned.1.call-done.v_in), channel_id=1, source_target_pairs={{0,16},{16,0},{32,48},{48,32},{64,80},{80,64},{96,112},{112,96},{1... | collective-permute-start | bytes 9633800 | tf_op jit(solution)/shard_map/ppermute | solution.py:49
  84.3 4.7 %own_half.1 = (f32[256,512]{1,0:T(8,128)S(1)}, bf16[4096,512]{1,0:T(8,128)(2,1)}) custom-call(bf16[256,8192]{1,0:T(8,128)(2,1)} %get-tuple-element.62.a_in.a_ref, bf16[12544,128]{1,0:T(8,128)(2,1)} %all-gather.2.cloned.1.call-done.v_in), custom_call_target="tpu_custom_call" | custom-call | tf_op jit(solution)/shard_map/own_half/pallas_call | solution.py:315
  92.3 3.4 %collective-permute-start.11 = (bf16[768,128]{1,0:T(8,128)(2,1)S(1)}, bf16[768,128]{1,0:T(8,128)(2,1)S(1)}, u32[]{:S(2)}, u32[]{:S(2)}) collective-permute-start(bf16[768,128]{1,0:T(8,128)(2,1)S(1)} %get-tuple-element.67.refs_0_), channel_id=1, source_target_pairs={{0,1},{1,2},{2,3},{3,0},{4,5},{5,6},{6,7},{7,4},{8,9},{9,10},{10,1... | collective-permute-start | bytes 589832 | tf_op jit(solution)/shard_map/ppermute | solution.py:41
  95.7 3.3 %collective-permute-start.15 = (bf16[768,128]{1,0:T(8,128)(2,1)S(1)}, bf16[768,128]{1,0:T(8,128)(2,1)S(1)}, u32[]{:S(2)}, u32[]{:S(2)}) collective-permute-start(bf16[768,128]{1,0:T(8,128)(2,1)S(1)} %get-tuple-element.67.refs_0_), channel_id=1, source_target_pairs={{0,2},{1,3},{2,0},{3,1},{4,6},{5,7},{6,4},{7,5},{8,10},{9,11},{10,... | collective-permute-start | bytes 589832 | tf_op jit(solution)/shard_map/ppermute | solution.py:41
  99.1 3.4 %collective-permute-start.14 = (bf16[768,128]{1,0:T(8,128)(2,1)S(1)}, bf16[768,128]{1,0:T(8,128)(2,1)S(1)}, u32[]{:S(2)}, u32[]{:S(2)}) collective-permute-start(bf16[768,128]{1,0:T(8,128)(2,1)S(1)} %get-tuple-element.67.refs_0_), channel_id=1, source_target_pairs={{0,3},{1,0},{2,1},{3,2},{4,7},{5,4},{6,5},{7,6},{8,11},{9,8},{10,9... | collective-permute-start | bytes 589832 | tf_op jit(solution)/shard_map/ppermute | solution.py:41
  102.5 6.7 %collective-permute-done.11.refs_1_ = bf16[768,128]{1,0:T(8,128)(2,1)S(1)} collective-permute-done((bf16[768,128]{1,0:T(8,128)(2,1)S(1)}, bf16[768,128]{1,0:T(8,128)(2,1)S(1)}, u32[]{:S(2)}, u32[]{:S(2)}) %collective-permute-start.11) | collective-permute-done | bytes 196640 | tf_op jit(solution)/shard_map/ppermute | solution.py:41
  109.3 4.6 %collective-permute-start.13 = (bf16[1536,128]{1,0:T(8,128)(2,1)S(1)}, bf16[1536,128]{1,0:T(8,128)(2,1)S(1)}, u32[]{:S(2)}, u32[]{:S(2)}) collective-permute-start(bf16[1536,128]{1,0:T(8,128)(2,1)S(1)} %cat.10.refs_0_), channel_id=1, source_target_pairs={{0,12},{1,13},{2,14},{3,15},{4,0},{5,1},{6,2},{7,3},{8,4},{9,5},{1... | collective-permute-start | bytes 1179656 | tf_op jit(solution)/shard_map/ppermute | solution.py:45
  115.9 5.1 %collective-permute-start.17 = (bf16[1536,128]{1,0:T(8,128)(2,1)S(1)}, bf16[1536,128]{1,0:T(8,128)(2,1)S(1)}, u32[]{:S(2)}, u32[]{:S(2)}) collective-permute-start(bf16[1536,128]{1,0:T(8,128)(2,1)S(1)} %cat.11.refs_3_), channel_id=1, source_target_pairs={{0,12},{1,13},{2,14},{3,15},{4,0},{5,1},{6,2},{7,3},{8,4},{9,5},{1... | collective-permute-start | bytes 1179656 | tf_op jit(solution)/shard_map/ppermute | solution.py:45
  123.0 5.9 %collective-permute-done.12.refs_1_ = bf16[1536,128]{1,0:T(8,128)(2,1)S(1)} collective-permute-done((bf16[1536,128]{1,0:T(8,128)(2,1)S(1)}, bf16[1536,128]{1,0:T(8,128)(2,1)S(1)}, u32[]{:S(2)}, u32[]{:S(2)}) %collective-permute-start.12) | collective-permute-done | bytes 393248 | tf_op jit(solution)/shard_map/ppermute | solution.py:45
  130.8 2.3 %collective-permute-done.16.refs_4_ = bf16[1536,128]{1,0:T(8,128)(2,1)S(1)} collective-permute-done((bf16[1536,128]{1,0:T(8,128)(2,1)S(1)}, bf16[1536,128]{1,0:T(8,128)(2,1)S(1)}, u32[]{:S(2)}, u32[]{:S(2)}) %collective-permute-start.16) | collective-permute-done | bytes 393248 | tf_op jit(solution)/shard_map/ppermute | solution.py:45
  135.1 3.0 %near.1.acc_ref = f32[256,512]{1,0:T(8,128)S(1)} custom-call(bf16[256,128]{1,0:T(8,128)(2,1)S(1)} %copy-done.4, bf16[4096,512]{1,0:T(8,128)(2,1)S(1)} %copy-done.1, bf16[4096,512]{1,0:T(8,128)(2,1)S(1)} %get-tuple-element.66.b_other, bf16[1536,128]{1,0:T(8,128)(2,1)S(1)} %cat.10.refs_0_, bf16[1536,128]{1,0:T(8,128)(2,1)S(1)} %collective-permute-done.12.refs_1_, ...), custom_call_target="tpu_custom_call" | custom-call | tf_op jit(solution)/shard_map/near/pallas_call | solution.py:339
  139.8 4.2 %collective-permute-done.19.refs_1_ = bf16[1536,128]{1,0:T(8,128)(2,1)S(1)} collective-permute-done((bf16[1536,128]{1,0:T(8,128)(2,1)S(1)}, bf16[1536,128]{1,0:T(8,128)(2,1)S(1)}, u32[]{:S(2)}, u32[]{:S(2)}) %collective-permute-start.19) | collective-permute-done | bytes 393248 | tf_op jit(solution)/shard_map/ppermute | solution.py:45
  (64 shorter events, 33.3 us)
Async XLA Ops:
  6.5 75.6 %all-gather.2.cloned.1.call-start = ((), (), s32[]{:S(2)}) async-start(), calls=%async_computation | async-start | bytes 3612672 | tf_op jit(solution)/shard_map/all_gather | solution.py:114
  8.4 12.5 %collective-permute-start = (bf16[784,128]{1,0:T(8,128)(2,1)S(1)}, bf16[784,128]{1,0:T(8,128)(2,1)S(1)}, u32[]{:S(2)}, u32[]{:S(2)}) collective-permute-start(bf16[784,128]{1,0:T(8,128)(2,1)S(1)} %cat.6.refs_0_), channel_id=1, source_target_pairs={{0,1},{1,2},{2,3},{3,0},{4,5},{5,6},{6,7},{7,4},{8,9},{9,10},{10,1... | collective-permute-start | bytes 602120 | tf_op jit(solution)/shard_map/ppermute | solution.py:41
  11.9 19.8 %collective-permute-start.1 = (bf16[784,128]{1,0:T(8,128)(2,1)S(1)}, bf16[784,128]{1,0:T(8,128)(2,1)S(1)}, u32[]{:S(2)}, u32[]{:S(2)}) collective-permute-start(bf16[784,128]{1,0:T(8,128)(2,1)S(1)} %cat.6.refs_0_), channel_id=1, source_target_pairs={{0,32},{16,48},{32,0},{48,16},{64,96},{80,112},{96,64},{112,80},{1... | collective-permute-start | bytes 602120 | tf_op jit(solution)/shard_map/ppermute | solution.py:49
  20.9 20.8 %copy-start.2 = (bf16[1568,128]{1,0:T(8,128)(2,1)}, bf16[1568,128]{1,0:T(8,128)(2,1)S(1)}, u32[]{:S(2)}) copy-start(bf16[1568,128]{1,0:T(8,128)(2,1)S(1)} %cat.7.refs_0_) | copy-start | bytes 1204228
  32.5 12.1 %collective-permute-start.3 = (bf16[784,128]{1,0:T(8,128)(2,1)S(1)}, bf16[784,128]{1,0:T(8,128)(2,1)S(1)}, u32[]{:S(2)}, u32[]{:S(2)}) collective-permute-start(bf16[784,128]{1,0:T(8,128)(2,1)S(1)} %cat.6.refs_0_), channel_id=1, source_target_pairs={{0,2},{1,3},{2,0},{3,1},{4,6},{5,7},{6,4},{7,5},{8,10},{9,11},{10,... | collective-permute-start | bytes 602120 | tf_op jit(solution)/shard_map/ppermute | solution.py:41
  34.6 12.4 %collective-permute-start.2 = (bf16[784,128]{1,0:T(8,128)(2,1)S(1)}, bf16[784,128]{1,0:T(8,128)(2,1)S(1)}, u32[]{:S(2)}, u32[]{:S(2)}) collective-permute-start(bf16[784,128]{1,0:T(8,128)(2,1)S(1)} %cat.6.refs_0_), channel_id=1, source_target_pairs={{0,3},{1,0},{2,1},{3,2},{4,7},{5,4},{6,5},{7,6},{8,11},{9,8},{10,9... | collective-permute-start | bytes 602120 | tf_op jit(solution)/shard_map/ppermute | solution.py:41
  36.6 17.9 %collective-permute-start.5 = (bf16[1568,128]{1,0:T(8,128)(2,1)S(1)}, bf16[1568,128]{1,0:T(8,128)(2,1)S(1)}, u32[]{:S(2)}, u32[]{:S(2)}) collective-permute-start(bf16[1568,128]{1,0:T(8,128)(2,1)S(1)} %cat.7.refs_0_), channel_id=1, source_target_pairs={{0,12},{1,13},{2,14},{3,15},{4,0},{5,1},{6,2},{7,3},{8,4},{9,5},{1... | collective-permute-start | bytes 1204232 | tf_op jit(solution)/shard_map/ppermute | solution.py:45
  41.7 12.8 %collective-permute-start.4 = (bf16[1568,128]{1,0:T(8,128)(2,1)S(1)}, bf16[1568,128]{1,0:T(8,128)(2,1)S(1)}, u32[]{:S(2)}, u32[]{:S(2)}) collective-permute-start(bf16[1568,128]{1,0:T(8,128)(2,1)S(1)} %cat.7.refs_0_), channel_id=1, source_target_pairs={{0,4},{1,5},{2,6},{3,7},{4,8},{5,9},{6,10},{7,11},{8,12},{9,13},{1... | collective-permute-start | bytes 1204232 | tf_op jit(solution)/shard_map/ppermute | solution.py:45
  47.7 13.7 %collective-permute-start.7 = (bf16[1568,128]{1,0:T(8,128)(2,1)S(1)}, bf16[1568,128]{1,0:T(8,128)(2,1)S(1)}, u32[]{:S(2)}, u32[]{:S(2)}) collective-permute-start(bf16[1568,128]{1,0:T(8,128)(2,1)S(1)} %cat.9.refs_3_), channel_id=1, source_target_pairs={{0,12},{1,13},{2,14},{3,15},{4,0},{5,1},{6,2},{7,3},{8,4},{9,5},{1... | collective-permute-start | bytes 1204232 | tf_op jit(solution)/shard_map/ppermute | solution.py:45
  52.5 11.0 %collective-permute-start.6 = (bf16[1568,128]{1,0:T(8,128)(2,1)S(1)}, bf16[1568,128]{1,0:T(8,128)(2,1)S(1)}, u32[]{:S(2)}, u32[]{:S(2)}) collective-permute-start(bf16[1568,128]{1,0:T(8,128)(2,1)S(1)} %cat.9.refs_3_), channel_id=1, source_target_pairs={{0,4},{1,5},{2,6},{3,7},{4,8},{5,9},{6,10},{7,11},{8,12},{9,13},{1... | collective-permute-start | bytes 1204232 | tf_op jit(solution)/shard_map/ppermute | solution.py:45
  54.5 20.0 %copy-start.7 = (bf16[1568,128]{1,0:T(8,128)(2,1)}, bf16[1568,128]{1,0:T(8,128)(2,1)S(1)}, u32[]{:S(2)}) copy-start(bf16[1568,128]{1,0:T(8,128)(2,1)S(1)} %collective-permute-done.5.refs_2_) | copy-start | bytes 1204228
  54.5 13.3 %collective-permute-start.8 = (bf16[1568,128]{1,0:T(8,128)(2,1)S(1)}, bf16[1568,128]{1,0:T(8,128)(2,1)S(1)}, u32[]{:S(2)}, u32[]{:S(2)}) collective-permute-start(bf16[1568,128]{1,0:T(8,128)(2,1)S(1)} %collective-permute-done.4.refs_1_), channel_id=1, source_target_pairs={{0,4},{1,5},{2,6},{3,7},{4,8},{5,9},{6,10},{7,11},{8,12},{9,13},{1... | collective-permute-start | bytes 1204232 | tf_op jit(solution)/shard_map/ppermute | solution.py:45
  63.5 11.0 %collective-permute-start.9 = (bf16[1568,128]{1,0:T(8,128)(2,1)S(1)}, bf16[1568,128]{1,0:T(8,128)(2,1)S(1)}, u32[]{:S(2)}, u32[]{:S(2)}) collective-permute-start(bf16[1568,128]{1,0:T(8,128)(2,1)S(1)} %collective-permute-done.6.refs_4_), channel_id=1, source_target_pairs={{0,4},{1,5},{2,6},{3,7},{4,8},{5,9},{6,10},{7,11},{8,12},{9,13},{1... | collective-permute-start | bytes 1204232 | tf_op jit(solution)/shard_map/ppermute | solution.py:45
  82.2 8.1 %collective-permute-start.10 = (bf16[12544,128]{1,0:T(8,128)(2,1)}, bf16[12544,128]{1,0:T(8,128)(2,1)S(1)}, u32[]{:S(2)}, u32[]{:S(2)}) collective-permute-start(bf16[12544,128]{1,0:T(8,128)(2,1)} %all-gather.2.cloned.1.call-done.v_in), channel_id=1, source_target_pairs={{0,16},{16,0},{32,48},{48,32},{64,80},{80,64},{96,112},{112,96},{1... | collective-permute-start | bytes 9633800 | tf_op jit(solution)/shard_map/ppermute | solution.py:49
  90.3 44.8 %copy-start.1 = (bf16[4096,512]{1,0:T(8,128)(2,1)S(1)}, bf16[4096,512]{1,0:T(8,128)(2,1)}, u32[]{:S(2)}) copy-start(bf16[4096,512]{1,0:T(8,128)(2,1)} %get-tuple-element.64.b_own) | copy-start | bytes 12582916
  92.3 16.9 %collective-permute-start.11 = (bf16[768,128]{1,0:T(8,128)(2,1)S(1)}, bf16[768,128]{1,0:T(8,128)(2,1)S(1)}, u32[]{:S(2)}, u32[]{:S(2)}) collective-permute-start(bf16[768,128]{1,0:T(8,128)(2,1)S(1)} %get-tuple-element.67.refs_0_), channel_id=1, source_target_pairs={{0,1},{1,2},{2,3},{3,0},{4,5},{5,6},{6,7},{7,4},{8,9},{9,10},{10,1... | collective-permute-start | bytes 589832 | tf_op jit(solution)/shard_map/ppermute | solution.py:41
  95.7 20.1 %collective-permute-start.15 = (bf16[768,128]{1,0:T(8,128)(2,1)S(1)}, bf16[768,128]{1,0:T(8,128)(2,1)S(1)}, u32[]{:S(2)}, u32[]{:S(2)}) collective-permute-start(bf16[768,128]{1,0:T(8,128)(2,1)S(1)} %get-tuple-element.67.refs_0_), channel_id=1, source_target_pairs={{0,2},{1,3},{2,0},{3,1},{4,6},{5,7},{6,4},{7,5},{8,10},{9,11},{10,... | collective-permute-start | bytes 589832 | tf_op jit(solution)/shard_map/ppermute | solution.py:41
  99.1 16.8 %collective-permute-start.14 = (bf16[768,128]{1,0:T(8,128)(2,1)S(1)}, bf16[768,128]{1,0:T(8,128)(2,1)S(1)}, u32[]{:S(2)}, u32[]{:S(2)}) collective-permute-start(bf16[768,128]{1,0:T(8,128)(2,1)S(1)} %get-tuple-element.67.refs_0_), channel_id=1, source_target_pairs={{0,3},{1,0},{2,1},{3,2},{4,7},{5,4},{6,5},{7,6},{8,11},{9,8},{10,9... | collective-permute-start | bytes 589832 | tf_op jit(solution)/shard_map/ppermute | solution.py:41
  109.3 13.7 %collective-permute-start.13 = (bf16[1536,128]{1,0:T(8,128)(2,1)S(1)}, bf16[1536,128]{1,0:T(8,128)(2,1)S(1)}, u32[]{:S(2)}, u32[]{:S(2)}) collective-permute-start(bf16[1536,128]{1,0:T(8,128)(2,1)S(1)} %cat.10.refs_0_), channel_id=1, source_target_pairs={{0,12},{1,13},{2,14},{3,15},{4,0},{5,1},{6,2},{7,3},{8,4},{9,5},{1... | collective-permute-start | bytes 1179656 | tf_op jit(solution)/shard_map/ppermute | solution.py:45
  113.9 15.0 %collective-permute-start.12 = (bf16[1536,128]{1,0:T(8,128)(2,1)S(1)}, bf16[1536,128]{1,0:T(8,128)(2,1)S(1)}, u32[]{:S(2)}, u32[]{:S(2)}) collective-permute-start(bf16[1536,128]{1,0:T(8,128)(2,1)S(1)} %cat.10.refs_0_), channel_id=1, source_target_pairs={{0,4},{1,5},{2,6},{3,7},{4,8},{5,9},{6,10},{7,11},{8,12},{9,13},{1... | collective-permute-start | bytes 1179656 | tf_op jit(solution)/shard_map/ppermute | solution.py:45
  115.9 14.9 %collective-permute-start.17 = (bf16[1536,128]{1,0:T(8,128)(2,1)S(1)}, bf16[1536,128]{1,0:T(8,128)(2,1)S(1)}, u32[]{:S(2)}, u32[]{:S(2)}) collective-permute-start(bf16[1536,128]{1,0:T(8,128)(2,1)S(1)} %cat.11.refs_3_), channel_id=1, source_target_pairs={{0,12},{1,13},{2,14},{3,15},{4,0},{5,1},{6,2},{7,3},{8,4},{9,5},{1... | collective-permute-start | bytes 1179656 | tf_op jit(solution)/shard_map/ppermute | solution.py:45
  121.0 12.1 %collective-permute-start.16 = (bf16[1536,128]{1,0:T(8,128)(2,1)S(1)}, bf16[1536,128]{1,0:T(8,128)(2,1)S(1)}, u32[]{:S(2)}, u32[]{:S(2)}) collective-permute-start(bf16[1536,128]{1,0:T(8,128)(2,1)S(1)} %cat.11.refs_3_), channel_id=1, source_target_pairs={{0,4},{1,5},{2,6},{3,7},{4,8},{5,9},{6,10},{7,11},{8,12},{9,13},{1... | collective-permute-start | bytes 1179656 | tf_op jit(solution)/shard_map/ppermute | solution.py:45
  128.9 10.9 %collective-permute-start.18 = (bf16[1536,128]{1,0:T(8,128)(2,1)S(1)}, bf16[1536,128]{1,0:T(8,128)(2,1)S(1)}, u32[]{:S(2)}, u32[]{:S(2)}) collective-permute-start(bf16[1536,128]{1,0:T(8,128)(2,1)S(1)} %collective-permute-done.12.refs_1_), channel_id=1, source_target_pairs={{0,4},{1,5},{2,6},{3,7},{4,8},{5,9},{6,10},{7,11},{8,12},{9,13},{1... | collective-permute-start | bytes 1179656 | tf_op jit(solution)/shard_map/ppermute | solution.py:45
  133.1 10.9 %collective-permute-start.19 = (bf16[1536,128]{1,0:T(8,128)(2,1)S(1)}, bf16[1536,128]{1,0:T(8,128)(2,1)S(1)}, u32[]{:S(2)}, u32[]{:S(2)}) collective-permute-start(bf16[1536,128]{1,0:T(8,128)(2,1)S(1)} %collective-permute-done.16.refs_4_), channel_id=1, source_target_pairs={{0,4},{1,5},{2,6},{3,7},{4,8},{5,9},{6,10},{7,11},{8,12},{9,13},{1... | collective-permute-start | bytes 1179656 | tf_op jit(solution)/shard_map/ppermute | solution.py:45
  (10 other events, 76.6 us)
Sparse Core Ops, SparseCore 0:
  32.6 49.4 all-gather.1

commit v6 on v5

--- a/solution.py
+++ b/solution.py
@@ -127,7 +127,6 @@
     two = cat(line3, line2)
     ahead2, back2 = both_axes(two, AHEAD), both_axes(two, BACK)
     ahead1, back1 = lax.optimization_barrier((ahead1, back1))
-    ahead2, back2 = lax.optimization_barrier((ahead2, back2))
     far = [both_axes(ahead1, AHEAD), both_axes(ahead2, AHEAD)]
     return [one, ahead1, back1, two, ahead2, back2], far
 

time: 153 us -> 154 us (level)
  the two profiles are of different devices: /device:TPU:8 before, /device:TPU:16 now
where the time goes in v6:
time: 154 us
  starting transfers between devices  64.5 us (42%)
  waiting for transfers between devices  54.7 us (36%)
  Pallas kernels  17.3 us (11%)
  between operations  13.8 us (9%)
  local copies, waits for them, and re-layouts  2.56 us (2%)
    ppermute x12, starting transfers between devices, both_axes(): return lax.ppermute(a, ('row', 'col'), perm)  34.4 us
    ppermute x12, waiting for transfers between devices, both_axes(): return lax.ppermute(a, ('row', 'col'), perm)  30.6 us
    ppermute x6, starting transfers between devices, col(): return lax.ppermute(a, 'col', perm)  22.9 us
    ppermute x6, waiting for transfers between devices, col(): return lax.ppermute(a, 'col', perm)  10.5 us
    ppermute x2, waiting for transfers between devices, row(): return lax.ppermute(a, 'row', perm)  10.1 us
    ppermute x2, starting transfers between devices, row(): return lax.ppermute(a, 'row', perm)  7.21 us
    pallas_call x1, Pallas kernels, local(): pl.pallas_call(strip_kernel, out_shape=[shape(ROWS * BS, 2 * HALF), shape...  4.97 us
    pallas_call x1, Pallas kernels, local(): pl.pallas_call(own_half_kernel, out_shape=[acc_shape, b_shape], in_specs=...  4.68 us
  transfers between devices with their start and end apart: 21, of which 15 were waited for; matrix products, arithmetic and copies ran while one was open for 0% of the time, Pallas kernels for 8%

profile of v6, /device:TPU:16, one launch (start us, length us, event | category | flops | bytes accessed | tf_op | source)
XLA Modules:
  0.0 153.6 jit_solution(10825082468328998407)
XLA Ops:
  8.4 3.5 %collective-permute-start = (bf16[784,128]{1,0:T(8,128)(2,1)S(1)}, bf16[784,128]{1,0:T(8,128)(2,1)S(1)}, u32[]{:S(2)}, u32[]{:S(2)}) collective-permute-start(bf16[784,128]{1,0:T(8,128)(2,1)S(1)} %cat.6.refs_0_), channel_id=1, source_target_pairs={{0,1},{1,2},{2,3},{3,0},{4,5},{5,6},{6,7},{7,4},{8,9},{9,10},{10,1... | collective-permute-start | bytes 602120 | tf_op jit(solution)/shard_map/ppermute | solution.py:41
  11.9 5.0 %collective-permute-start.1 = (bf16[784,128]{1,0:T(8,128)(2,1)S(1)}, bf16[784,128]{1,0:T(8,128)(2,1)S(1)}, u32[]{:S(2)}, u32[]{:S(2)}) collective-permute-start(bf16[784,128]{1,0:T(8,128)(2,1)S(1)} %cat.6.refs_0_), channel_id=1, source_target_pairs={{0,32},{16,48},{32,0},{48,16},{64,96},{80,112},{96,64},{112,80},{1... | collective-permute-start | bytes 602120 | tf_op jit(solution)/shard_map/ppermute | solution.py:49
  17.1 8.8 %collective-permute-done.1.refs_1_ = bf16[784,128]{1,0:T(8,128)(2,1)S(1)} collective-permute-done((bf16[784,128]{1,0:T(8,128)(2,1)S(1)}, bf16[784,128]{1,0:T(8,128)(2,1)S(1)}, u32[]{:S(2)}, u32[]{:S(2)}) %collective-permute-start.1) | collective-permute-done | bytes 200736 | tf_op jit(solution)/shard_map/ppermute | solution.py:49
  26.7 6.4 %collective-permute-start.3 = (bf16[784,128]{1,0:T(8,128)(2,1)S(1)}, bf16[784,128]{1,0:T(8,128)(2,1)S(1)}, u32[]{:S(2)}, u32[]{:S(2)}) collective-permute-start(bf16[784,128]{1,0:T(8,128)(2,1)S(1)} %cat.6.refs_0_), channel_id=1, source_target_pairs={{0,2},{1,3},{2,0},{3,1},{4,6},{5,7},{6,4},{7,5},{8,10},{9,11},{10,... | collective-permute-start | bytes 602120 | tf_op jit(solution)/shard_map/ppermute | solution.py:41
  33.2 3.8 %collective-permute-start.2 = (bf16[784,128]{1,0:T(8,128)(2,1)S(1)}, bf16[784,128]{1,0:T(8,128)(2,1)S(1)}, u32[]{:S(2)}, u32[]{:S(2)}) collective-permute-start(bf16[784,128]{1,0:T(8,128)(2,1)S(1)} %cat.6.refs_0_), channel_id=1, source_target_pairs={{0,3},{1,0},{2,1},{3,2},{4,7},{5,4},{6,5},{7,6},{8,11},{9,8},{10,9... | collective-permute-start | bytes 602120 | tf_op jit(solution)/shard_map/ppermute | solution.py:41
  37.0 5.1 %collective-permute-start.5 = (bf16[1568,128]{1,0:T(8,128)(2,1)S(1)}, bf16[1568,128]{1,0:T(8,128)(2,1)S(1)}, u32[]{:S(2)}, u32[]{:S(2)}) collective-permute-start(bf16[1568,128]{1,0:T(8,128)(2,1)S(1)} %cat.7.refs_0_), channel_id=1, source_target_pairs={{0,12},{1,13},{2,14},{3,15},{4,0},{5,1},{6,2},{7,3},{8,4},{9,5},{1... | collective-permute-start | bytes 1204232 | tf_op jit(solution)/shard_map/ppermute | solution.py:45
  46.2 4.3 %collective-permute-start.7 = (bf16[1568,128]{1,0:T(8,128)(2,1)S(1)}, bf16[1568,128]{1,0:T(8,128)(2,1)S(1)}, u32[]{:S(2)}, u32[]{:S(2)}) collective-permute-start(bf16[1568,128]{1,0:T(8,128)(2,1)S(1)} %cat.9.refs_3_), channel_id=1, source_target_pairs={{0,12},{1,13},{2,14},{3,15},{4,0},{5,1},{6,2},{7,3},{8,4},{9,5},{1... | collective-permute-start | bytes 1204232 | tf_op jit(solution)/shard_map/ppermute | solution.py:45
  52.5 2.5 %collective-permute-done.4.refs_1_ = bf16[1568,128]{1,0:T(8,128)(2,1)S(1)} collective-permute-done((bf16[1568,128]{1,0:T(8,128)(2,1)S(1)}, bf16[1568,128]{1,0:T(8,128)(2,1)S(1)}, u32[]{:S(2)}, u32[]{:S(2)}) %collective-permute-start.4) | collective-permute-done | bytes 401440 | tf_op jit(solution)/shard_map/ppermute | solution.py:45
  56.9 3.2 %collective-permute-done.7.refs_5_ = bf16[1568,128]{1,0:T(8,128)(2,1)S(1)} collective-permute-done((bf16[1568,128]{1,0:T(8,128)(2,1)S(1)}, bf16[1568,128]{1,0:T(8,128)(2,1)S(1)}, u32[]{:S(2)}, u32[]{:S(2)}) %collective-permute-start.7) | collective-permute-done | bytes 401440 | tf_op jit(solution)/shard_map/ppermute | solution.py:45
  66.0 6.7 %collective-permute-done.9.refs_7_ = bf16[1568,128]{1,0:T(8,128)(2,1)S(1)} collective-permute-done((bf16[1568,128]{1,0:T(8,128)(2,1)S(1)}, bf16[1568,128]{1,0:T(8,128)(2,1)S(1)}, u32[]{:S(2)}, u32[]{:S(2)}) %collective-permute-start.9) | collective-permute-done | bytes 401440 | tf_op jit(solution)/shard_map/ppermute | solution.py:45
  73.5 5.0 %strips.1 = (bf16[256,8192]{1,0:T(8,128)(2,1)}, bf16[256,128]{1,0:T(8,128)(2,1)}) custom-call(f32[8,128]{1,0:T(8,128)} %copy-done.6, bf16[1568,128]{1,0:T(8,128)(2,1)} %copy-done.2, bf16[1568,128]{1,0:T(8,128)(2,1)} %copy-done.8, bf16[1568,128]{1,0:T(8,128)(2,1)} %copy-done.7, bf16[1568,128]{1,0:T(8,128)(2,1)} %copy-done.3, bf16[1568,128]{1,0:T(8,128)(2,1)} %copy-done.10, ...), custom_call_target="tpu_custom_call" | custom-call | tf_op jit(solution)/shard_map/strips/pallas_call | solution.py:303
  78.5 3.6 %all-gather.2.cloned.1.call-done.v_in = bf16[12544,128]{1,0:T(8,128)(2,1)} async-done(((bf16[1568,128]{1,0:T(8,128)(2,1)}), bf16[12544,128]{1,0:T(8,128)(2,1)}) %all-gather.2.cloned.1.call-update) | async-done | bytes 3211280 | tf_op jit(solution)/shard_map/all_gather | solution.py:114
  84.2 4.7 %own_half.1 = (f32[256,512]{1,0:T(8,128)S(1)}, bf16[4096,512]{1,0:T(8,128)(2,1)}) custom-call(bf16[256,8192]{1,0:T(8,128)(2,1)} %get-tuple-element.60.a_in.a_ref, bf16[12544,128]{1,0:T(8,128)(2,1)} %all-gather.2.cloned.1.call-done.v_in), custom_call_target="tpu_custom_call" | custom-call | tf_op jit(solution)/shard_map/own_half/pallas_call | solution.py:314
  92.3 3.4 %collective-permute-start.11 = (bf16[768,128]{1,0:T(8,128)(2,1)S(1)}, bf16[768,128]{1,0:T(8,128)(2,1)S(1)}, u32[]{:S(2)}, u32[]{:S(2)}) collective-permute-start(bf16[768,128]{1,0:T(8,128)(2,1)S(1)} %get-tuple-element.65.refs_0_), channel_id=1, source_target_pairs={{0,1},{1,2},{2,3},{3,0},{4,5},{5,6},{6,7},{7,4},{8,9},{9,10},{10,1... | collective-permute-start | bytes 589832 | tf_op jit(solution)/shard_map/ppermute | solution.py:41
  95.7 2.4 %collective-permute-start.15 = (bf16[768,128]{1,0:T(8,128)(2,1)S(1)}, bf16[768,128]{1,0:T(8,128)(2,1)S(1)}, u32[]{:S(2)}, u32[]{:S(2)}) collective-permute-start(bf16[768,128]{1,0:T(8,128)(2,1)S(1)} %get-tuple-element.65.refs_0_), channel_id=1, source_target_pairs={{0,2},{1,3},{2,0},{3,1},{4,6},{5,7},{6,4},{7,5},{8,10},{9,11},{10,... | collective-permute-start | bytes 589832 | tf_op jit(solution)/shard_map/ppermute | solution.py:41
  98.1 3.3 %collective-permute-start.14 = (bf16[768,128]{1,0:T(8,128)(2,1)S(1)}, bf16[768,128]{1,0:T(8,128)(2,1)S(1)}, u32[]{:S(2)}, u32[]{:S(2)}) collective-permute-start(bf16[768,128]{1,0:T(8,128)(2,1)S(1)} %get-tuple-element.65.refs_0_), channel_id=1, source_target_pairs={{0,3},{1,0},{2,1},{3,2},{4,7},{5,4},{6,5},{7,6},{8,11},{9,8},{10,9... | collective-permute-start | bytes 589832 | tf_op jit(solution)/shard_map/ppermute | solution.py:41
  101.4 8.9 %collective-permute-done.11.refs_1_ = bf16[768,128]{1,0:T(8,128)(2,1)S(1)} collective-permute-done((bf16[768,128]{1,0:T(8,128)(2,1)S(1)}, bf16[768,128]{1,0:T(8,128)(2,1)S(1)}, u32[]{:S(2)}, u32[]{:S(2)}) %collective-permute-start.11) | collective-permute-done | bytes 196640 | tf_op jit(solution)/shard_map/ppermute | solution.py:41
  110.3 4.6 %collective-permute-start.13 = (bf16[1536,128]{1,0:T(8,128)(2,1)S(1)}, bf16[1536,128]{1,0:T(8,128)(2,1)S(1)}, u32[]{:S(2)}, u32[]{:S(2)}) collective-permute-start(bf16[1536,128]{1,0:T(8,128)(2,1)S(1)} %cat.10.refs_0_), channel_id=1, source_target_pairs={{0,12},{1,13},{2,14},{3,15},{4,0},{5,1},{6,2},{7,3},{8,4},{9,5},{1... | collective-permute-start | bytes 1179656 | tf_op jit(solution)/shard_map/ppermute | solution.py:45
  117.0 2.7 %collective-permute-start.16 = (bf16[1536,128]{1,0:T(8,128)(2,1)S(1)}, bf16[1536,128]{1,0:T(8,128)(2,1)S(1)}, u32[]{:S(2)}, u32[]{:S(2)}) collective-permute-start(bf16[1536,128]{1,0:T(8,128)(2,1)S(1)} %cat.11.refs_3_), channel_id=1, source_target_pairs={{0,4},{1,5},{2,6},{3,7},{4,8},{5,9},{6,10},{7,11},{8,12},{9,13},{1... | collective-permute-start | bytes 1179656 | tf_op jit(solution)/shard_map/ppermute | solution.py:45
  119.7 4.4 %collective-permute-start.17 = (bf16[1536,128]{1,0:T(8,128)(2,1)S(1)}, bf16[1536,128]{1,0:T(8,128)(2,1)S(1)}, u32[]{:S(2)}, u32[]{:S(2)}) collective-permute-start(bf16[1536,128]{1,0:T(8,128)(2,1)S(1)} %cat.11.refs_3_), channel_id=1, source_target_pairs={{0,12},{1,13},{2,14},{3,15},{4,0},{5,1},{6,2},{7,3},{8,4},{9,5},{1... | collective-permute-start | bytes 1179656 | tf_op jit(solution)/shard_map/ppermute | solution.py:45
  124.0 4.9 %collective-permute-done.12.refs_1_ = bf16[1536,128]{1,0:T(8,128)(2,1)S(1)} collective-permute-done((bf16[1536,128]{1,0:T(8,128)(2,1)S(1)}, bf16[1536,128]{1,0:T(8,128)(2,1)S(1)}, u32[]{:S(2)}, u32[]{:S(2)}) %collective-permute-start.12) | collective-permute-done | bytes 393248 | tf_op jit(solution)/shard_map/ppermute | solution.py:45
  130.8 3.5 %collective-permute-done.16.refs_4_ = bf16[1536,128]{1,0:T(8,128)(2,1)S(1)} collective-permute-done((bf16[1536,128]{1,0:T(8,128)(2,1)S(1)}, bf16[1536,128]{1,0:T(8,128)(2,1)S(1)}, u32[]{:S(2)}, u32[]{:S(2)}) %collective-permute-start.16) | collective-permute-done | bytes 393248 | tf_op jit(solution)/shard_map/ppermute | solution.py:45
  136.2 3.0 %near.1.acc_ref = f32[256,512]{1,0:T(8,128)S(1)} custom-call(bf16[256,128]{1,0:T(8,128)(2,1)S(1)} %copy-done.4, bf16[4096,512]{1,0:T(8,128)(2,1)S(1)} %copy-done.1, bf16[4096,512]{1,0:T(8,128)(2,1)S(1)} %get-tuple-element.64.b_other, bf16[1536,128]{1,0:T(8,128)(2,1)S(1)} %cat.10.refs_0_, bf16[1536,128]{1,0:T(8,128)(2,1)S(1)} %collective-permute-done.12.refs_1_, ...), custom_call_target="tpu_custom_call" | custom-call | tf_op jit(solution)/shard_map/near/pallas_call | solution.py:338
  139.8 5.4 %collective-permute-done.19.refs_1_ = bf16[1536,128]{1,0:T(8,128)(2,1)S(1)} collective-permute-done((bf16[1536,128]{1,0:T(8,128)(2,1)S(1)}, bf16[1536,128]{1,0:T(8,128)(2,1)S(1)}, u32[]{:S(2)}, u32[]{:S(2)}) %collective-permute-start.19) | collective-permute-done | bytes 393248 | tf_op jit(solution)/shard_map/ppermute | solution.py:45
  (64 shorter events, 30.8 us)
Async XLA Ops:
  6.5 75.5 %all-gather.2.cloned.1.call-start = ((), (), s32[]{:S(2)}) async-start(), calls=%async_computation | async-start | bytes 3612672 | tf_op jit(solution)/shard_map/all_gather | solution.py:114
  8.4 8.6 %collective-permute-start = (bf16[784,128]{1,0:T(8,128)(2,1)S(1)}, bf16[784,128]{1,0:T(8,128)(2,1)S(1)}, u32[]{:S(2)}, u32[]{:S(2)}) collective-permute-start(bf16[784,128]{1,0:T(8,128)(2,1)S(1)} %cat.6.refs_0_), channel_id=1, source_target_pairs={{0,1},{1,2},{2,3},{3,0},{4,5},{5,6},{6,7},{7,4},{8,9},{9,10},{10,1... | collective-permute-start | bytes 602120 | tf_op jit(solution)/shard_map/ppermute | solution.py:41
  11.9 14.0 %collective-permute-start.1 = (bf16[784,128]{1,0:T(8,128)(2,1)S(1)}, bf16[784,128]{1,0:T(8,128)(2,1)S(1)}, u32[]{:S(2)}, u32[]{:S(2)}) collective-permute-start(bf16[784,128]{1,0:T(8,128)(2,1)S(1)} %cat.6.refs_0_), channel_id=1, source_target_pairs={{0,32},{16,48},{32,0},{48,16},{64,96},{80,112},{96,64},{112,80},{1... | collective-permute-start | bytes 602120 | tf_op jit(solution)/shard_map/ppermute | solution.py:49
  17.1 25.1 %copy-start.2 = (bf16[1568,128]{1,0:T(8,128)(2,1)}, bf16[1568,128]{1,0:T(8,128)(2,1)S(1)}, u32[]{:S(2)}) copy-start(bf16[1568,128]{1,0:T(8,128)(2,1)S(1)} %cat.7.refs_0_) | copy-start | bytes 1204228
  26.7 17.3 %collective-permute-start.3 = (bf16[784,128]{1,0:T(8,128)(2,1)S(1)}, bf16[784,128]{1,0:T(8,128)(2,1)S(1)}, u32[]{:S(2)}, u32[]{:S(2)}) collective-permute-start(bf16[784,128]{1,0:T(8,128)(2,1)S(1)} %cat.6.refs_0_), channel_id=1, source_target_pairs={{0,2},{1,3},{2,0},{3,1},{4,6},{5,7},{6,4},{7,5},{8,10},{9,11},{10,... | collective-permute-start | bytes 602120 | tf_op jit(solution)/shard_map/ppermute | solution.py:41
  33.2 12.4 %collective-permute-start.2 = (bf16[784,128]{1,0:T(8,128)(2,1)S(1)}, bf16[784,128]{1,0:T(8,128)(2,1)S(1)}, u32[]{:S(2)}, u32[]{:S(2)}) collective-permute-start(bf16[784,128]{1,0:T(8,128)(2,1)S(1)} %cat.6.refs_0_), channel_id=1, source_target_pairs={{0,3},{1,0},{2,1},{3,2},{4,7},{5,4},{6,5},{7,6},{8,11},{9,8},{10,9... | collective-permute-start | bytes 602120 | tf_op jit(solution)/shard_map/ppermute | solution.py:41
  37.0 15.5 %collective-permute-start.5 = (bf16[1568,128]{1,0:T(8,128)(2,1)S(1)}, bf16[1568,128]{1,0:T(8,128)(2,1)S(1)}, u32[]{:S(2)}, u32[]{:S(2)}) collective-permute-start(bf16[1568,128]{1,0:T(8,128)(2,1)S(1)} %cat.7.refs_0_), channel_id=1, source_target_pairs={{0,12},{1,13},{2,14},{3,15},{4,0},{5,1},{6,2},{7,3},{8,4},{9,5},{1... | collective-permute-start | bytes 1204232 | tf_op jit(solution)/shard_map/ppermute | solution.py:45
  42.1 12.9 %collective-permute-start.4 = (bf16[1568,128]{1,0:T(8,128)(2,1)S(1)}, bf16[1568,128]{1,0:T(8,128)(2,1)S(1)}, u32[]{:S(2)}, u32[]{:S(2)}) collective-permute-start(bf16[1568,128]{1,0:T(8,128)(2,1)S(1)} %cat.7.refs_0_), channel_id=1, source_target_pairs={{0,4},{1,5},{2,6},{3,7},{4,8},{5,9},{6,10},{7,11},{8,12},{9,13},{1... | collective-permute-start | bytes 1204232 | tf_op jit(solution)/shard_map/ppermute | solution.py:45
  46.2 13.9 %collective-permute-start.7 = (bf16[1568,128]{1,0:T(8,128)(2,1)S(1)}, bf16[1568,128]{1,0:T(8,128)(2,1)S(1)}, u32[]{:S(2)}, u32[]{:S(2)}) collective-permute-start(bf16[1568,128]{1,0:T(8,128)(2,1)S(1)} %cat.9.refs_3_), channel_id=1, source_target_pairs={{0,12},{1,13},{2,14},{3,15},{4,0},{5,1},{6,2},{7,3},{8,4},{9,5},{1... | collective-permute-start | bytes 1204232 | tf_op jit(solution)/shard_map/ppermute | solution.py:45
  50.5 11.2 %collective-permute-start.6 = (bf16[1568,128]{1,0:T(8,128)(2,1)S(1)}, bf16[1568,128]{1,0:T(8,128)(2,1)S(1)}, u32[]{:S(2)}, u32[]{:S(2)}) collective-permute-start(bf16[1568,128]{1,0:T(8,128)(2,1)S(1)} %cat.9.refs_3_), channel_id=1, source_target_pairs={{0,4},{1,5},{2,6},{3,7},{4,8},{5,9},{6,10},{7,11},{8,12},{9,13},{1... | collective-permute-start | bytes 1204232 | tf_op jit(solution)/shard_map/ppermute | solution.py:45
  52.5 20.2 %copy-start.7 = (bf16[1568,128]{1,0:T(8,128)(2,1)}, bf16[1568,128]{1,0:T(8,128)(2,1)S(1)}, u32[]{:S(2)}) copy-start(bf16[1568,128]{1,0:T(8,128)(2,1)S(1)} %collective-permute-done.5.refs_2_) | copy-start | bytes 1204228
  55.0 11.0 %collective-permute-start.8 = (bf16[1568,128]{1,0:T(8,128)(2,1)S(1)}, bf16[1568,128]{1,0:T(8,128)(2,1)S(1)}, u32[]{:S(2)}, u32[]{:S(2)}) collective-permute-start(bf16[1568,128]{1,0:T(8,128)(2,1)S(1)} %collective-permute-done.4.refs_1_), channel_id=1, source_target_pairs={{0,4},{1,5},{2,6},{3,7},{4,8},{5,9},{6,10},{7,11},{8,12},{9,13},{1... | collective-permute-start | bytes 1204232 | tf_op jit(solution)/shard_map/ppermute | solution.py:45
  61.7 11.0 %collective-permute-start.9 = (bf16[1568,128]{1,0:T(8,128)(2,1)S(1)}, bf16[1568,128]{1,0:T(8,128)(2,1)S(1)}, u32[]{:S(2)}, u32[]{:S(2)}) collective-permute-start(bf16[1568,128]{1,0:T(8,128)(2,1)S(1)} %collective-permute-done.6.refs_4_), channel_id=1, source_target_pairs={{0,4},{1,5},{2,6},{3,7},{4,8},{5,9},{6,10},{7,11},{8,12},{9,13},{1... | collective-permute-start | bytes 1204232 | tf_op jit(solution)/shard_map/ppermute | solution.py:45
  82.1 8.1 %collective-permute-start.10 = (bf16[12544,128]{1,0:T(8,128)(2,1)}, bf16[12544,128]{1,0:T(8,128)(2,1)S(1)}, u32[]{:S(2)}, u32[]{:S(2)}) collective-permute-start(bf16[12544,128]{1,0:T(8,128)(2,1)} %all-gather.2.cloned.1.call-done.v_in), channel_id=1, source_target_pairs={{0,16},{16,0},{32,48},{48,32},{64,80},{80,64},{96,112},{112,96},{1... | collective-permute-start | bytes 9633800 | tf_op jit(solution)/shard_map/ppermute | solution.py:49
  90.2 46.0 %copy-start.1 = (bf16[4096,512]{1,0:T(8,128)(2,1)S(1)}, bf16[4096,512]{1,0:T(8,128)(2,1)}, u32[]{:S(2)}) copy-start(bf16[4096,512]{1,0:T(8,128)(2,1)} %get-tuple-element.62.b_own) | copy-start | bytes 12582916
  92.3 18.1 %collective-permute-start.11 = (bf16[768,128]{1,0:T(8,128)(2,1)S(1)}, bf16[768,128]{1,0:T(8,128)(2,1)S(1)}, u32[]{:S(2)}, u32[]{:S(2)}) collective-permute-start(bf16[768,128]{1,0:T(8,128)(2,1)S(1)} %get-tuple-element.65.refs_0_), channel_id=1, source_target_pairs={{0,1},{1,2},{2,3},{3,0},{4,5},{5,6},{6,7},{7,4},{8,9},{9,10},{10,1... | collective-permute-start | bytes 589832 | tf_op jit(solution)/shard_map/ppermute | solution.py:41
  95.7 21.2 %collective-permute-start.15 = (bf16[768,128]{1,0:T(8,128)(2,1)S(1)}, bf16[768,128]{1,0:T(8,128)(2,1)S(1)}, u32[]{:S(2)}, u32[]{:S(2)}) collective-permute-start(bf16[768,128]{1,0:T(8,128)(2,1)S(1)} %get-tuple-element.65.refs_0_), channel_id=1, source_target_pairs={{0,2},{1,3},{2,0},{3,1},{4,6},{5,7},{6,4},{7,5},{8,10},{9,11},{10,... | collective-permute-start | bytes 589832 | tf_op jit(solution)/shard_map/ppermute | solution.py:41
  98.1 18.8 %collective-permute-start.14 = (bf16[768,128]{1,0:T(8,128)(2,1)S(1)}, bf16[768,128]{1,0:T(8,128)(2,1)S(1)}, u32[]{:S(2)}, u32[]{:S(2)}) collective-permute-start(bf16[768,128]{1,0:T(8,128)(2,1)S(1)} %get-tuple-element.65.refs_0_), channel_id=1, source_target_pairs={{0,3},{1,0},{2,1},{3,2},{4,7},{5,4},{6,5},{7,6},{8,11},{9,8},{10,9... | collective-permute-start | bytes 589832 | tf_op jit(solution)/shard_map/ppermute | solution.py:41
  110.3 13.7 %collective-permute-start.13 = (bf16[1536,128]{1,0:T(8,128)(2,1)S(1)}, bf16[1536,128]{1,0:T(8,128)(2,1)S(1)}, u32[]{:S(2)}, u32[]{:S(2)}) collective-permute-start(bf16[1536,128]{1,0:T(8,128)(2,1)S(1)} %cat.10.refs_0_), channel_id=1, source_target_pairs={{0,12},{1,13},{2,14},{3,15},{4,0},{5,1},{6,2},{7,3},{8,4},{9,5},{1... | collective-permute-start | bytes 1179656 | tf_op jit(solution)/shard_map/ppermute | solution.py:45
  115.0 13.9 %collective-permute-start.12 = (bf16[1536,128]{1,0:T(8,128)(2,1)S(1)}, bf16[1536,128]{1,0:T(8,128)(2,1)S(1)}, u32[]{:S(2)}, u32[]{:S(2)}) collective-permute-start(bf16[1536,128]{1,0:T(8,128)(2,1)S(1)} %cat.10.refs_0_), channel_id=1, source_target_pairs={{0,4},{1,5},{2,6},{3,7},{4,8},{5,9},{6,10},{7,11},{8,12},{9,13},{1... | collective-permute-start | bytes 1179656 | tf_op jit(solution)/shard_map/ppermute | solution.py:45
  117.0 17.3 %collective-permute-start.16 = (bf16[1536,128]{1,0:T(8,128)(2,1)S(1)}, bf16[1536,128]{1,0:T(8,128)(2,1)S(1)}, u32[]{:S(2)}, u32[]{:S(2)}) collective-permute-start(bf16[1536,128]{1,0:T(8,128)(2,1)S(1)} %cat.11.refs_3_), channel_id=1, source_target_pairs={{0,4},{1,5},{2,6},{3,7},{4,8},{5,9},{6,10},{7,11},{8,12},{9,13},{1... | collective-permute-start | bytes 1179656 | tf_op jit(solution)/shard_map/ppermute | solution.py:45
  119.7 16.5 %collective-permute-start.17 = (bf16[1536,128]{1,0:T(8,128)(2,1)S(1)}, bf16[1536,128]{1,0:T(8,128)(2,1)S(1)}, u32[]{:S(2)}, u32[]{:S(2)}) collective-permute-start(bf16[1536,128]{1,0:T(8,128)(2,1)S(1)} %cat.11.refs_3_), channel_id=1, source_target_pairs={{0,12},{1,13},{2,14},{3,15},{4,0},{5,1},{6,2},{7,3},{8,4},{9,5},{1... | collective-permute-start | bytes 1179656 | tf_op jit(solution)/shard_map/ppermute | solution.py:45
  128.9 10.9 %collective-permute-start.18 = (bf16[1536,128]{1,0:T(8,128)(2,1)S(1)}, bf16[1536,128]{1,0:T(8,128)(2,1)S(1)}, u32[]{:S(2)}, u32[]{:S(2)}) collective-permute-start(bf16[1536,128]{1,0:T(8,128)(2,1)S(1)} %collective-permute-done.12.refs_1_), channel_id=1, source_target_pairs={{0,4},{1,5},{2,6},{3,7},{4,8},{5,9},{6,10},{7,11},{8,12},{9,13},{1... | collective-permute-start | bytes 1179656 | tf_op jit(solution)/shard_map/ppermute | solution.py:45
  134.3 10.9 %collective-permute-start.19 = (bf16[1536,128]{1,0:T(8,128)(2,1)S(1)}, bf16[1536,128]{1,0:T(8,128)(2,1)S(1)}, u32[]{:S(2)}, u32[]{:S(2)}) collective-permute-start(bf16[1536,128]{1,0:T(8,128)(2,1)S(1)} %collective-permute-done.16.refs_4_), channel_id=1, source_target_pairs={{0,4},{1,5},{2,6},{3,7},{4,8},{5,9},{6,10},{7,11},{8,12},{9,13},{1... | collective-permute-start | bytes 1179656 | tf_op jit(solution)/shard_map/ppermute | solution.py:45
  (10 other events, 75.0 us)
Sparse Core Ops, SparseCore 0:
  26.9 55.1 all-gather.1
